TPU v7x, 32 devices: a whole 2x2x4 slice. The times are simulated.
32 devices in a mesh: groups: 2 (over y), row: 8 (over z, x), col: 2 (over core).
Axes of the slice: x: 2, y: 2, z: 4, core: 2. Of those that a mesh axis runs over, the one named last changes fastest.
Arguments:
- tokens: bfloat16 [768, 6144], P(('groups', 'col'), 'row'), parts along dimension 0, may hold values from -6 to 6
- cotangent: bfloat16 [768, 6144], P(('groups', 'col'), 'row'), parts along dimension 0, may hold values from -6 to 6
- up_weight: bfloat16 [6144, 24576], P('col', 'row'), may hold values from -0.109375 to 0.109375
- up_bias: float32 [24576], P('row'), may hold values from -3 to 3
- down_weight: bfloat16 [24576, 6144], P('row', 'col'), may hold values from -0.0546875 to 0.0546875
- norm_gain: float32 [6144], replicated, may hold values from 0.25 to 1.75
Outputs:
- block_out: bfloat16 [768, 6144], P(('groups', 'col'), 'row'), parts along dimension 0
- grad_x: bfloat16 [768, 6144], P(('groups', 'col'), 'row'), parts along dimension 0
- grad_in: bfloat16 [12288, 24576], P(('groups', 'col'), 'row'), parts along dimension 0
- grad_out: bfloat16 [49152, 6144], P(('groups', 'row'), 'col'), parts along dimension 0
- grad_bias: float32 [49152], P(('groups', 'row')), parts along dimension 0
- grad_gain: float32 [12288], P(('groups', 'row')), parts along dimension 0
There are 2 independent parts, one for each index of `groups`. A program takes and returns all parts, laid end to end along the dimension named above; an argument that names none is the same for every part. Nothing has to cross between parts.
All inputs are finite; a program needn't handle non-finite values.
Results may differ from a plain program's by a relative error of at most 0.0075.
Values may be sent and summed in bfloat16 or wider, within the bound.
No kernel may reach another device: no remote copies, remote signals or barrier semaphores. Data moves between devices by JAX's collectives and lax.ppermute only.
A program may use at most 320 MiB of HBM per device.

v0:
```python
import jax
import jax.numpy as jnp
from jax import lax
from jax.sharding import PartitionSpec as P

norm_eps = 1e-06
root_half = 0.7071067811865476
pdf_scale = 0.3989422804014327


def gelu_parts(hidden):
    cumulative = 0.5 * (1.0 + lax.erf(hidden * root_half))
    density = jnp.exp(-0.5 * hidden * hidden) * pdf_scale
    return (hidden * cumulative, cumulative + hidden * density)


def contract(left, right, left_dim, right_dim):
    return lax.dot_general(
        left, right, (((left_dim,), (right_dim,)), ((), ())), preferred_element_type=jnp.float32
    )


def block_grad(left, right, blocks):
    left_blocks = left.reshape(blocks, -1, left.shape[1])
    right_blocks = right.reshape(blocks, -1, right.shape[1])
    pieces = jnp.einsum(
        "btl,btr->blr", left_blocks, right_blocks, preferred_element_type=jnp.float32
    ).astype(jnp.bfloat16)
    pieces = lax.optimization_barrier(pieces)
    return jnp.sum(pieces.astype(jnp.float32), axis=0).astype(jnp.bfloat16)


def local(tokens, cotangent, up_weight, up_bias, down_weight, norm_gain):
    full_tokens, full_cotangent = (
        lax.all_gather(tokens, "row", axis=1, tiled=True),
        lax.all_gather(cotangent, "row", axis=1, tiled=True),
    )
    model_width = full_tokens.shape[1]
    shard_width = tokens.shape[1]
    tok_count = tokens.shape[0]
    col_count = lax.axis_size("col")
    shard_start = lax.axis_index("row") * shard_width
    as_float = full_tokens.astype(jnp.float32)
    token_mean = jnp.mean(as_float, axis=1, keepdims=True)
    centered = as_float - token_mean
    inverse_std = lax.rsqrt(jnp.mean(centered * centered, axis=1, keepdims=True) + norm_eps)
    whitened = centered * inverse_std
    normed = (whitened * norm_gain).astype(jnp.bfloat16)
    normed_cols, cot_cols = (
        lax.all_to_all(normed, "col", split_axis=1, concat_axis=0, tiled=True),
        lax.all_to_all(full_cotangent, "col", split_axis=1, concat_axis=0, tiled=True),
    )
    hidden_part = jnp.dot(normed_cols, up_weight, preferred_element_type=jnp.float32)
    act_part = contract(cot_cols, down_weight, 1, 1)
    hidden_sum, act_grad = lax.psum((hidden_part, act_part), "col")
    hidden = hidden_sum + up_bias
    gelu_value, gelu_slope = gelu_parts(hidden)
    activation_all = gelu_value.astype(jnp.bfloat16)
    hidden_grad_all = (act_grad * gelu_slope).astype(jnp.bfloat16)
    branch_half = jnp.dot(activation_all, down_weight, preferred_element_type=jnp.float32)
    branch_part = lax.all_to_all(
        branch_half.astype(jnp.bfloat16), "col", split_axis=0, concat_axis=1, tiled=True
    ).astype(branch_half.dtype)
    normed_half = contract(hidden_grad_all, up_weight, 1, 1)
    normed_partial = lax.all_to_all(
        normed_half.astype(jnp.bfloat16), "col", split_axis=0, concat_axis=1, tiled=True
    ).astype(normed_half.dtype)
    own_rows = lax.dynamic_slice_in_dim(
        hidden_grad_all, lax.axis_index("col") * tok_count, tok_count, 0
    )
    bias_part = jnp.sum(own_rows.astype(jnp.float32), axis=0)
    grad_out = block_grad(activation_all, cot_cols, col_count)
    grad_in = block_grad(normed_cols, hidden_grad_all, col_count)
    branch = lax.psum_scatter(branch_part, "row", scatter_dimension=1, tiled=True)
    block_out = (tokens.astype(jnp.float32) + branch).astype(jnp.bfloat16)
    normed_grad = lax.psum_scatter(normed_partial, "row", scatter_dimension=1, tiled=True)
    local_white = lax.dynamic_slice_in_dim(whitened, shard_start, shard_width, 1)
    gain_local = lax.dynamic_slice_in_dim(norm_gain, shard_start, shard_width, 0)
    scaled = normed_grad * gain_local
    first_sum, second_sum = lax.psum(
        (jnp.sum(scaled, axis=1), jnp.sum(scaled * local_white, axis=1)), "row"
    )
    first_stat = (first_sum / model_width)[:, None]
    second_stat = (second_sum / model_width)[:, None]
    grad_x = (
        cotangent.astype(jnp.float32)
        + inverse_std * (scaled - first_stat - local_white * second_stat)
    ).astype(jnp.bfloat16)
    gain_part = jnp.sum(normed_grad * local_white, axis=0)
    grad_bias, grad_gain = lax.psum((bias_part, gain_part), "col")
    return (block_out, grad_x, grad_in, grad_out, grad_bias, grad_gain)


def solution(mesh):
    return jax.shard_map(
        local,
        mesh=mesh,
        in_specs=(
            P(("groups", "col"), "row"),
            P(("groups", "col"), "row"),
            P("col", "row"),
            P("row"),
            P("row", "col"),
            P(),
        ),
        out_specs=(
            P(("groups", "col"), "row"),
            P(("groups", "col"), "row"),
            P(("groups", "col"), "row"),
            P(("groups", "row"), "col"),
            P(("groups", "row")),
            P(("groups", "row")),
        ),
        check_vma=False,
    )
```

profile of v0, /device:TPU:0, one launch (start us, length us, event | category | flops | bytes accessed | tf_op | source)
XLA Modules:
  0.0 435.0 jit_solution(13710262088363707435)
XLA Ops:
  7.2 0.0 all-gather.5.cloned.1.call-start
  7.2 0.7 all-gather.5.cloned.1.call-update
  7.9 0.0 all-gather.3.cloned.1.call-start
  7.9 0.7 all-gather.3.cloned.1.call-update
  8.6 56.3 %all-gather.5.cloned.1.call-done = bf16[192,6144]{1,0:T(8,128)(2,1)} async-done(((bf16[192,768]{1,0:T(8,128)(2,1)}), bf16[192,6144]{1,0:T(8,128)(2,1)}) %all-gather.5.cloned.1.call-update) | async-done | bytes 2359312 | tf_op jit(solution)/shard_map/all_gather | solution.py:36
  64.9 0.0 copy-start.4
  64.9 3.2 copy.24
  68.2 49.8 %all-gather.3.cloned.1.call-done = bf16[192,6144]{1,0:T(8,128)(2,1)} async-done(((bf16[192,768]{1,0:T(8,128)(2,1)}), bf16[192,6144]{1,0:T(8,128)(2,1)}) %all-gather.3.cloned.1.call-update) | async-done | bytes 2359312 | tf_op jit(solution)/shard_map/all_gather | solution.py:35
  117.9 0.0 copy-start
  117.9 2.2 convert_reduce_fusion
  120.2 2.4 fusion.2
  122.6 0.0 copy-done.4
  122.6 0.0 copy-done
  122.6 3.2 fusion
  125.8 0.2 copy.25
  126.0 5.6 %all_to_all.64 = bf16[192,2,3072]{2,0,1:T(8,128)(2,1)S(1)} all-to-all(bf16[192,2,3072]{2,0,1:T(8,128)(2,1)S(1)} %bitcast.43), channel_id=1, replica_groups=mesh['groups'=2,'row'=8,'col'=2] {'col'}, dimensions={1} | all-to-all | bytes 4718592 | tf_op jit(solution)/shard_map/all_to_all | solution.py:50
  131.6 0.0 copy-start.1
  131.6 4.9 %all-to-all-start.2 = ((bf16[192,2,3072]{2,0,1:T(8,128)(2,1)}), bf16[192,2,3072]{2,0,1:T(8,128)(2,1)}, u32[]{:S(2)}, u32[]{:S(2)}) async-start(bf16[192,2,3072]{2,0,1:T(8,128)(2,1)} %bitcast.38), calls=%async_computation.3 | async-start | bytes 4718592 | tf_op jit(solution)/shard_map/all_to_all | solution.py:51
  136.5 0.0 all-reduce.5.cloned.1.call-start
  136.6 13.0 %fusion.11 = f32[384,3072]{1,0:T(8,128)} fusion(bf16[384,3072]{1,0:T(8,128)(2,1)S(1)} %bitcast.46, bf16[3072,3072]{1,0:T(8,128)(2,1)} %param.8), kind=kOutput, calls=%fused_computation.35 | convolution fusion | flops 7247757312 | bytes 25952256 | tf_op jit(solution)/shard_map/dot_general | solution.py:53
  149.6 0.0 copy-done.1
  149.6 0.0 all-to-all-done.2
  149.6 13.5 %fusion.12 = f32[384,3072]{1,0:T(8,128)} fusion(bf16[384,3072]{1,0:T(8,128)(2,1)} %bitcast.5, bf16[3072,3072]{1,0:T(8,128)(2,1)} %param.10), kind=kOutput, calls=%fused_computation.36 | convolution fusion | flops 7247757312 | bytes 25952256 | tf_op jit(solution)/shard_map/dot_general | solution.py:18
  163.1 0.0 copy-start.5
  163.1 0.0 all-reduce.5.cloned.1.call-update
  163.1 0.2 reduce-scatter.5.cloned.1.call-start
  163.3 39.6 %all-reduce.5.cloned.1.call-done = (f32[384,3072]{1,0:T(8,128)}, f32[384,3072]{1,0:T(8,128)}) async-done(((f32[384,3072]{1,0:T(8,128)}, f32[384,3072]{1,0:T(8,128)}), (f32[384,3072]{1,0:T(8,128)}, f32[384,3072]{1,0:T(8,128)})) %all-reduce.5.cloned.1.call-update) | async-done | bytes 9437200 | tf_op jit(solution)/shard_map/psum | solution.py:55
  202.9 0.0 copy-done.5
  202.9 5.9 %fusion.8 = (bf16[384,3072]{1,0:T(8,128)(2,1)S(1)}, bf16[384,3072]{1,0:T(8,128)(2,1)}) fusion(f32[384,3072]{1,0:T(8,128)} %get-tuple-element.14, f32[384,3072]{1,0:T(8,128)} %get-tuple-element.13, f32[3072]{0:T(1024)S(1)} %copy-done.5), kind=kLoop, calls=%fused_computation.13 | loop fusion | flops 15335424 | bytes 14168064 | tf_op jit(solution)/shard_map/convert_element_type | solution.py:59
  208.9 11.2 %convolution_convert_fusion.2 = bf16[384,3072]{1,0:T(8,128)(2,1)S(1)} fusion(bf16[384,3072]{1,0:T(8,128)(2,1)S(1)} %get-tuple-element.15, bf16[3072,3072]{1,0:T(8,128)(2,1)} %param.8), kind=kOutput, calls=%fused_computation.19 | convolution fusion | flops 7248936960 | bytes 23592960 | tf_op jit(solution)/shard_map/dot_general | solution.py:18
  220.0 5.6 %all_to_all.65 = bf16[2,192,3072]{2,1,0:T(8,128)(2,1)S(1)} all-to-all(bf16[2,192,3072]{2,1,0:T(8,128)(2,1)S(1)} %bitcast.48), channel_id=1, replica_groups=mesh['groups'=2,'row'=8,'col'=2] {'col'}, dimensions={0} | all-to-all | bytes 4718592 | tf_op jit(solution)/shard_map/all_to_all | solution.py:65
  225.7 0.6 convert_bitcast_fusion
  226.2 2.7 copy.21
  229.0 0.0 reduce-scatter.5.cloned.1.call-update
  229.0 0.0 reduce-scatter.3.cloned.1.call-start
  229.0 12.0 %convolution_convert_fusion.3 = bf16[384,3072]{1,0:T(8,128)(2,1)S(1)} fusion(bf16[384,3072]{1,0:T(8,128)(2,1)} %get-tuple-element.16, bf16[3072,3072]{1,0:T(8,128)(2,1)} %param.10), kind=kOutput, calls=%fused_computation.20 | convolution fusion | flops 7248936960 | bytes 23592960 | tf_op jit(solution)/shard_map/dot_general | solution.py:60
  241.0 5.6 %all_to_all.66 = bf16[2,192,3072]{2,1,0:T(8,128)(2,1)S(1)} all-to-all(bf16[2,192,3072]{2,1,0:T(8,128)(2,1)S(1)} %bitcast.49), channel_id=1, replica_groups=mesh['groups'=2,'row'=8,'col'=2] {'col'}, dimensions={0} | all-to-all | bytes 4718592 | tf_op jit(solution)/shard_map/all_to_all | solution.py:61
  246.7 0.6 convert_bitcast_fusion.1
  247.3 2.7 copy.20
  250.0 0.0 reduce-scatter.3.cloned.1.call-update
  250.0 0.1 dynamic_slice.9
  250.1 17.9 %convolution_convert_fusion.1 = bf16[2,3072,3072]{2,1,0:T(8,128)(2,1)} fusion(bf16[2,192,3072]{2,1,0:T(8,128)(2,1)S(1)} %bitcast.42, bf16[192,2,3072]{2,0,1:T(8,128)(2,1)} %copy-done.1), kind=kOutput, calls=%fused_computation.1 | convolution fusion | flops 7266631680 | bytes 42467328 | tf_op jit(solution)/shard_map/btl,btr->blr/dot_general | solution.py:26
  268.0 18.0 %convolution_convert_fusion = bf16[2,3072,3072]{2,1,0:T(8,128)(2,1)} fusion(bf16[2,192,3072]{2,1,0:T(8,128)(2,1)} %bitcast.45, bf16[192,2,3072]{2,0,1:T(8,128)(2,1)} %all-to-all-done.2), kind=kOutput, calls=%fused_computation | convolution fusion | flops 7266631680 | bytes 42467328 | tf_op jit(solution)/shard_map/btl,btr->blr/dot_general | solution.py:26
  286.0 24.2 %reduce_sum.82 = bf16[3072,3072]{1,0:T(8,128)(2,1)} reduce(bf16[2,3072,3072]{2,1,0:T(8,128)(2,1)} %convolution_convert_fusion.1, bf16[]{:T(256)} %constant.39.clone.1), dimensions={0}, to_apply=%region_10.0 | reduce | flops 9437184 | bytes 56623104 | tf_op jit(solution)/shard_map/reduce_sum | solution.py:30
  310.3 0.0 copy-start.2
  310.3 0.0 copy-start.3
  310.3 24.1 %reduce_sum.83 = bf16[3072,3072]{1,0:T(8,128)(2,1)} reduce(bf16[2,3072,3072]{2,1,0:T(8,128)(2,1)} %convolution_convert_fusion, bf16[]{:T(256)} %constant.39.clone.1), dimensions={0}, to_apply=%region_11.0 | reduce | flops 9437184 | bytes 56623104 | tf_op jit(solution)/shard_map/reduce_sum | solution.py:30
  334.4 0.2 convert_reduce_fusion.1
  334.6 0.0 reduce-scatter.5.cloned.1.call-done
  334.6 1.5 multiply_reduce_fusion
  336.1 22.7 %all-reduce = (f32[192]{0:T(256)S(1)}, f32[192]{0:T(256)S(1)}) all-reduce(f32[192]{0:T(256)S(1)} %get-tuple-element.7, f32[192]{0:T(256)S(1)} %get-tuple-element.8), channel_id=1, replica_groups=mesh['groups'=2,'row'=8,'col'=2] {'row'}, use_global_device_ids=true, to_apply=%region_9.0 | all-reduce | flops 384 | bytes 3072 | tf_op jit(solution)/shard_map/psum | solution.py:80
  358.8 3.9 all-reduce.1
  362.7 61.7 %reduce-scatter.3.cloned.1.call-done = f32[192,768]{1,0:T(8,128)} async-done(((f32[192,6144]{1,0:T(8,128)}), f32[192,768]{1,0:T(8,128)}) %reduce-scatter.3.cloned.1.call-update) | async-done | bytes 589840 | tf_op jit(solution)/shard_map/reduce_scatter | solution.py:74
  424.5 0.0 copy-done.2
  424.5 1.8 add_convert_fusion.1
  426.3 0.0 copy-done.3
  426.3 2.2 add_convert_fusion
  (3 shorter events, 0.0 us)
Async XLA Ops:
  7.2 57.7 %all-gather.5.cloned.1.call-start = ((), (), s32[]{:S(2)}) async-start(), calls=%async_computation.8 | async-start | bytes 2654208 | tf_op jit(solution)/shard_map/all_gather | solution.py:36
  7.9 110.0 %all-gather.3.cloned.1.call-start = ((), (), s32[]{:S(2)}) async-start(), calls=%async_computation.6 | async-start | bytes 2654208 | tf_op jit(solution)/shard_map/all_gather | solution.py:35
  64.9 57.7 %copy-start.4 = (f32[6144]{0:T(1024)S(1)}, f32[6144]{0:T(1024)}, u32[]{:S(2)}) copy-start(f32[6144]{0:T(1024)} %param.11) | copy-start | bytes 73732
  117.9 4.7 %copy-start = (bf16[192,6144]{1,0:T(8,128)(2,1)S(1)}, bf16[192,6144]{1,0:T(8,128)(2,1)}, u32[]{:S(2)}) copy-start(bf16[192,6144]{1,0:T(8,128)(2,1)} %all-gather.3.cloned.1.call-done) | copy-start | bytes 7077892
  131.6 17.9 %copy-start.1 = (bf16[192,2,3072]{2,0,1:T(8,128)(2,1)}, bf16[192,2,3072]{2,0,1:T(8,128)(2,1)S(1)}, u32[]{:S(2)}) copy-start(bf16[192,2,3072]{2,0,1:T(8,128)(2,1)S(1)} %all_to_all.64) | copy-start | bytes 7077892
  131.6 17.9 %all-to-all-start.2 = ((bf16[192,2,3072]{2,0,1:T(8,128)(2,1)}), bf16[192,2,3072]{2,0,1:T(8,128)(2,1)}, u32[]{:S(2)}, u32[]{:S(2)}) async-start(bf16[192,2,3072]{2,0,1:T(8,128)(2,1)} %bitcast.38), calls=%async_computation.3 | async-start | bytes 4718592 | tf_op jit(solution)/shard_map/all_to_all | solution.py:51
  136.5 66.4 %all-reduce.5.cloned.1.call-start = ((), (), s32[]{:S(2)}) async-start(), calls=%async_computation.10 | async-start | bytes 18874368 | tf_op jit(solution)/shard_map/psum | solution.py:55
  163.1 39.9 %copy-start.5 = (f32[3072]{0:T(1024)S(1)}, f32[3072]{0:T(1024)}, u32[]{:S(2)}) copy-start(f32[3072]{0:T(1024)} %param.9) | copy-start | bytes 36868
  163.1 171.5 %reduce-scatter.5.cloned.1.call-start = ((), (), s32[]{:S(2)}) async-start(), calls=%async_computation.9 | async-start | bytes 5308416 | tf_op jit(solution)/shard_map/reduce_scatter | solution.py:76
  229.0 195.5 %reduce-scatter.3.cloned.1.call-start = ((), (), s32[]{:S(2)}) async-start(), calls=%async_computation.7 | async-start | bytes 5308416 | tf_op jit(solution)/shard_map/reduce_scatter | solution.py:74
  310.3 114.2 %copy-start.2 = (bf16[192,768]{1,0:T(8,128)(2,1)S(1)}, bf16[192,768]{1,0:T(8,128)(2,1)}, u32[]{:S(2)}) copy-start(bf16[192,768]{1,0:T(8,128)(2,1)} %param.6) | copy-start | bytes 884740
  310.3 116.0 %copy-start.3 = (bf16[192,768]{1,0:T(8,128)(2,1)S(1)}, bf16[192,768]{1,0:T(8,128)(2,1)}, u32[]{:S(2)}) copy-start(bf16[192,768]{1,0:T(8,128)(2,1)} %param.7) | copy-start | bytes 884740
Sparse Core Ops, SparseCore 0:
  10.2 54.7 all-gather.4
  67.1 50.8 all-gather.2
  163.2 39.6 all-reduce.4
  229.1 96.4 reduce-scatter.4
  329.1 95.3 reduce-scatter.2
where the time goes:
time: 436 us; the launch traced here: 435 us
  waiting for transfers between devices  209 us (48%)
  matrix products  85.6 us (20%)
  other arithmetic  69 us (16%)
  blocking collectives  43.5 us (10%)
  between operations  13.9 us (3%)
  local copies, waits for them, and re-layouts  8.95 us (2%)
  starting transfers between devices  5.28 us (1%)
    reduce_scatter x1, waiting for transfers between devices, local(): lax.psum_scatter(branch_part, 'row', scatter_dimension=1, tiled=True)  61.7 us
    all_gather x1, waiting for transfers between devices, local(): lax.all_gather(cotangent, 'row', axis=1, tiled=True)  56.3 us
    all_gather x1, waiting for transfers between devices, local(): lax.all_gather(tokens, 'row', axis=1, tiled=True)  49.8 us
    reduce_sum x2, other arithmetic, block_grad(): return jnp.sum(pieces.astype(jnp.float32), axis=0).astype(jnp.bfloat16)  48.4 us
    psum x1, waiting for transfers between devices, local(): hidden_sum, act_grad = lax.psum((hidden_part, act_part), 'col')  39.6 us
    dot_general x2, matrix products, block_grad(): jnp.einsum('btl,btr->blr', left_blocks, right_blocks, preferred_element_t...  35.9 us
    dot_general x2, matrix products, contract(): lax.dot_general(left, right, (((left_dim,), (right_dim,)), ((), ())), pre...  24.6 us
    psum x1, blocking collectives, local(): lax.psum((jnp.sum(scaled, axis=1), jnp.sum(scaled * local_white, axis=1))...  22.7 us
  transfers between devices with their start and end apart: 6, of which 4 were waited for; matrix products, arithmetic and copies ran while one was open for 27% of the time, Pallas kernels for 0%

commit v1 on v0

v1 whole, which is shorter than its diff:
```python
import jax
import jax.numpy as jnp
from jax import lax
from jax.sharding import PartitionSpec as P

norm_eps = 1e-06
root_half = 0.7071067811865476
pdf_scale = 0.3989422804014327
bf16 = jnp.bfloat16
f32 = jnp.float32
ring_limit = 8


def gelu_parts(hidden):
    cumulative = 0.5 * (1.0 + lax.erf(hidden * root_half))
    density = jnp.exp(-0.5 * hidden * hidden) * pdf_scale
    return (hidden * cumulative, cumulative + hidden * density)


def contract(left, right, left_dim, right_dim):
    return lax.dot_general(
        left, right, (((left_dim,), (right_dim,)), ((), ())), preferred_element_type=f32
    )


class Ring:
    def __init__(self, n):
        self.n = n
        self.order = list(range(0, n, 2)) + list(range(n - 1, 0, -2))
        row = lax.axis_index("row")
        half = row // 2
        self.place = jnp.where(row % 2 == 0, half, n - 1 - half)

    def shift(self, x, step):
        n, order = self.n, self.order
        return lax.ppermute(x, "row", [(order[i], order[(i + step) % n]) for i in range(n)])

    def row_at(self, offset):
        n = self.n
        place = (self.place + offset) % n
        return jnp.where(place < n // 2, 2 * place, 2 * (n - 1 - place) + 1)

    def every(self, x):
        n = self.n
        if n > ring_limit:
            return lax.all_gather(x, "row")
        sent = [lax.ppermute(x, "row", [(i, (i + k) % n) for i in range(n)]) for k in range(1, n)]
        return jnp.stack([x] + sent)

    def total(self, x):
        step = 1
        while step < self.n:
            x = x + lax.ppermute(x, "row", [(i, i ^ step) for i in range(self.n)])
            step *= 2
        return x

    def gather(self, x):
        n = self.n
        if n > ring_limit:
            rows = lax.all_gather(x, "row")
            return [lax.dynamic_index_in_dim(rows, self.row_at(k), 0, keepdims=False) for k in range(n)]
        blocks = [None] * n
        blocks[0] = up = down = x
        for k in range(1, n // 2):
            up, down = self.shift(up, -1), self.shift(down, 1)
            blocks[k], blocks[n - k] = up, down
        cut = x.shape[0] // 2
        blocks[n // 2] = jnp.concatenate([self.shift(up[:cut], -1), self.shift(down[cut:], 1)], axis=0)
        return blocks

    def scatter_sum(self, blocks):
        n = self.n
        if n > ring_limit:
            stacked = jnp.stack(blocks)
            offsets = [(self.order.index(r) - self.place) % n for r in range(n)]
            by_row = jnp.stack([lax.dynamic_index_in_dim(stacked, k, 0, keepdims=False) for k in offsets])
            return lax.psum_scatter(by_row.astype(f32), "row", scatter_dimension=0)
        mid = n // 2
        cut = blocks[0].shape[0] // 2
        ahead = self.shift(blocks[mid][:cut], 1)
        back = self.shift(blocks[mid][cut:], -1)
        for k in range(mid - 1, 0, -1):
            to, fro = blocks[k], blocks[n - k]
            if k == mid - 1:
                ahead = jnp.concatenate([(to[:cut].astype(f32) + ahead.astype(f32)).astype(bf16), to[cut:]], axis=0)
                back = jnp.concatenate([fro[:cut], (fro[cut:].astype(f32) + back.astype(f32)).astype(bf16)], axis=0)
            else:
                ahead = (to.astype(f32) + ahead.astype(f32)).astype(bf16)
                back = (fro.astype(f32) + back.astype(f32)).astype(bf16)
            ahead, back = self.shift(ahead, 1), self.shift(back, -1)
        return blocks[0].astype(f32) + ahead.astype(f32) + back.astype(f32)


def swap(x):
    return lax.ppermute(x, "col", [(0, 1), (1, 0)])


def turned(x):
    half = x.shape[0] // 2
    return jnp.concatenate([x[half:], x[:half]], axis=0)


def local(tokens, cotangent, up_weight, up_bias, down_weight, norm_gain):
    tok_count, shard_width = tokens.shape
    n = lax.axis_size("row")
    model_width = n * shard_width
    half_width = model_width // 2
    core = lax.axis_index("col")
    row = lax.axis_index("row")
    ring = Ring(n)
    pairs = n // 2
    first_row = core * pairs

    rows_near = [ring.row_at(j) for j in range(pairs)]
    rows_far = [ring.row_at(j + pairs) for j in range(pairs)]
    near = [(r // pairs) == core for r in rows_near]
    slot = [jnp.where(s, a, b) - first_row for s, a, b in zip(near, rows_near, rows_far)]

    as_float = tokens.astype(f32)
    shard_mean = jnp.mean(as_float, axis=1)
    shard_dev = jnp.sum((as_float - shard_mean[:, None]) ** 2, axis=1)
    own_stats = jnp.stack([shard_mean, shard_dev])
    stats = ring.every(own_stats)
    token_mean = jnp.mean(stats[:, 0], axis=0)
    spread = jnp.sum(stats[:, 1], axis=0) + shard_width * jnp.sum((stats[:, 0] - token_mean) ** 2, axis=0)
    inverse_std = lax.rsqrt(spread / model_width + norm_eps)[:, None]
    whitened = (as_float - token_mean[:, None]) * inverse_std
    gain_local = lax.dynamic_slice_in_dim(norm_gain, row * shard_width, shard_width, 0)
    gain_half = lax.dynamic_slice_in_dim(norm_gain, core * half_width, half_width, 0)
    normed = (whitened * gain_local).astype(bf16)

    def halves(x):
        blocks = ring.gather(x)
        out = jnp.zeros((2 * tok_count, half_width), x.dtype)
        for j in range(pairs):
            keep = jnp.where(near[j], blocks[j], blocks[j + pairs])
            send = jnp.where(near[j], blocks[j + pairs], blocks[j])
            both = jnp.concatenate([keep, swap(send)], axis=0)
            out = lax.dynamic_update_slice(out, both, (0, slot[j] * shard_width))
        return out

    normed_cols = halves(normed)
    cot_cols = halves(cotangent)

    width = up_weight.shape[1]
    mine, theirs = core * (width // 2), (1 - core) * (width // 2)

    def summed(part):
        give = lax.dynamic_slice_in_dim(part, theirs, width // 2, 1)
        own = lax.dynamic_slice_in_dim(part, mine, width // 2, 1)
        return own + swap(turned(give))

    def joined(own):
        other = swap(turned(own))
        return jnp.where(
            core == 0,
            jnp.concatenate([own, other], axis=1),
            jnp.concatenate([other, own], axis=1),
        )

    hidden = summed(jnp.dot(normed_cols, up_weight, preferred_element_type=f32))
    hidden = hidden + lax.dynamic_slice_in_dim(up_bias, mine, width // 2, 0)
    act_grad = summed(contract(cot_cols, down_weight, 1, 1))
    gelu_value, gelu_slope = gelu_parts(hidden)
    activation = joined(gelu_value.astype(bf16))
    hidden_grad = joined((act_grad * gelu_slope).astype(bf16))

    def scattered(part):
        keep, recv = part[:tok_count], swap(part[tok_count:])
        blocks = [None] * n
        for j in range(pairs):
            a = lax.dynamic_slice_in_dim(keep, slot[j] * shard_width, shard_width, 1)
            other_slot = jnp.where(near[j], rows_far[j], rows_near[j]) - (1 - core) * pairs
            b = lax.dynamic_slice_in_dim(recv, other_slot * shard_width, shard_width, 1)
            blocks[j] = jnp.where(near[j], a, b)
            blocks[j + pairs] = jnp.where(near[j], b, a)
        return ring.scatter_sum(blocks)

    branch = scattered(jnp.dot(activation, down_weight, preferred_element_type=f32).astype(bf16))
    block_out = (as_float + branch).astype(bf16)

    normed_half = contract(hidden_grad, up_weight, 1, 1)
    product = normed_half * normed_cols.astype(f32)
    first_part = jnp.sum(normed_half * gain_half, axis=1)
    second_part = jnp.sum(product, axis=1)
    gain_part = jnp.sum(product, axis=0)
    by_token = jnp.stack([first_part, second_part]).reshape(2, 2, tok_count)
    by_token = jnp.where(core == 0, by_token, by_token[:, ::-1])
    gain_full = lax.dynamic_update_slice(jnp.zeros((model_width,), f32), gain_part, (core * half_width,))
    small = jnp.concatenate([by_token.reshape(-1), gain_full])
    small = ring.total(small + swap(small))
    by_token = small[: 4 * tok_count].reshape(2, 2, tok_count)
    by_token = lax.dynamic_index_in_dim(by_token, core, 1, keepdims=False) / model_width
    grad_gain = lax.dynamic_slice_in_dim(small, 4 * tok_count + row * shard_width, shard_width, 0) / gain_local

    normed_grad = scattered(normed_half.astype(bf16))
    grad_out = contract(activation, cot_cols, 0, 0).astype(bf16)
    grad_in = contract(normed_cols, hidden_grad, 0, 0).astype(bf16)
    grad_bias = jnp.sum(hidden_grad.astype(f32), axis=0)
    scaled = normed_grad * gain_local
    grad_x = (
        cotangent.astype(f32)
        + inverse_std * (scaled - by_token[0][:, None] - whitened * by_token[1][:, None])
    ).astype(bf16)
    return (block_out, grad_x, grad_in, grad_out, grad_bias, grad_gain)


def solution(mesh):
    return jax.shard_map(
        local,
        mesh=mesh,
        in_specs=(
            P(("groups", "col"), "row"),
            P(("groups", "col"), "row"),
            P("col", "row"),
            P("row"),
            P("row", "col"),
            P(),
        ),
        out_specs=(
            P(("groups", "col"), "row"),
            P(("groups", "col"), "row"),
            P(("groups", "col"), "row"),
            P(("groups", "row"), "col"),
            P(("groups", "row")),
            P(("groups", "row")),
        ),
        check_vma=False,
    )
```

time: 436 us -> 252 us (0.58)
  waiting for transfers between devices: 209 us -> 72.2 us
  starting transfers between devices: 5.28 us -> 51.3 us
  blocking collectives: 43.5 us -> 0 us
  other arithmetic: 69 us -> 26.8 us
  between operations: 13.9 us -> 1.42 us
    all_gather x2 -> x0, waiting for transfers between devices: 106 us -> none  [the longest x1 56.3 us: local(): lax.all_gather(cotangent, 'row', axis=1, tiled=True)]
    ppermute x0 -> x57, waiting for transfers between devices: none -> 72.2 us  [the longest x32 64.2 us: shift(): lax.ppermute(x, 'row', [(order[i], order[(i + step) % n]) for i in range(...]
    reduce_scatter x2 -> x0, waiting for transfers between devices: 61.8 us -> none  [the longest x1 61.7 us: local(): lax.psum_scatter(branch_part, 'row', scatter_dimension=1, tiled=True)]
    ppermute x0 -> x57, starting transfers between devices: none -> 51.3 us  [the longest x32 30 us: shift(): lax.ppermute(x, 'row', [(order[i], order[(i + step) % n]) for i in range(...]
    reduce_sum x6 -> x5, other arithmetic: 54.7 us -> 5.15 us  [the longest x1 2.84 us: local(): grad_bias = jnp.sum(hidden_grad.astype(f32), axis=0)]
    psum x1 -> x0, waiting for transfers between devices: 39.6 us -> none  [local(): hidden_sum, act_grad = lax.psum((hidden_part, act_part), 'col')]
    dot_general x2 -> x4, matrix products: 24.6 us -> 61.8 us  [contract(): lax.dot_general(left, right, (((left_dim,), (right_dim,)), ((), ())), pre...]
    dot_general x4 -> x2, matrix products: 60.9 us -> 27.4 us  [the longest x1 14.8 us: local(): jnp.dot(activation, down_weight, preferred_element_type=f32).astype(bf16)]
  transfers between devices with their start and end apart: 6 -> 57, of which waited for: 4 -> 26; matrix products, arithmetic and copies ran while one was open for 27% -> 40% of each run, Pallas kernels for 0% -> 0%
where the time goes in v1:
time: 252 us
  matrix products  89.1 us (35%)
  waiting for transfers between devices  72.2 us (29%)
  starting transfers between devices  51.3 us (20%)
  other arithmetic  26.8 us (11%)
  local copies, waits for them, and re-layouts  10.7 us (4%)
    ppermute x32, waiting for transfers between devices, shift(): lax.ppermute(x, 'row', [(order[i], order[(i + step) % n]) for i in range(...  64.2 us
    dot_general x4, matrix products, contract(): lax.dot_general(left, right, (((left_dim,), (right_dim,)), ((), ())), pre...  61.8 us
    ppermute x32, starting transfers between devices, shift(): lax.ppermute(x, 'row', [(order[i], order[(i + step) % n]) for i in range(...  30 us
    dot_general x1, matrix products, local(): jnp.dot(activation, down_weight, preferred_element_type=f32).astype(bf16)  14.8 us
    ppermute x7, starting transfers between devices, every(): lax.ppermute(x, 'row', [(i, (i + k) % n) for i in range(n)])  14.7 us
    dot_general x1, matrix products, local(): hidden = summed(jnp.dot(normed_cols, up_weight, preferred_element_type=f32))  12.6 us
    ppermute x15, waiting for transfers between devices, swap(): return lax.ppermute(x, 'col', [(0, 1), (1, 0)])  8.02 us
  transfers between devices with their start and end apart: 57, of which 26 were waited for; matrix products, arithmetic and copies ran while one was open for 40% of the time, Pallas kernels for 0%

profile of v1, /device:TPU:0, one launch (start us, length us, event | category | flops | bytes accessed | tf_op | source)
XLA Modules:
  0.0 251.6 jit_solution(14817778548353157995)
XLA Ops:
  0.6 1.1 convert_reduce_fusion.1
  1.7 1.2 fusion.9
  2.9 5.1 %collective-permute-start.5 = (f32[2,192]{1,0:T(2,128)S(1)}, f32[2,192]{1,0:T(2,128)S(1)}, u32[]{:S(2)}, u32[]{:S(2)}) collective-permute-start(f32[2,192]{1,0:T(2,128)S(1)} %get-tuple-element.62), channel_id=1, source_target_pairs={{0,12},{2,14},{4,0},{6,2},{8,4},{10,6},{12,8},{14,10},{1,13},{3,15... | collective-permute-start | bytes 4616 | tf_op jit(solution)/shard_map/ppermute | solution.py:47
  8.4 3.5 %collective-permute-start.3 = (f32[2,192]{1,0:T(2,128)S(1)}, f32[2,192]{1,0:T(2,128)S(1)}, u32[]{:S(2)}, u32[]{:S(2)}) collective-permute-start(f32[2,192]{1,0:T(2,128)S(1)} %get-tuple-element.62), channel_id=1, source_target_pairs={{0,8},{2,10},{4,12},{6,14},{8,0},{10,2},{12,4},{14,6},{1,9},{3,11}... | collective-permute-start | bytes 4616 | tf_op jit(solution)/shard_map/ppermute | solution.py:47
  12.9 1.5 collective-permute-start
  14.4 3.2 %collective-permute-start.6 = (f32[2,192]{1,0:T(2,128)S(1)}, f32[2,192]{1,0:T(2,128)S(1)}, u32[]{:S(2)}, u32[]{:S(2)}) collective-permute-start(f32[2,192]{1,0:T(2,128)S(1)} %get-tuple-element.62), channel_id=1, source_target_pairs={{0,14},{2,0},{4,2},{6,4},{8,6},{10,8},{12,10},{14,12},{1,15},{3,1}... | collective-permute-start | bytes 4616 | tf_op jit(solution)/shard_map/ppermute | solution.py:47
  18.5 2.0 collective-permute-start.34
  20.6 1.2 fusion.13
  21.9 2.0 collective-permute-start.7
  23.9 4.7 %collective-permute-done.30 = bf16[192,768]{1,0:T(8,128)(2,1)S(1)} collective-permute-done((bf16[192,768]{1,0:T(8,128)(2,1)}, bf16[192,768]{1,0:T(8,128)(2,1)S(1)}, u32[]{:S(2)}, u32[]{:S(2)}) %collective-permute-start.30) | collective-permute-done | bytes 294944 | tf_op jit(solution)/shard_map/ppermute | solution.py:36
  28.7 1.9 collective-permute-start.35
  30.6 4.4 %collective-permute-done.11 = bf16[192,768]{1,0:T(8,128)(2,1)S(1)} collective-permute-done((bf16[192,768]{1,0:T(8,128)(2,1)S(1)}, bf16[192,768]{1,0:T(8,128)(2,1)S(1)}, u32[]{:S(2)}, u32[]{:S(2)}) %collective-permute-start.11) | collective-permute-done | bytes 294944 | tf_op jit(solution)/shard_map/ppermute | solution.py:36
  35.0 1.9 collective-permute-start.12
  37.0 4.2 %collective-permute-done.31 = bf16[192,768]{1,0:T(8,128)(2,1)S(1)} collective-permute-done((bf16[192,768]{1,0:T(8,128)(2,1)S(1)}, bf16[192,768]{1,0:T(8,128)(2,1)S(1)}, u32[]{:S(2)}, u32[]{:S(2)}) %collective-permute-start.31) | collective-permute-done | bytes 294944 | tf_op jit(solution)/shard_map/ppermute | solution.py:36
  41.5 2.0 collective-permute-start.36
  43.4 1.0 collective-permute-done.12
  44.5 3.1 %collective-permute-done.8 = bf16[192,768]{1,0:T(8,128)(2,1)S(1)} collective-permute-done((bf16[192,768]{1,0:T(8,128)(2,1)S(1)}, bf16[192,768]{1,0:T(8,128)(2,1)S(1)}, u32[]{:S(2)}, u32[]{:S(2)}) %collective-permute-start.8) | collective-permute-done | bytes 294944 | tf_op jit(solution)/shard_map/ppermute | solution.py:36
  47.8 3.0 %collective-permute-done.32 = bf16[192,768]{1,0:T(8,128)(2,1)S(1)} collective-permute-done((bf16[192,768]{1,0:T(8,128)(2,1)S(1)}, bf16[192,768]{1,0:T(8,128)(2,1)S(1)}, u32[]{:S(2)}, u32[]{:S(2)}) %collective-permute-start.32) | collective-permute-done | bytes 294944 | tf_op jit(solution)/shard_map/ppermute | solution.py:36
  51.1 1.1 collective-permute-start.33
  52.3 4.9 %collective-permute-done.13 = bf16[192,768]{1,0:T(8,128)(2,1)S(1)} collective-permute-done((bf16[192,768]{1,0:T(8,128)(2,1)S(1)}, bf16[192,768]{1,0:T(8,128)(2,1)S(1)}, u32[]{:S(2)}, u32[]{:S(2)}) %collective-permute-start.13) | collective-permute-done | bytes 294944 | tf_op jit(solution)/shard_map/ppermute | solution.py:36
  57.3 1.4 collective-permute-done.9
  60.5 4.9 %collective-permute-done.37 = bf16[96,768]{1,0:T(8,128)(2,1)S(1)} collective-permute-done((bf16[96,768]{1,0:T(8,128)(2,1)S(1)}, bf16[96,768]{1,0:T(8,128)(2,1)S(1)}, u32[]{:S(2)}, u32[]{:S(2)}) %collective-permute-start.37) | collective-permute-done | bytes 147488 | tf_op jit(solution)/shard_map/ppermute | solution.py:36
  66.2 4.4 %collective-permute-done.10 = bf16[96,768]{1,0:T(8,128)(2,1)S(1)} collective-permute-done((bf16[96,768]{1,0:T(8,128)(2,1)S(1)}, bf16[96,768]{1,0:T(8,128)(2,1)S(1)}, u32[]{:S(2)}, u32[]{:S(2)}) %collective-permute-start.10) | collective-permute-done | bytes 147488 | tf_op jit(solution)/shard_map/ppermute | solution.py:36
  71.5 1.1 collective-permute-done.38
  74.0 11.7 %fusion.37 = f32[384,3072]{1,0:T(8,128)S(1)} fusion(bf16[384,3072]{1,0:T(8,128)(2,1)S(1)} %maximum_dynamic-update-slice_fusion.7, bf16[3072,3072]{1,0:T(8,128)(2,1)} %param.10), kind=kOutput, calls=%fused_computation.122 | convolution fusion | flops 7247757312 | bytes 25952256 | tf_op jit(solution)/shard_map/dot_general | solution.py:21
  86.4 12.6 %fusion.36 = f32[384,3072]{1,0:T(8,128)S(1)} fusion(bf16[384,3072]{1,0:T(8,128)(2,1)S(1)} %maximum_dynamic-update-slice_fusion.3, bf16[3072,3072]{1,0:T(8,128)(2,1)} %param.8), kind=kOutput, calls=%fused_computation.121 | convolution fusion | flops 7247757312 | bytes 25952256 | tf_op jit(solution)/shard_map/dot_general | solution.py:161
  99.4 1.7 copy-done.5
  101.2 1.6 pad_maximum_fusion
  103.1 1.6 pad_maximum_fusion.1
  104.9 2.6 %collective-permute-done.19 = f32[384,1536]{1,0:T(8,128)S(1)} collective-permute-done((f32[384,1536]{1,0:T(8,128)}, f32[384,1536]{1,0:T(8,128)S(1)}, u32[]{:S(2)}, u32[]{:S(2)}) %collective-permute-start.19) | collective-permute-done | bytes 2359328 | tf_op jit(solution)/shard_map/ppermute | solution.py:95
  107.5 1.4 copy-done.7
  108.9 2.1 collective-permute-done.42
  111.0 4.4 %fusion.7 = (bf16[384,1536]{1,0:T(8,128)(2,1)S(1)}, bf16[384,1536]{1,0:T(8,128)(2,1)S(1)}) fusion(f32[384,1536]{1,0:T(8,128)} %collective-permute-done.42, f32[384,3072]{1,0:T(8,128)} %copy-done.4, s32[]{:T(128)S(6)} %select_n.376, f32[1536]{0:T(1024)S(1)} %dynamic_slice.79, f32[384,1536]{1,0:T(8,128)} %copy-done.7, f32[384,3072]{1,0:T(8,128)} %copy-done.5), kind=kLoop, calls=%fused_computation.14 | loop fusion | flops 8847360 | bytes 11802628 | tf_op jit(solution)/shard_map/convert_element_type | solution.py:166
  116.4 2.2 collective-permute-done.20
  118.6 14.8 %convolution_convert_fusion.2 = bf16[384,3072]{1,0:T(8,128)(2,1)S(1)} fusion(bf16[3072,3072]{1,0:T(8,128)(2,1)} %param.10, bf16[384,1536]{1,0:T(8,128)(2,1)} %collective-permute-done.20, bf16[384,1536]{1,0:T(8,128)(2,1)S(1)} %get-tuple-element.12, pred[]{:T(512)S(6)} %eq.32), kind=kOutput, calls=%fused_computation.5 | convolution fusion | flops 7259553792 | bytes 23592960 | tf_op jit(solution)/shard_map/dot_general | solution.py:179
  133.4 1.2 fusion.30
  134.9 17.2 %fusion.1 = (f32[384]{0:T(512)S(1)}, f32[3072]{0:T(1024)S(1)}, f32[384]{0:T(512)S(1)}, bf16[384,3072]{1,0:T(8,128)(2,1)}) fusion(bf16[384,3072]{1,0:T(8,128)(2,1)} %copy-done.8, f32[3072]{0:T(1024)S(1)} %dynamic-slice-done, bf16[3072,3072]{1,0:T(8,128)(2,1)} %param.8, bf16[384,1536]{1,0:T(8,128)(2,1)} %collective-permute-done.43, ...), kind=kOutput, calls=%fused_computation.8 | convolution fusion | flops 7266627584 | bytes 25979904 | tf_op jit(solution)/shard_map/dot_general | solution.py:21
  153.0 2.8 %fusion.29 = (bf16[192,3072]{1,0:T(8,128)(2,1)S(1)}, bf16[192,3072]{1,0:T(8,128)(2,1)}) fusion(bf16[384,3072]{1,0:T(8,128)(2,1)} %get-tuple-element.13), kind=kLoop, calls=%fused_computation.114 | loop fusion | bytes 4718592 | tf_op jit(solution)/shard_map/slice | solution.py:169
  157.0 16.3 %convolution_convert_fusion.1 = bf16[3072,3072]{1,0:T(8,128)(2,1)} fusion(bf16[384,3072]{1,0:T(8,128)(2,1)} %copy-done.8, bf16[384,1536]{1,0:T(8,128)(2,1)} %collective-permute-done.43, bf16[384,1536]{1,0:T(8,128)(2,1)S(1)} %get-tuple-element.11, pred[]{:T(512)S(6)} %eq.32), kind=kOutput, calls=%fused_computation.1 | convolution fusion | flops 7267811328 | bytes 23592960 | tf_op jit(solution)/shard_map/dot_general | solution.py:21
  173.7 16.6 %convolution_convert_fusion = bf16[3072,3072]{1,0:T(8,128)(2,1)} fusion(bf16[384,3072]{1,0:T(8,128)(2,1)} %copy-done.9, bf16[384,1536]{1,0:T(8,128)(2,1)} %collective-permute-done.20, bf16[384,1536]{1,0:T(8,128)(2,1)S(1)} %copy-done.3, pred[]{:T(512)S(6)} %eq.32), kind=kOutput, calls=%fused_computation | convolution fusion | flops 7267811328 | bytes 23592960 | tf_op jit(solution)/shard_map/dot_general | solution.py:21
  190.3 1.8 collective-permute-start.56
  192.1 1.4 broadcast_select_fusion.3
  194.5 1.1 collective-permute-start.26
  197.1 1.1 collective-permute-start.49
  198.1 3.1 %collective-permute-done.26 = bf16[96,768]{1,0:T(8,128)(2,1)S(1)} collective-permute-done((bf16[96,768]{1,0:T(8,128)(2,1)S(1)}, bf16[96,768]{1,0:T(8,128)(2,1)S(1)}, u32[]{:S(2)}, u32[]{:S(2)}) %collective-permute-start.26) | collective-permute-done | bytes 147488 | tf_op jit(solution)/shard_map/ppermute | solution.py:36
  201.3 1.1 collective-permute-start.27
  204.5 1.3 collective-permute-start.50
  205.8 6.7 %collective-permute-done.23 = bf16[192,768]{1,0:T(8,128)(2,1)S(1)} collective-permute-done((bf16[192,768]{1,0:T(8,128)(2,1)S(1)}, bf16[192,768]{1,0:T(8,128)(2,1)S(1)}, u32[]{:S(2)}, u32[]{:S(2)}) %collective-permute-start.23) | collective-permute-done | bytes 294944 | tf_op jit(solution)/shard_map/ppermute | solution.py:36
  212.5 1.1 add_convert_fusion.7
  214.6 4.2 %collective-permute-done.46 = bf16[192,768]{1,0:T(8,128)(2,1)S(1)} collective-permute-done((bf16[192,768]{1,0:T(8,128)(2,1)S(1)}, bf16[192,768]{1,0:T(8,128)(2,1)S(1)}, u32[]{:S(2)}, u32[]{:S(2)}) %collective-permute-start.46) | collective-permute-done | bytes 294944 | tf_op jit(solution)/shard_map/ppermute | solution.py:36
  219.9 2.8 %convert_reduce_fusion = f32[3072]{0:T(1024)} fusion(bf16[384,1536]{1,0:T(8,128)(2,1)S(1)} %get-tuple-element.11, bf16[384,1536]{1,0:T(8,128)(2,1)} %collective-permute-done.43, pred[]{:T(512)S(6)} %eq.32), kind=kLoop, calls=%fused_computation.2 | loop fusion | flops 12973056 | bytes 2371585 | tf_op jit(solution)/shard_map/reduce_sum | solution.py:199
  222.8 1.2 collective-permute-done.24
  224.0 2.0 add_convert_fusion.6
  226.0 1.1 collective-permute-start.28
  228.2 1.3 collective-permute-start.51
  232.5 2.5 collective-permute-done.28
  235.0 1.2 add_convert_fusion.4
  236.2 1.2 collective-permute-start.29
  237.4 3.9 %collective-permute-done.51 = bf16[192,768]{1,0:T(8,128)(2,1)} collective-permute-done((bf16[192,768]{1,0:T(8,128)(2,1)}, bf16[192,768]{1,0:T(8,128)(2,1)}, u32[]{:S(2)}, u32[]{:S(2)}) %collective-permute-start.51) | collective-permute-done | bytes 294944 | tf_op jit(solution)/shard_map/ppermute | solution.py:36
  241.3 1.2 add_convert_fusion
  242.5 1.2 collective-permute-start.52
  243.7 2.0 collective-permute-done.29
  245.8 3.5 %collective-permute-done.52 = bf16[192,768]{1,0:T(8,128)(2,1)S(1)} collective-permute-done((bf16[192,768]{1,0:T(8,128)(2,1)S(1)}, bf16[192,768]{1,0:T(8,128)(2,1)S(1)}, u32[]{:S(2)}, u32[]{:S(2)}) %collective-permute-start.52) | collective-permute-done | bytes 294944 | tf_op jit(solution)/shard_map/ppermute | solution.py:36
  249.3 2.3 fusion.17
  (186 shorter events, 24.6 us)
Async XLA Ops:
  2.9 9.9 %collective-permute-start.5 = (f32[2,192]{1,0:T(2,128)S(1)}, f32[2,192]{1,0:T(2,128)S(1)}, u32[]{:S(2)}, u32[]{:S(2)}) collective-permute-start(f32[2,192]{1,0:T(2,128)S(1)} %get-tuple-element.62), channel_id=1, source_target_pairs={{0,12},{2,14},{4,0},{6,2},{8,4},{10,6},{12,8},{14,10},{1,13},{3,15... | collective-permute-start | bytes 4616 | tf_op jit(solution)/shard_map/ppermute | solution.py:47
  8.0 6.3 %collective-permute-start.4 = (f32[2,192]{1,0:T(2,128)S(1)}, f32[2,192]{1,0:T(2,128)S(1)}, u32[]{:S(2)}, u32[]{:S(2)}) collective-permute-start(f32[2,192]{1,0:T(2,128)S(1)} %get-tuple-element.62), channel_id=1, source_target_pairs={{0,10},{2,12},{4,14},{6,0},{8,2},{10,4},{12,6},{14,8},{1,11},{3,13... | collective-permute-start | bytes 4616 | tf_op jit(solution)/shard_map/ppermute | solution.py:47
  8.4 10.0 %collective-permute-start.3 = (f32[2,192]{1,0:T(2,128)S(1)}, f32[2,192]{1,0:T(2,128)S(1)}, u32[]{:S(2)}, u32[]{:S(2)}) collective-permute-start(f32[2,192]{1,0:T(2,128)S(1)} %get-tuple-element.62), channel_id=1, source_target_pairs={{0,8},{2,10},{4,12},{6,14},{8,0},{10,2},{12,4},{14,6},{1,9},{3,11}... | collective-permute-start | bytes 4616 | tf_op jit(solution)/shard_map/ppermute | solution.py:47
  11.9 6.6 %collective-permute-start.2 = (f32[2,192]{1,0:T(2,128)S(1)}, f32[2,192]{1,0:T(2,128)S(1)}, u32[]{:S(2)}, u32[]{:S(2)}) collective-permute-start(f32[2,192]{1,0:T(2,128)S(1)} %get-tuple-element.62), channel_id=1, source_target_pairs={{0,6},{2,8},{4,10},{6,12},{8,14},{10,0},{12,2},{14,4},{1,7},{3,9},... | collective-permute-start | bytes 4616 | tf_op jit(solution)/shard_map/ppermute | solution.py:47
  11.9 8.6 %collective-permute-start.1 = (f32[2,192]{1,0:T(2,128)S(1)}, f32[2,192]{1,0:T(2,128)S(1)}, u32[]{:S(2)}, u32[]{:S(2)}) collective-permute-start(f32[2,192]{1,0:T(2,128)S(1)} %get-tuple-element.62), channel_id=1, source_target_pairs={{0,4},{2,6},{4,8},{6,10},{8,12},{10,14},{12,0},{14,2},{1,5},{3,7},... | collective-permute-start | bytes 4616 | tf_op jit(solution)/shard_map/ppermute | solution.py:47
  12.9 7.6 %collective-permute-start = (f32[2,192]{1,0:T(2,128)S(1)}, f32[2,192]{1,0:T(2,128)S(1)}, u32[]{:S(2)}, u32[]{:S(2)}) collective-permute-start(f32[2,192]{1,0:T(2,128)S(1)} %get-tuple-element.62), channel_id=1, source_target_pairs={{0,2},{2,4},{4,6},{6,8},{8,10},{10,12},{12,14},{14,0},{1,3},{3,5},... | collective-permute-start | bytes 4616 | tf_op jit(solution)/shard_map/ppermute | solution.py:47
  14.4 6.1 %collective-permute-start.6 = (f32[2,192]{1,0:T(2,128)S(1)}, f32[2,192]{1,0:T(2,128)S(1)}, u32[]{:S(2)}, u32[]{:S(2)}) collective-permute-start(f32[2,192]{1,0:T(2,128)S(1)} %get-tuple-element.62), channel_id=1, source_target_pairs={{0,14},{2,0},{4,2},{6,4},{8,6},{10,8},{12,10},{14,12},{1,15},{3,1}... | collective-permute-start | bytes 4616 | tf_op jit(solution)/shard_map/ppermute | solution.py:47
  18.4 10.2 %collective-permute-start.30 = (bf16[192,768]{1,0:T(8,128)(2,1)}, bf16[192,768]{1,0:T(8,128)(2,1)S(1)}, u32[]{:S(2)}, u32[]{:S(2)}) collective-permute-start(bf16[192,768]{1,0:T(8,128)(2,1)} %param.7), channel_id=1, source_target_pairs={{0,2},{4,0},{8,4},{12,8},{14,12},{10,14},{6,10},{2,6},{1,3},{5,1},... | collective-permute-start | bytes 884744 | tf_op jit(solution)/shard_map/ppermute | solution.py:36
  18.5 10.2 %collective-permute-start.34 = (bf16[192,768]{1,0:T(8,128)(2,1)}, bf16[192,768]{1,0:T(8,128)(2,1)S(1)}, u32[]{:S(2)}, u32[]{:S(2)}) collective-permute-start(bf16[192,768]{1,0:T(8,128)(2,1)} %param.7), channel_id=1, source_target_pairs={{0,4},{4,8},{8,12},{12,14},{14,10},{10,6},{6,2},{2,0},{1,5},{5,9},... | collective-permute-start | bytes 884744 | tf_op jit(solution)/shard_map/ppermute | solution.py:36
  21.8 13.2 %collective-permute-start.11 = (bf16[192,768]{1,0:T(8,128)(2,1)S(1)}, bf16[192,768]{1,0:T(8,128)(2,1)S(1)}, u32[]{:S(2)}, u32[]{:S(2)}) collective-permute-start(bf16[192,768]{1,0:T(8,128)(2,1)S(1)} %fusion.13), channel_id=1, source_target_pairs={{0,4},{4,8},{8,12},{12,14},{14,10},{10,6},{6,2},{2,0},{1,5},{5,9},... | collective-permute-start | bytes 884744 | tf_op jit(solution)/shard_map/ppermute | solution.py:36
  21.9 15.1 %collective-permute-start.7 = (bf16[192,768]{1,0:T(8,128)(2,1)S(1)}, bf16[192,768]{1,0:T(8,128)(2,1)S(1)}, u32[]{:S(2)}, u32[]{:S(2)}) collective-permute-start(bf16[192,768]{1,0:T(8,128)(2,1)S(1)} %fusion.13), channel_id=1, source_target_pairs={{0,2},{4,0},{8,4},{12,8},{14,12},{10,14},{6,10},{2,6},{1,3},{5,1},... | collective-permute-start | bytes 884744 | tf_op jit(solution)/shard_map/ppermute | solution.py:36
  28.6 12.6 %collective-permute-start.31 = (bf16[192,768]{1,0:T(8,128)(2,1)S(1)}, bf16[192,768]{1,0:T(8,128)(2,1)S(1)}, u32[]{:S(2)}, u32[]{:S(2)}) collective-permute-start(bf16[192,768]{1,0:T(8,128)(2,1)S(1)} %collective-permute-done.30), channel_id=1, source_target_pairs={{0,2},{4,0},{8,4},{12,8},{14,12},{10,14},{6,10},{2,6},{1,3},{5,1},... | collective-permute-start | bytes 884744 | tf_op jit(solution)/shard_map/ppermute | solution.py:36
  28.7 12.6 %collective-permute-start.35 = (bf16[192,768]{1,0:T(8,128)(2,1)S(1)}, bf16[192,768]{1,0:T(8,128)(2,1)S(1)}, u32[]{:S(2)}, u32[]{:S(2)}) collective-permute-start(bf16[192,768]{1,0:T(8,128)(2,1)S(1)} %collective-permute-done.34), channel_id=1, source_target_pairs={{0,4},{4,8},{8,12},{12,14},{14,10},{10,6},{6,2},{2,0},{1,5},{5,9},... | collective-permute-start | bytes 884744 | tf_op jit(solution)/shard_map/ppermute | solution.py:36
  35.0 9.5 %collective-permute-start.12 = (bf16[192,768]{1,0:T(8,128)(2,1)S(1)}, bf16[192,768]{1,0:T(8,128)(2,1)S(1)}, u32[]{:S(2)}, u32[]{:S(2)}) collective-permute-start(bf16[192,768]{1,0:T(8,128)(2,1)S(1)} %collective-permute-done.11), channel_id=1, source_target_pairs={{0,4},{4,8},{8,12},{12,14},{14,10},{10,6},{6,2},{2,0},{1,5},{5,9},... | collective-permute-start | bytes 884744 | tf_op jit(solution)/shard_map/ppermute | solution.py:36
  37.0 10.6 %collective-permute-start.8 = (bf16[192,768]{1,0:T(8,128)(2,1)S(1)}, bf16[192,768]{1,0:T(8,128)(2,1)S(1)}, u32[]{:S(2)}, u32[]{:S(2)}) collective-permute-start(bf16[192,768]{1,0:T(8,128)(2,1)S(1)} %collective-permute-done.7), channel_id=1, source_target_pairs={{0,2},{4,0},{8,4},{12,8},{14,12},{10,14},{6,10},{2,6},{1,3},{5,1},... | collective-permute-start | bytes 884744 | tf_op jit(solution)/shard_map/ppermute | solution.py:36
  41.2 9.5 %collective-permute-start.32 = (bf16[192,768]{1,0:T(8,128)(2,1)S(1)}, bf16[192,768]{1,0:T(8,128)(2,1)S(1)}, u32[]{:S(2)}, u32[]{:S(2)}) collective-permute-start(bf16[192,768]{1,0:T(8,128)(2,1)S(1)} %collective-permute-done.31), channel_id=1, source_target_pairs={{0,2},{4,0},{8,4},{12,8},{14,12},{10,14},{6,10},{2,6},{1,3},{5,1},... | collective-permute-start | bytes 884744 | tf_op jit(solution)/shard_map/ppermute | solution.py:36
  41.4 32.2 %collective-permute-start.40 = (bf16[192,768]{1,0:T(8,128)(2,1)S(1)}, bf16[192,768]{1,0:T(8,128)(2,1)S(1)}, u32[]{:S(2)}, u32[]{:S(2)}) collective-permute-start(bf16[192,768]{1,0:T(8,128)(2,1)S(1)} %get-tuple-element.39), channel_id=1, source_target_pairs={{0,1},{1,0},{2,3},{3,2},{4,5},{5,4},{6,7},{7,6},{8,9},{9,8},{10,11... | collective-permute-start | bytes 884744 | tf_op jit(solution)/shard_map/ppermute | solution.py:95
  41.5 9.7 %collective-permute-start.36 = (bf16[192,768]{1,0:T(8,128)(2,1)S(1)}, bf16[192,768]{1,0:T(8,128)(2,1)S(1)}, u32[]{:S(2)}, u32[]{:S(2)}) collective-permute-start(bf16[192,768]{1,0:T(8,128)(2,1)S(1)} %collective-permute-done.35), channel_id=1, source_target_pairs={{0,4},{4,8},{8,12},{12,14},{14,10},{10,6},{6,2},{2,0},{1,5},{5,9},... | collective-permute-start | bytes 884744 | tf_op jit(solution)/shard_map/ppermute | solution.py:36
  47.6 38.6 %collective-permute-start.17 = (bf16[192,768]{1,0:T(8,128)(2,1)S(1)}, bf16[192,768]{1,0:T(8,128)(2,1)S(1)}, u32[]{:S(2)}, u32[]{:S(2)}) collective-permute-start(bf16[192,768]{1,0:T(8,128)(2,1)S(1)} %get-tuple-element.47), channel_id=1, source_target_pairs={{0,1},{1,0},{2,3},{3,2},{4,5},{5,4},{6,7},{7,6},{8,9},{9,8},{10,11... | collective-permute-start | bytes 884744 | tf_op jit(solution)/shard_map/ppermute | solution.py:95
  47.7 9.5 %collective-permute-start.13 = (bf16[192,768]{1,0:T(8,128)(2,1)S(1)}, bf16[192,768]{1,0:T(8,128)(2,1)S(1)}, u32[]{:S(2)}, u32[]{:S(2)}) collective-permute-start(bf16[192,768]{1,0:T(8,128)(2,1)S(1)} %collective-permute-done.12), channel_id=1, source_target_pairs={{0,4},{4,8},{8,12},{12,14},{14,10},{10,6},{6,2},{2,0},{1,5},{5,9},... | collective-permute-start | bytes 884744 | tf_op jit(solution)/shard_map/ppermute | solution.py:36
  50.7 8.0 %collective-permute-start.9 = (bf16[192,768]{1,0:T(8,128)(2,1)S(1)}, bf16[192,768]{1,0:T(8,128)(2,1)S(1)}, u32[]{:S(2)}, u32[]{:S(2)}) collective-permute-start(bf16[192,768]{1,0:T(8,128)(2,1)S(1)} %collective-permute-done.8), channel_id=1, source_target_pairs={{0,2},{4,0},{8,4},{12,8},{14,12},{10,14},{6,10},{2,6},{1,3},{5,1},... | collective-permute-start | bytes 884744 | tf_op jit(solution)/shard_map/ppermute | solution.py:36
  51.1 15.0 %copy-start.10 = (bf16[192,768]{1,0:T(8,128)(2,1)S(1)}, bf16[192,768]{1,0:T(8,128)(2,1)}, u32[]{:S(2)}) copy-start(bf16[192,768]{1,0:T(8,128)(2,1)} %param.7) | copy-start | bytes 884740
  51.1 9.1 %collective-permute-start.33 = (bf16[96,768]{1,0:T(8,128)(2,1)S(1)}, bf16[96,768]{1,0:T(8,128)(2,1)S(1)}, u32[]{:S(2)}, u32[]{:S(2)}) collective-permute-start(bf16[96,768]{1,0:T(8,128)(2,1)S(1)} %slice.160), channel_id=1, source_target_pairs={{0,2},{4,0},{8,4},{12,8},{14,12},{10,14},{6,10},{2,6},{1,3},{5,1},... | collective-permute-start | bytes 442376 | tf_op jit(solution)/shard_map/ppermute | solution.py:36
  57.2 16.7 %collective-permute-start.41 = (bf16[192,768]{1,0:T(8,128)(2,1)S(1)}, bf16[192,768]{1,0:T(8,128)(2,1)S(1)}, u32[]{:S(2)}, u32[]{:S(2)}) collective-permute-start(bf16[192,768]{1,0:T(8,128)(2,1)S(1)} %get-tuple-element.37), channel_id=1, source_target_pairs={{0,1},{1,0},{2,3},{3,2},{4,5},{5,4},{6,7},{7,6},{8,9},{9,8},{10,11... | collective-permute-start | bytes 884744 | tf_op jit(solution)/shard_map/ppermute | solution.py:95
  57.3 13.9 %copy-start = (bf16[192,768]{1,0:T(8,128)(2,1)S(1)}, bf16[192,768]{1,0:T(8,128)(2,1)}, u32[]{:S(2)}) copy-start(bf16[192,768]{1,0:T(8,128)(2,1)} %param.6) | copy-start | bytes 884740
  58.7 6.7 %collective-permute-start.37 = (bf16[96,768]{1,0:T(8,128)(2,1)S(1)}, bf16[96,768]{1,0:T(8,128)(2,1)S(1)}, u32[]{:S(2)}, u32[]{:S(2)}) collective-permute-start(bf16[96,768]{1,0:T(8,128)(2,1)S(1)} %slice.161), channel_id=1, source_target_pairs={{0,4},{4,8},{8,12},{12,14},{14,10},{10,6},{6,2},{2,0},{1,5},{5,9},... | collective-permute-start | bytes 442376 | tf_op jit(solution)/shard_map/ppermute | solution.py:36
  60.3 10.3 %collective-permute-start.14 = (bf16[96,768]{1,0:T(8,128)(2,1)S(1)}, bf16[96,768]{1,0:T(8,128)(2,1)S(1)}, u32[]{:S(2)}, u32[]{:S(2)}) collective-permute-start(bf16[96,768]{1,0:T(8,128)(2,1)S(1)} %slice.149), channel_id=1, source_target_pairs={{0,4},{4,8},{8,12},{12,14},{14,10},{10,6},{6,2},{2,0},{1,5},{5,9},... | collective-permute-start | bytes 442376 | tf_op jit(solution)/shard_map/ppermute | solution.py:36
  65.4 5.1 %collective-permute-start.10 = (bf16[96,768]{1,0:T(8,128)(2,1)S(1)}, bf16[96,768]{1,0:T(8,128)(2,1)S(1)}, u32[]{:S(2)}, u32[]{:S(2)}) collective-permute-start(bf16[96,768]{1,0:T(8,128)(2,1)S(1)} %slice.148), channel_id=1, source_target_pairs={{0,2},{4,0},{8,4},{12,8},{14,12},{10,14},{6,10},{2,6},{1,3},{5,1},... | collective-permute-start | bytes 442376 | tf_op jit(solution)/shard_map/ppermute | solution.py:36
  70.5 2.5 %collective-permute-start.39 = (bf16[192,768]{1,0:T(8,128)(2,1)S(1)}, bf16[192,768]{1,0:T(8,128)(2,1)S(1)}, u32[]{:S(2)}, u32[]{:S(2)}) collective-permute-start(bf16[192,768]{1,0:T(8,128)(2,1)S(1)} %get-tuple-element.41), channel_id=1, source_target_pairs={{0,1},{1,0},{2,3},{3,2},{4,5},{5,4},{6,7},{7,6},{8,9},{9,8},{10,11... | collective-permute-start | bytes 884744 | tf_op jit(solution)/shard_map/ppermute | solution.py:95
  70.6 2.0 collective-permute-start.38
  72.6 13.6 %collective-permute-start.16 = (bf16[192,768]{1,0:T(8,128)(2,1)S(1)}, bf16[192,768]{1,0:T(8,128)(2,1)S(1)}, u32[]{:S(2)}, u32[]{:S(2)}) collective-permute-start(bf16[192,768]{1,0:T(8,128)(2,1)S(1)} %get-tuple-element.49), channel_id=1, source_target_pairs={{0,1},{1,0},{2,3},{3,2},{4,5},{5,4},{6,7},{7,6},{8,9},{9,8},{10,11... | collective-permute-start | bytes 884744 | tf_op jit(solution)/shard_map/ppermute | solution.py:95
  73.1 13.2 %collective-permute-start.18 = (bf16[192,768]{1,0:T(8,128)(2,1)S(1)}, bf16[192,768]{1,0:T(8,128)(2,1)S(1)}, u32[]{:S(2)}, u32[]{:S(2)}) collective-permute-start(bf16[192,768]{1,0:T(8,128)(2,1)S(1)} %get-tuple-element.45), channel_id=1, source_target_pairs={{0,1},{1,0},{2,3},{3,2},{4,5},{5,4},{6,7},{7,6},{8,9},{9,8},{10,11... | collective-permute-start | bytes 884744 | tf_op jit(solution)/shard_map/ppermute | solution.py:95
  73.6 12.2 %collective-permute-start.15 = (bf16[192,768]{1,0:T(8,128)(2,1)S(1)}, bf16[192,768]{1,0:T(8,128)(2,1)S(1)}, u32[]{:S(2)}, u32[]{:S(2)}) collective-permute-start(bf16[192,768]{1,0:T(8,128)(2,1)S(1)} %get-tuple-element.51), channel_id=1, source_target_pairs={{0,1},{1,0},{2,3},{3,2},{4,5},{5,4},{6,7},{7,6},{8,9},{9,8},{10,11... | collective-permute-start | bytes 884744 | tf_op jit(solution)/shard_map/ppermute | solution.py:95
  85.7 13.2 %copy-start.4 = (f32[384,3072]{1,0:T(8,128)}, f32[384,3072]{1,0:T(8,128)S(1)}, u32[]{:S(2)}) copy-start(f32[384,3072]{1,0:T(8,128)S(1)} %fusion.37) | copy-start | bytes 14155780
  102.8 4.7 %collective-permute-start.19 = (f32[384,1536]{1,0:T(8,128)}, f32[384,1536]{1,0:T(8,128)S(1)}, u32[]{:S(2)}, u32[]{:S(2)}) collective-permute-start(f32[384,1536]{1,0:T(8,128)} %pad_maximum_fusion), channel_id=1, source_target_pairs={{0,1},{1,0},{2,3},{3,2},{4,5},{5,4},{6,7},{7,6},{8,9},{9,8},{10,11... | collective-permute-start | bytes 7077896 | tf_op jit(solution)/shard_map/ppermute | solution.py:95
  104.7 6.3 %collective-permute-start.42 = (f32[384,1536]{1,0:T(8,128)}, f32[384,1536]{1,0:T(8,128)}, u32[]{:S(2)}, u32[]{:S(2)}) collective-permute-start(f32[384,1536]{1,0:T(8,128)} %pad_maximum_fusion.1), channel_id=1, source_target_pairs={{0,1},{1,0},{2,3},{3,2},{4,5},{5,4},{6,7},{7,6},{8,9},{9,8},{10,11... | collective-permute-start | bytes 7077896 | tf_op jit(solution)/shard_map/ppermute | solution.py:95
  115.6 3.0 %collective-permute-start.20 = (bf16[384,1536]{1,0:T(8,128)(2,1)S(1)}, bf16[384,1536]{1,0:T(8,128)(2,1)}, u32[]{:S(2)}, u32[]{:S(2)}) collective-permute-start(bf16[384,1536]{1,0:T(8,128)(2,1)S(1)} %pad_maximum_fusion.2), channel_id=1, source_target_pairs={{0,1},{1,0},{2,3},{3,2},{4,5},{5,4},{6,7},{7,6},{8,9},{9,8},{10,11... | collective-permute-start | bytes 3538952 | tf_op jit(solution)/shard_map/ppermute | solution.py:95
  116.2 18.8 %collective-permute-start.43 = (bf16[384,1536]{1,0:T(8,128)(2,1)S(1)}, bf16[384,1536]{1,0:T(8,128)(2,1)}, u32[]{:S(2)}, u32[]{:S(2)}) collective-permute-start(bf16[384,1536]{1,0:T(8,128)(2,1)S(1)} %pad_maximum_fusion.3), channel_id=1, source_target_pairs={{0,1},{1,0},{2,3},{3,2},{4,5},{5,4},{6,7},{7,6},{8,9},{9,8},{10,11... | collective-permute-start | bytes 3538952 | tf_op jit(solution)/shard_map/ppermute | solution.py:95
  134.6 57.5 %collective-permute-start.21 = (bf16[192,3072]{1,0:T(8,128)(2,1)}, bf16[192,3072]{1,0:T(8,128)(2,1)}, u32[]{:S(2)}, u32[]{:S(2)}) collective-permute-start(bf16[192,3072]{1,0:T(8,128)(2,1)} %get-tuple-element.31), channel_id=1, source_target_pairs={{0,1},{1,0},{2,3},{3,2},{4,5},{5,4},{6,7},{7,6},{8,9},{9,8},{10,11... | collective-permute-start | bytes 3538952 | tf_op jit(solution)/shard_map/ppermute | solution.py:95
  152.8 3.4 %collective-permute-start.53 = (f32[6912]{0:T(1024)S(1)}, f32[6912]{0:T(1024)S(1)}, u32[]{:S(2)}, u32[]{:S(2)}) collective-permute-start(f32[6912]{0:T(1024)S(1)} %pad_maximum_fusion.8), channel_id=1, source_target_pairs={{0,1},{1,0},{2,3},{3,2},{4,5},{5,4},{6,7},{7,6},{8,9},{9,8},{10,11... | collective-permute-start | bytes 82952 | tf_op jit(solution)/shard_map/ppermute | solution.py:95
  155.8 39.8 %collective-permute-start.44 = (bf16[192,3072]{1,0:T(8,128)(2,1)}, bf16[192,3072]{1,0:T(8,128)(2,1)S(1)}, u32[]{:S(2)}, u32[]{:S(2)}) collective-permute-start(bf16[192,3072]{1,0:T(8,128)(2,1)} %get-tuple-element.24), channel_id=1, source_target_pairs={{0,1},{1,0},{2,3},{3,2},{4,5},{5,4},{6,7},{7,6},{8,9},{9,8},{10,11... | collective-permute-start | bytes 3538952 | tf_op jit(solution)/shard_map/ppermute | solution.py:95
  156.2 17.5 %copy-start.3 = (bf16[384,1536]{1,0:T(8,128)(2,1)S(1)}, bf16[384,1536]{1,0:T(8,128)(2,1)}, u32[]{:S(2)}) copy-start(bf16[384,1536]{1,0:T(8,128)(2,1)} %copy-done.2) | copy-start | bytes 3538948
  156.2 17.0 %collective-permute-start.54 = (f32[6912]{0:T(1024)S(1)}, f32[6912]{0:T(1024)S(1)}, u32[]{:S(2)}, u32[]{:S(2)}) collective-permute-start(f32[6912]{0:T(1024)S(1)} %fusion.25), channel_id=1, source_target_pairs={{0,2},{2,0},{4,6},{6,4},{8,10},{10,8},{12,14},{14,12},{1,3},{3,1},... | collective-permute-start | bytes 82952 | tf_op jit(solution)/shard_map/ppermute | solution.py:53
  173.2 17.0 %collective-permute-start.55 = (f32[6912]{0:T(1024)S(1)}, f32[6912]{0:T(1024)S(1)}, u32[]{:S(2)}, u32[]{:S(2)}) collective-permute-start(f32[6912]{0:T(1024)S(1)} %add.316), channel_id=1, source_target_pairs={{0,4},{2,6},{4,0},{6,2},{8,12},{10,14},{12,8},{14,10},{1,5},{3,7},... | collective-permute-start | bytes 82952 | tf_op jit(solution)/shard_map/ppermute | solution.py:53
  190.3 32.5 %collective-permute-start.56 = (f32[6912]{0:T(1024)S(1)}, f32[6912]{0:T(1024)S(1)}, u32[]{:S(2)}, u32[]{:S(2)}) collective-permute-start(f32[6912]{0:T(1024)S(1)} %add.317), channel_id=1, source_target_pairs={{0,8},{2,10},{4,12},{6,14},{8,0},{10,2},{12,4},{14,6},{1,9},{3,11}... | collective-permute-start | bytes 82952 | tf_op jit(solution)/shard_map/ppermute | solution.py:53
  193.5 8.9 %collective-permute-start.22 = (bf16[96,768]{1,0:T(8,128)(2,1)S(1)}, bf16[96,768]{1,0:T(8,128)(2,1)S(1)}, u32[]{:S(2)}, u32[]{:S(2)}) collective-permute-start(bf16[96,768]{1,0:T(8,128)(2,1)S(1)} %get-tuple-element.56), channel_id=1, source_target_pairs={{0,4},{4,8},{8,12},{12,14},{14,10},{10,6},{6,2},{2,0},{1,5},{5,9},... | collective-permute-start | bytes 442376 | tf_op jit(solution)/shard_map/ppermute | solution.py:36
  194.5 6.7 %collective-permute-start.26 = (bf16[96,768]{1,0:T(8,128)(2,1)S(1)}, bf16[96,768]{1,0:T(8,128)(2,1)S(1)}, u32[]{:S(2)}, u32[]{:S(2)}) collective-permute-start(bf16[96,768]{1,0:T(8,128)(2,1)S(1)} %get-tuple-element.57), channel_id=1, source_target_pairs={{0,2},{4,0},{8,4},{12,8},{14,12},{10,14},{6,10},{2,6},{1,3},{5,1},... | collective-permute-start | bytes 442376 | tf_op jit(solution)/shard_map/ppermute | solution.py:36
  195.6 31.6 %copy-start.6 = (bf16[192,3072]{1,0:T(8,128)(2,1)}, bf16[192,3072]{1,0:T(8,128)(2,1)S(1)}, u32[]{:S(2)}) copy-start(bf16[192,3072]{1,0:T(8,128)(2,1)S(1)} %collective-permute-done.44) | copy-start | bytes 3538948
  196.0 7.5 %collective-permute-start.45 = (bf16[96,768]{1,0:T(8,128)(2,1)S(1)}, bf16[96,768]{1,0:T(8,128)(2,1)S(1)}, u32[]{:S(2)}, u32[]{:S(2)}) collective-permute-start(bf16[96,768]{1,0:T(8,128)(2,1)S(1)} %get-tuple-element.54), channel_id=1, source_target_pairs={{0,4},{4,8},{8,12},{12,14},{14,10},{10,6},{6,2},{2,0},{1,5},{5,9},... | collective-permute-start | bytes 442376 | tf_op jit(solution)/shard_map/ppermute | solution.py:36
  197.1 7.4 %collective-permute-start.49 = (bf16[96,768]{1,0:T(8,128)(2,1)S(1)}, bf16[96,768]{1,0:T(8,128)(2,1)S(1)}, u32[]{:S(2)}, u32[]{:S(2)}) collective-permute-start(bf16[96,768]{1,0:T(8,128)(2,1)S(1)} %get-tuple-element.55), channel_id=1, source_target_pairs={{0,2},{4,0},{8,4},{12,8},{14,12},{10,14},{6,10},{2,6},{1,3},{5,1},... | collective-permute-start | bytes 442376 | tf_op jit(solution)/shard_map/ppermute | solution.py:36
  201.3 21.5 %collective-permute-start.27 = (bf16[192,768]{1,0:T(8,128)(2,1)S(1)}, bf16[192,768]{1,0:T(8,128)(2,1)S(1)}, u32[]{:S(2)}, u32[]{:S(2)}) collective-permute-start(bf16[192,768]{1,0:T(8,128)(2,1)S(1)} %pad_maximum_fusion.5), channel_id=1, source_target_pairs={{0,2},{4,0},{8,4},{12,8},{14,12},{10,14},{6,10},{2,6},{1,3},{5,1},... | collective-permute-start | bytes 884744 | tf_op jit(solution)/shard_map/ppermute | solution.py:36
  202.5 10.0 %collective-permute-start.23 = (bf16[192,768]{1,0:T(8,128)(2,1)S(1)}, bf16[192,768]{1,0:T(8,128)(2,1)S(1)}, u32[]{:S(2)}, u32[]{:S(2)}) collective-permute-start(bf16[192,768]{1,0:T(8,128)(2,1)S(1)} %pad_maximum_fusion.4), channel_id=1, source_target_pairs={{0,4},{4,8},{8,12},{12,14},{14,10},{10,6},{6,2},{2,0},{1,5},{5,9},... | collective-permute-start | bytes 884744 | tf_op jit(solution)/shard_map/ppermute | solution.py:36
  203.6 15.2 %collective-permute-start.46 = (bf16[192,768]{1,0:T(8,128)(2,1)S(1)}, bf16[192,768]{1,0:T(8,128)(2,1)S(1)}, u32[]{:S(2)}, u32[]{:S(2)}) collective-permute-start(bf16[192,768]{1,0:T(8,128)(2,1)S(1)} %pad_maximum_fusion.6), channel_id=1, source_target_pairs={{0,4},{4,8},{8,12},{12,14},{14,10},{10,6},{6,2},{2,0},{1,5},{5,9},... | collective-permute-start | bytes 884744 | tf_op jit(solution)/shard_map/ppermute | solution.py:36
  204.5 22.6 %collective-permute-start.50 = (bf16[192,768]{1,0:T(8,128)(2,1)S(1)}, bf16[192,768]{1,0:T(8,128)(2,1)S(1)}, u32[]{:S(2)}, u32[]{:S(2)}) collective-permute-start(bf16[192,768]{1,0:T(8,128)(2,1)S(1)} %pad_maximum_fusion.7), channel_id=1, source_target_pairs={{0,2},{4,0},{8,4},{12,8},{14,12},{10,14},{6,10},{2,6},{1,3},{5,1},... | collective-permute-start | bytes 884744 | tf_op jit(solution)/shard_map/ppermute | solution.py:36
  213.6 10.4 %collective-permute-start.24 = (bf16[192,768]{1,0:T(8,128)(2,1)S(1)}, bf16[192,768]{1,0:T(8,128)(2,1)S(1)}, u32[]{:S(2)}, u32[]{:S(2)}) collective-permute-start(bf16[192,768]{1,0:T(8,128)(2,1)S(1)} %add_convert_fusion.7), channel_id=1, source_target_pairs={{0,4},{4,8},{8,12},{12,14},{14,10},{10,6},{6,2},{2,0},{1,5},{5,9},... | collective-permute-start | bytes 884744 | tf_op jit(solution)/shard_map/ppermute | solution.py:36
  218.9 8.2 %collective-permute-start.47 = (bf16[192,768]{1,0:T(8,128)(2,1)S(1)}, bf16[192,768]{1,0:T(8,128)(2,1)S(1)}, u32[]{:S(2)}, u32[]{:S(2)}) collective-permute-start(bf16[192,768]{1,0:T(8,128)(2,1)S(1)} %add_convert_fusion.3), channel_id=1, source_target_pairs={{0,4},{4,8},{8,12},{12,14},{14,10},{10,6},{6,2},{2,0},{1,5},{5,9},... | collective-permute-start | bytes 884744 | tf_op jit(solution)/shard_map/ppermute | solution.py:36
  226.0 23.2 %copy-start.1 = (bf16[192,768]{1,0:T(8,128)(2,1)S(1)}, bf16[192,768]{1,0:T(8,128)(2,1)}, u32[]{:S(2)}) copy-start(bf16[192,768]{1,0:T(8,128)(2,1)} %param.6) | copy-start | bytes 884740
  226.0 23.2 %copy-start.11 = (bf16[192,768]{1,0:T(8,128)(2,1)S(1)}, bf16[192,768]{1,0:T(8,128)(2,1)}, u32[]{:S(2)}) copy-start(bf16[192,768]{1,0:T(8,128)(2,1)} %param.7) | copy-start | bytes 884740
  226.0 8.9 %collective-permute-start.28 = (bf16[192,768]{1,0:T(8,128)(2,1)}, bf16[192,768]{1,0:T(8,128)(2,1)}, u32[]{:S(2)}, u32[]{:S(2)}) collective-permute-start(bf16[192,768]{1,0:T(8,128)(2,1)} %get-tuple-element.26), channel_id=1, source_target_pairs={{0,2},{4,0},{8,4},{12,8},{14,12},{10,14},{6,10},{2,6},{1,3},{5,1},... | collective-permute-start | bytes 884744 | tf_op jit(solution)/shard_map/ppermute | solution.py:36
  228.2 13.1 %collective-permute-start.51 = (bf16[192,768]{1,0:T(8,128)(2,1)}, bf16[192,768]{1,0:T(8,128)(2,1)}, u32[]{:S(2)}, u32[]{:S(2)}) collective-permute-start(bf16[192,768]{1,0:T(8,128)(2,1)} %get-tuple-element.19), channel_id=1, source_target_pairs={{0,2},{4,0},{8,4},{12,8},{14,12},{10,14},{6,10},{2,6},{1,3},{5,1},... | collective-permute-start | bytes 884744 | tf_op jit(solution)/shard_map/ppermute | solution.py:36
  230.8 12.9 %collective-permute-start.25 = (bf16[192,768]{1,0:T(8,128)(2,1)S(1)}, bf16[192,768]{1,0:T(8,128)(2,1)S(1)}, u32[]{:S(2)}, u32[]{:S(2)}) collective-permute-start(bf16[192,768]{1,0:T(8,128)(2,1)S(1)} %get-tuple-element.25), channel_id=1, source_target_pairs={{0,4},{4,8},{8,12},{12,14},{14,10},{10,6},{6,2},{2,0},{1,5},{5,9},... | collective-permute-start | bytes 884744 | tf_op jit(solution)/shard_map/ppermute | solution.py:36
  231.5 12.2 %collective-permute-start.48 = (bf16[192,768]{1,0:T(8,128)(2,1)S(1)}, bf16[192,768]{1,0:T(8,128)(2,1)S(1)}, u32[]{:S(2)}, u32[]{:S(2)}) collective-permute-start(bf16[192,768]{1,0:T(8,128)(2,1)S(1)} %get-tuple-element.18), channel_id=1, source_target_pairs={{0,4},{4,8},{8,12},{12,14},{14,10},{10,6},{6,2},{2,0},{1,5},{5,9},... | collective-permute-start | bytes 884744 | tf_op jit(solution)/shard_map/ppermute | solution.py:36
  236.2 9.6 %collective-permute-start.29 = (bf16[192,768]{1,0:T(8,128)(2,1)S(1)}, bf16[192,768]{1,0:T(8,128)(2,1)S(1)}, u32[]{:S(2)}, u32[]{:S(2)}) collective-permute-start(bf16[192,768]{1,0:T(8,128)(2,1)S(1)} %add_convert_fusion.4), channel_id=1, source_target_pairs={{0,2},{4,0},{8,4},{12,8},{14,12},{10,14},{6,10},{2,6},{1,3},{5,1},... | collective-permute-start | bytes 884744 | tf_op jit(solution)/shard_map/ppermute | solution.py:36
  242.5 6.8 %collective-permute-start.52 = (bf16[192,768]{1,0:T(8,128)(2,1)S(1)}, bf16[192,768]{1,0:T(8,128)(2,1)S(1)}, u32[]{:S(2)}, u32[]{:S(2)}) collective-permute-start(bf16[192,768]{1,0:T(8,128)(2,1)S(1)} %add_convert_fusion), channel_id=1, source_target_pairs={{0,2},{4,0},{8,4},{12,8},{14,12},{10,14},{6,10},{2,6},{1,3},{5,1},... | collective-permute-start | bytes 884744 | tf_op jit(solution)/shard_map/ppermute | solution.py:36
  (9 other events, 54.0 us)

commit v2 on v1

--- a/solution.py
+++ b/solution.py
@@ -1,6 +1,8 @@
 import jax
 import jax.numpy as jnp
 from jax import lax
+from jax.experimental import pallas as pl
+from jax.experimental.pallas import tpu as pltpu
 from jax.sharding import PartitionSpec as P
 
 norm_eps = 1e-06
@@ -100,7 +102,445 @@
     return jnp.concatenate([x[half:], x[:half]], axis=0)
 
 
-def local(tokens, cotangent, up_weight, up_bias, down_weight, norm_gain):
+FAR = pl.BlockSpec(memory_space=pltpu.HBM)
+MARK = jax.ShapeDtypeStruct((8, 128), f32)
+
+
+def params(mib):
+    return pltpu.CompilerParams(vmem_limit_bytes=mib * 2**20)
+
+
+def cost(*_):
+    return pl.CostEstimate(flops=1024, bytes_accessed=1024, transcendentals=0)
+
+
+def whole(a):
+    return pl.BlockSpec(a.shape, lambda i, *_: (0,) * a.ndim)
+
+
+def mark_spec():
+    return pl.BlockSpec(MARK.shape, lambda *_: (0, 0))
+
+
+def columns(at, width):
+    return pl.ds(pl.multiple_of(at * width, 128), width)
+
+
+def held(x):
+    return pltpu.with_memory_space_constraint(x, pltpu.HBM)
+
+
+def tie(arrays, after):
+    count = len(arrays)
+
+    def body(*refs):
+        del refs
+
+    return pl.pallas_call(
+        body,
+        out_shape=[jax.ShapeDtypeStruct(a.shape, a.dtype) for a in arrays],
+        in_specs=[FAR] * (count + len(after)),
+        out_specs=[FAR] * count,
+        input_output_aliases={i: i for i in range(count)},
+        compiler_params=params(1),
+        cost_estimate=cost(),
+    )(*arrays, *after)
+
+
+def shard_stats(blocks, earlier=None):
+    rows, width = blocks[0].shape
+    count = len(blocks)
+    last = earlier is not None
+    known = list(earlier) if last else []
+    total = count + len(known)
+
+    def body(*refs):
+        stats = []
+        for k in range(count):
+            block = refs[k][...].astype(f32)
+            mean = jnp.sum(block, axis=1, keepdims=True) * (1.0 / width)
+            away = block - mean
+            spread = jnp.sum(away * away, axis=1, keepdims=True)
+            stats.append((mean, spread))
+        if not last:
+            for k in range(count):
+                refs[count + k][...] = jnp.concatenate(stats[k], axis=1)
+            return
+        stats += [(r[:, :1], r[:, 1:]) for r in refs[count:-1]]
+        mean = sum(m for m, _ in stats) * (1.0 / total)
+        spread = sum(v for _, v in stats) + width * sum((m - mean) ** 2 for m, _ in stats)
+        refs[-1][...] = jnp.concatenate([mean, lax.rsqrt(spread * (1.0 / (total * width)) + norm_eps)], axis=1)
+
+    outputs = 1 if last else count
+    return pl.pallas_call(
+        body,
+        grid=(1,),
+        in_specs=[whole(x) for x in list(blocks) + known],
+        out_specs=[pl.BlockSpec((rows, 2), lambda i: (0, 0))] * outputs,
+        out_shape=[jax.ShapeDtypeStruct((rows, 2), f32)] * outputs,
+        compiler_params=params(12),
+        cost_estimate=cost(),
+    )(*blocks, *known)
+
+
+def assemble(blocks, came, near, slots, norm=None, after=()):
+    n = len(blocks)
+    pairs = len(came)
+    own, width = came[0].shape
+    operands = [held(x) for x in [*blocks, *came]] + (list(norm) if norm else [])
+
+    def body(near_ref, slot_ref, *refs):
+        out_ref, mark_ref = refs[-2:]
+        mark_ref[...] = jnp.zeros(MARK.shape, f32)
+        if norm:
+            here, there, gain = refs[n + pairs : n + pairs + 3]
+        for j in range(pairs):
+            flag = jnp.full((own, width), near_ref[j], jnp.int32) == 1
+            kept = jnp.where(flag, refs[j][...].astype(f32), refs[j + pairs][...].astype(f32))
+            at = columns(slot_ref[j], width)
+            got = refs[n + j][...].astype(f32)
+            if norm:
+                scale = gain[:, at]
+                kept = (kept - here[:, :1]) * here[:, 1:] * scale
+                got = (got - there[:, :1]) * there[:, 1:] * scale
+            out_ref[:own, at] = kept.astype(bf16)
+            out_ref[own:, at] = got.astype(bf16)
+
+    return pl.pallas_call(
+        body,
+        grid_spec=pltpu.PrefetchScalarGridSpec(
+            num_scalar_prefetch=2,
+            grid=(1,),
+            in_specs=[whole(x) for x in operands] + [FAR] * len(after),
+            out_specs=[pl.BlockSpec((2 * own, pairs * width), lambda i, *_: (0, 0)), mark_spec()],
+        ),
+        out_shape=[jax.ShapeDtypeStruct((2 * own, pairs * width), bf16), MARK],
+        compiler_params=params(24),
+        cost_estimate=cost(),
+    )(near, slots, *operands, *after)
+
+
+def side_product(left, weight, side, by_rows, turn, after=()):
+    rows, depth = left.shape
+    width = (weight.shape[0] if by_rows else weight.shape[1]) // 2
+    block = 512
+    steps = width // block
+    half = rows // 2
+
+    def body(side_ref, left_ref, weight_ref, *rest):
+        part = contract(left_ref[...], weight_ref[...], 1, 1 if by_rows else 0)
+        if turn:
+            rest[-2][:half] = part[half:]
+            rest[-2][half:] = part[:half]
+        else:
+            rest[-2][...] = part
+        rest[-1][...] = jnp.zeros(MARK.shape, f32)
+
+    if by_rows:
+        weight_spec = pl.BlockSpec((block, depth), lambda i, s: (s[0] * steps + i, 0))
+    else:
+        weight_spec = pl.BlockSpec((depth, block), lambda i, s: (0, s[0] * steps + i))
+    return pl.pallas_call(
+        body,
+        grid_spec=pltpu.PrefetchScalarGridSpec(
+            num_scalar_prefetch=1,
+            grid=(steps,),
+            in_specs=[whole(left), weight_spec] + [FAR] * len(after),
+            out_specs=[pl.BlockSpec((rows, block), lambda i, s: (0, i)), mark_spec()],
+        ),
+        out_shape=[jax.ShapeDtypeStruct((rows, width), f32), MARK],
+        compiler_params=params(24),
+        cost_estimate=cost(rows, depth, width),
+    )(side.reshape(1), left, held(weight), *after)
+
+
+def gelu_half(kept, came, bias, core, after=()):
+    rows, width = kept.shape
+    block = 512
+    steps = width // block
+    half = rows // 2
+
+    def body(core_ref, kept_ref, came_ref, bias_ref, *rest):
+        value_ref, turned_ref, slope_ref = rest[-3:]
+        value, slope = gelu_parts(kept_ref[...] + came_ref[...] + bias_ref[...])
+        value = value.astype(bf16)
+        value_ref[...] = value
+        turned_ref[:half] = value[half:]
+        turned_ref[half:] = value[:half]
+        slope_ref[...] = slope
+
+    spec = pl.BlockSpec((rows, block), lambda i, s: (0, i))
+    return pl.pallas_call(
+        body,
+        grid_spec=pltpu.PrefetchScalarGridSpec(
+            num_scalar_prefetch=1,
+            grid=(steps,),
+            in_specs=[spec, spec, pl.BlockSpec((1, block), lambda i, s: (0, s[0] * steps + i))] + [FAR] * len(after),
+            out_specs=[spec] * 3,
+        ),
+        out_shape=[jax.ShapeDtypeStruct((rows, width), t) for t in (bf16, bf16, f32)],
+        compiler_params=params(24),
+        cost_estimate=cost(),
+    )(core.reshape(1), kept, came, bias, *after)
+
+
+def slope_half(kept, came, slope, after=()):
+    rows, width = kept.shape
+    block = 512
+    half = rows // 2
+
+    def body(kept_ref, came_ref, slope_ref, *rest):
+        value_ref, turned_ref, mark_ref = rest[-3:]
+        mark_ref[...] = jnp.zeros(MARK.shape, f32)
+        value = ((kept_ref[...] + came_ref[...]) * slope_ref[...]).astype(bf16)
+        value_ref[...] = value
+        turned_ref[:half] = value[half:]
+        turned_ref[half:] = value[:half]
+
+    spec = pl.BlockSpec((rows, block), lambda i: (0, i))
+    return pl.pallas_call(
+        body,
+        grid=(width // block,),
+        in_specs=[spec] * 3 + [FAR] * len(after),
+        out_specs=[spec] * 2 + [mark_spec()],
+        out_shape=[jax.ShapeDtypeStruct((rows, width), bf16)] * 2 + [MARK],
+        compiler_params=params(24),
+        cost_estimate=cost(),
+    )(kept, came, slope, *after)
+
+
+def branch_pairs(own, came, weight, where, first, shard_width, after=()):
+    rows, depth = own.shape
+    half = rows // 2
+
+    def body(where_ref, own_ref, came_ref, weight_own, weight_came, *rest):
+        out = contract(own_ref[...], weight_own[...], 1, 0) + contract(came_ref[...], weight_came[...], 1, 0)
+        out = out.astype(bf16)
+        rest[-3][0] = out[:half]
+        rest[-2][0] = out[half:]
+        rest[-1][...] = jnp.zeros(MARK.shape, f32)
+
+    out_spec = pl.BlockSpec((1, half, shard_width), lambda i, s: (i, 0, 0))
+    return pl.pallas_call(
+        body,
+        grid_spec=pltpu.PrefetchScalarGridSpec(
+            num_scalar_prefetch=1,
+            grid=(2,),
+            in_specs=[
+                whole(own),
+                whole(came),
+                pl.BlockSpec((depth, shard_width), lambda i, s: (s[4], s[first + i])),
+                pl.BlockSpec((depth, shard_width), lambda i, s: (s[5], s[first + i])),
+            ]
+            + [FAR] * len(after),
+            out_specs=[out_spec] * 2 + [mark_spec()],
+        ),
+        out_shape=[jax.ShapeDtypeStruct((2, half, shard_width), bf16)] * 2 + [MARK],
+        compiler_params=params(24),
+        cost_estimate=cost(rows, 2 * depth, 2 * shard_width),
+    )(where, own, came, held(weight), held(weight), *after)
+
+
+def normed_pairs(own, came, weight, gain, normed, where, first, shard_width, small, after=()):
+    rows, depth = own.shape
+    half = rows // 2
+    opening = small is None
+    extra = [] if opening else [small]
+    n = 8
+
+    def body(where_ref, own_ref, came_ref, weight_own, weight_came, gain_ref, normed_ref, *rest):
+        keep_ref, give_ref, small_ref, first_ref, second_ref = rest[-5:]
+        step = pl.program_id(0)
+        grad = contract(own_ref[...], weight_own[...], 1, 1) + contract(came_ref[...], weight_came[...], 1, 1)
+        rounded = grad.astype(bf16)
+        keep_ref[0] = rounded[:half]
+        give_ref[0] = rounded[half:]
+        product = grad * normed_ref[...].astype(f32)
+
+        @pl.when(step == 0)
+        def _():
+            small_ref[...] = jnp.zeros(small_ref.shape, f32) if opening else rest[0][...]
+            first_ref[...] = jnp.zeros(first_ref.shape, f32)
+            second_ref[...] = jnp.zeros(second_ref.shape, f32)
+
+        small_ref[pl.ds(where_ref[6 + first + step], 1), :] = jnp.sum(product, axis=0, keepdims=True)
+        scaled = grad * gain_ref[...]
+        lanes = range(0, shard_width, 128)
+        first_ref[...] += sum(scaled[:, k : k + 128] for k in lanes)
+        second_ref[...] += sum(product[:, k : k + 128] for k in lanes)
+
+        @pl.when(step == 1)
+        def _():
+            for at, ref in ((0, first_ref), (256, second_ref)):
+                by_token = jnp.sum(ref[...].T, axis=0, keepdims=True)
+                small_ref[pl.ds(n + where_ref[4], 1), at : at + half] += by_token[:, :half]
+                small_ref[pl.ds(n + where_ref[5], 1), at : at + half] += by_token[:, half:]
+
+    out_spec = pl.BlockSpec((1, half, shard_width), lambda i, s: (i, 0, 0))
+    small_spec = pl.BlockSpec((2 * n, shard_width), lambda i, s: (0, 0))
+    return pl.pallas_call(
+        body,
+        grid_spec=pltpu.PrefetchScalarGridSpec(
+            num_scalar_prefetch=1,
+            grid=(2,),
+            in_specs=[
+                whole(own),
+                whole(came),
+                pl.BlockSpec((shard_width, depth), lambda i, s: (s[first + i], s[4])),
+                pl.BlockSpec((shard_width, depth), lambda i, s: (s[first + i], s[5])),
+                pl.BlockSpec((1, shard_width), lambda i, s: (0, s[first + i])),
+                pl.BlockSpec((rows, shard_width), lambda i, s: (0, s[first + i])),
+            ]
+            + [small_spec] * len(extra)
+            + [FAR] * len(after),
+            out_specs=[out_spec, out_spec, small_spec],
+            scratch_shapes=[pltpu.VMEM((rows, 128), f32)] * 2,
+        ),
+        out_shape=[
+            jax.ShapeDtypeStruct((2, half, shard_width), bf16),
+            jax.ShapeDtypeStruct((2, half, shard_width), bf16),
+            jax.ShapeDtypeStruct((2 * n, shard_width), f32),
+        ],
+        compiler_params=params(24),
+        cost_estimate=cost(),
+    )(where, own, came, held(weight), held(weight), gain, normed, *extra, *after)
+
+
+def out_grad(left, right, side, part, into, after=()):
+    tokens, height = left.shape
+    width = right.shape[1]
+    block = height // 4
+    extra = [] if into is None else [into]
+
+    def body(side_ref, left_ref, right_ref, *rest):
+        rest[-2][...] = contract(left_ref[...], right_ref[...], 0, 0).astype(bf16)
+        rest[-1][...] = jnp.zeros(MARK.shape, f32)
+
+    return pl.pallas_call(
+        body,
+        grid_spec=pltpu.PrefetchScalarGridSpec(
+            num_scalar_prefetch=1,
+            grid=(2,),
+            in_specs=[pl.BlockSpec((tokens, block), lambda i, s: (0, 2 * part + i)), whole(right)]
+            + [FAR] * (len(extra) + len(after)),
+            out_specs=[pl.BlockSpec((block, width), lambda i, s: (4 * s[0] + 2 * part + i, 0)), mark_spec()],
+        ),
+        out_shape=[pltpu.HBM((2 * height, width), bf16), MARK],
+        input_output_aliases={} if into is None else {3: 0},
+        compiler_params=params(24),
+        cost_estimate=cost(height // 2, tokens, width),
+    )(side.reshape(1), left, right, *extra, *after)
+
+
+def in_grad(left, own, came, core, quarter, into, after=()):
+    tokens, height = left.shape
+    width = own.shape[1]
+    block = height // 8
+    extra = [] if into is None else [into]
+
+    def body(core_ref, left_ref, own_ref, came_ref, *rest):
+        outs = rest[len(extra) + len(after) :]
+        at_own, at_came = columns(core_ref[0], width), columns(1 - core_ref[0], width)
+        outs[0][:, at_own] = contract(left_ref[...], own_ref[...], 0, 0).astype(bf16)
+        outs[0][:, at_came] = contract(left_ref[...], came_ref[...], 0, 0).astype(bf16)
+        outs[1][...] = jnp.zeros(MARK.shape, f32)
+        if into is None:
+
+            @pl.when(pl.program_id(0) == 0)
+            def _():
+                outs[2][:, at_own] = jnp.sum(own_ref[...].astype(f32), axis=0, keepdims=True)
+                outs[2][:, at_came] = jnp.sum(came_ref[...].astype(f32), axis=0, keepdims=True)
+
+    out_shape = [pltpu.HBM((height, 2 * width), bf16), MARK]
+    out_specs = [pl.BlockSpec((block, 2 * width), lambda i, s: (2 * quarter + i, 0)), mark_spec()]
+    if into is None:
+        out_shape.append(jax.ShapeDtypeStruct((1, 2 * width), f32))
+        out_specs.append(pl.BlockSpec((1, 2 * width), lambda i, s: (0, 0)))
+    return pl.pallas_call(
+        body,
+        grid_spec=pltpu.PrefetchScalarGridSpec(
+            num_scalar_prefetch=1,
+            grid=(2,),
+            in_specs=[pl.BlockSpec((tokens, block), lambda i, s: (0, 2 * quarter + i)), whole(own), whole(came)]
+            + [FAR] * (len(extra) + len(after)),
+            out_specs=out_specs,
+        ),
+        out_shape=out_shape,
+        input_output_aliases={} if into is None else {4: 0},
+        compiler_params=params(24),
+        cost_estimate=cost(height // 4, tokens, 2 * width),
+    )(core.reshape(1), left, own, came, *extra, *after)
+
+
+class Sum:
+    def __init__(self, ring, near, kept, came, far):
+        self.ring, self.near, self.kept, self.came, self.far = ring, near, kept, came, far
+
+    def block(self, near_ref, offset, kept_ref, came_ref):
+        sel = near_ref[offset % 4]
+        sel = sel if offset < 4 else 1 - sel
+        flag = jnp.full(kept_ref.shape[1:], sel, jnp.int32) == 1
+        return jnp.where(flag, kept_ref[0].astype(f32), came_ref[0].astype(f32))
+
+    def partial(self, offsets, got, small, after):
+        own, width = self.came[0].shape[1:]
+        operands, specs = [], []
+        for offset, taken in zip(offsets, got):
+            pair = offset % 4
+            here = [self.kept[pair // 2], self.came[pair // 2]]
+            operands += here
+            specs += [pl.BlockSpec((1, own, width), lambda i, s, at=pair % 2: (at, 0, 0))] * 2
+            if taken is not None:
+                operands.append(taken)
+                specs.append(whole(taken))
+        out_shape = [jax.ShapeDtypeStruct((own, width), bf16) for _ in offsets]
+        if small is not None:
+            operands += list(small)
+            specs += [whole(t) for t in small]
+            out_shape.append(jax.ShapeDtypeStruct(small[0].shape, f32))
+        out_specs = [whole(o) for o in out_shape] + [mark_spec()]
+        out_shape.append(MARK)
+
+        def body(near_ref, *refs):
+            refs = list(refs)
+            outs = refs[len(operands) + len(after) :]
+            for k, (offset, taken) in enumerate(zip(offsets, got)):
+                total = self.block(near_ref, offset, refs.pop(0), refs.pop(0))
+                if taken is not None:
+                    total = total + refs.pop(0)[...].astype(f32)
+                outs[k][...] = total.astype(bf16)
+            if small is not None:
+                outs[-2][...] = refs[0][...] + refs[1][...]
+            outs[-1][...] = jnp.zeros(MARK.shape, f32)
+
+        return pl.pallas_call(
+            body,
+            grid_spec=pltpu.PrefetchScalarGridSpec(
+                num_scalar_prefetch=1,
+                grid=(1,),
+                in_specs=specs + [FAR] * len(after),
+                out_specs=out_specs,
+            ),
+            out_shape=out_shape,
+            compiler_params=params(16),
+            cost_estimate=cost(),
+        )(self.near, *operands, *after)
+
+    def hop(self, k, got, small=None, after=()):
+        ways = [self.far] if k == 1 else [0, 1]
+        offsets = [(4, 3, 2, 1)[k - 1] if way == 0 else (4, 5, 6, 7)[k - 1] for way in ways]
+        outs = self.partial(offsets, [got[way] for way in ways], small, after)
+        got = [None, None]
+        for way, part in zip(ways, outs):
+            got[way] = self.ring.shift(part, 1 if way == 0 else -1)
+        return got, outs[len(ways)] if small is not None else None, outs[-1]
+
+    def last(self, near0, got):
+        block = jnp.where(near0, self.kept[0][0], self.came[0][0])
+        return block.astype(f32) + got[0].astype(f32) + got[1].astype(f32)
+
+
+def wide(tokens, cotangent, up_weight, up_bias, down_weight, norm_gain):
     tok_count, shard_width = tokens.shape
     n = lax.axis_size("row")
     model_width = n * shard_width
@@ -205,6 +645,129 @@
     return (block_out, grad_x, grad_in, grad_out, grad_bias, grad_gain)
 
 
+def local(tokens, cotangent, up_weight, up_bias, down_weight, norm_gain):
+    tok_count, shard_width = tokens.shape
+    n = lax.axis_size("row")
+    if n != ring_limit:
+        return wide(tokens, cotangent, up_weight, up_bias, down_weight, norm_gain)
+    model_width = n * shard_width
+    half_width = model_width // 2
+    core = lax.axis_index("col")
+    row = lax.axis_index("row")
+    other = 1 - core
+    ring = Ring(n)
+    pairs = n // 2
+    mid = tok_count // 2
+
+    rows_near = [ring.row_at(j) for j in range(pairs)]
+    rows_far = [ring.row_at(j + pairs) for j in range(pairs)]
+    near = [(r // pairs) == core for r in rows_near]
+    rows_here = [jnp.where(s, a, b) for s, a, b in zip(near, rows_near, rows_far)]
+    near_flags = jnp.stack([s.astype(jnp.int32) for s in near])
+    where = jnp.stack([r - core * pairs for r in rows_here] + [core, other] + rows_here).astype(jnp.int32)
+    gain_local = lax.dynamic_slice_in_dim(norm_gain, row * shard_width, shard_width, 0)
+    gain_half = lax.dynamic_slice_in_dim(norm_gain, core * half_width, half_width, 0)[None]
+
+    def hop(up, down):
+        return ring.shift(up, -1), ring.shift(down, 1)
+
+    def crossed(blocks):
+        return [swap(jnp.where(near[j], blocks[j + pairs], blocks[j])) for j in range(pairs)]
+
+    t1 = hop(tokens, tokens)
+    s0 = shard_stats([tokens])
+    t1 = tie(t1, s0)
+    t2 = hop(*t1)
+    up_near, down_near = up_weight, down_weight
+    s1 = shard_stats(t1)
+    t2 = tie(t2, s1)
+    t3 = hop(*t2)
+    s2 = shard_stats(t2)
+    t3 = tie(t3, s2)
+    t4 = ring.shift(t3[0], -1)
+    late = tie([cotangent], [t3[0]])[0]
+    c1 = hop(late, late)
+    s3 = shard_stats(t3)
+    norms = shard_stats([t4], s0 + s1 + s2 + s3)[0]
+    t_blocks = [tokens, t1[0], t2[0], t3[0], t4, t3[1], t2[1], t1[1]]
+    normed_cols, mark = assemble(t_blocks, crossed(t_blocks), near_flags, where, (norms, swap(norms), gain_half))
+
+    c1 = tie(c1, [mark])
+    c2 = hop(*c1)
+    hidden_give, mark = side_product(normed_cols, up_near, other, False, True, after=[c1[0]])
+    c2 = tie(c2, [mark])
+    c3 = hop(*c2)
+    hidden_came = swap(tie([hidden_give], [c2[0]])[0])
+    hidden_keep, mark = side_product(normed_cols, up_near, core, False, False, after=[c2[0]])
+    c3 = tie(c3, [mark])
+    c4 = ring.shift(c3[1], 1)
+    act_own, act_turned, slope = gelu_half(hidden_keep, hidden_came, up_bias[None], core, after=[c3[0]])
+    act_came = swap(act_turned)
+    b1, b1_give, mark = branch_pairs(act_own, act_came, down_near, where, 0, shard_width)
+    c4 = tie([c4], [mark])[0]
+    c_blocks = [cotangent, c1[0], c2[0], c3[0], c4, c3[1], c2[1], c1[1]]
+    cot_cols, _ = assemble(c_blocks, crossed(c_blocks), near_flags, where, after=[mark])
+
+    branch = Sum(ring, near_flags, [b1, None], [swap(b1_give), None], 0)
+    got, _, mark = branch.hop(1, [None, None], after=[mark])
+    b2, b2_give, mark = branch_pairs(act_own, act_came, down_near, where, 2, shard_width, after=[mark])
+    branch.kept[1], branch.came[1] = b2, swap(b2_give)
+    grad_give, mark = side_product(cot_cols, down_near, other, True, True, after=[mark])
+    got, _, mark = branch.hop(2, got, after=[mark])
+    grad_came = swap(tie([grad_give], [mark])[0])
+    grad_keep, mark = side_product(cot_cols, down_near, core, True, False, after=[mark])
+    got, _, mark = branch.hop(3, got, after=[mark])
+    hid_own, hid_turned, mark = slope_half(grad_keep, grad_came, slope, after=[mark])
+    hid_came = swap(hid_turned)
+    grad_out, mark = out_grad(act_own, cot_cols, core, 0, None, after=[mark])
+
+    n1, n1_give, small = normed_pairs(
+        hid_own, hid_came, up_near, gain_half, normed_cols, where, 0, shard_width, None, after=[mark]
+    )
+    branch_got, _, mark = branch.hop(4, got, after=[small])
+    n1_give = tie([n1_give], [mark])[0]
+    grad_out, mark = out_grad(act_own, cot_cols, core, 1, grad_out, after=[mark])
+    norm = Sum(ring, near_flags, [n1, None], [swap(n1_give), None], 1)
+    got, _, mark = norm.hop(1, [None, None], after=[mark])
+    n2, n2_give, small = normed_pairs(
+        hid_own, hid_came, up_near, gain_half, normed_cols, where, 2, shard_width, small, after=[mark]
+    )
+    branch_got = tie(branch_got, [small])
+    n2_give, small = tie([n2_give, small], [branch_got[0], got[1]])
+    norm.kept[1], norm.came[1] = n2, swap(n2_give)
+    small_got = swap(small)
+    grad_out, mark = out_grad(act_came, cot_cols, other, 0, grad_out, after=[small])
+    block_out = (tokens.astype(f32) + branch.last(near[0], branch_got)).astype(bf16)
+
+    def toward(x, step):
+        return lax.ppermute(x, "row", [(i, i ^ step) for i in range(n)])
+
+    got, small, mark = norm.hop(2, got, (small, small_got), after=[mark])
+    small_got = toward(small, 1)
+    grad_out, mark = out_grad(act_came, cot_cols, other, 1, grad_out, after=[mark])
+    grad_in, mark, grad_bias = in_grad(normed_cols, hid_own, hid_came, core, 0, None, after=[mark])
+    got, small, mark = norm.hop(3, got, (small, small_got), after=[mark])
+    small_got = toward(small, 2)
+    grad_in, mark = in_grad(normed_cols, hid_own, hid_came, core, 1, grad_in, after=[mark])
+    grad_in, mark = in_grad(normed_cols, hid_own, hid_came, core, 2, grad_in, after=[mark])
+    got, small, mark = norm.hop(4, got, (small, small_got), after=[mark])
+    small_got = toward(small, 4)
+    grad_in, mark = in_grad(normed_cols, hid_own, hid_came, core, 3, grad_in, after=[mark])
+    got = tie(got, [mark])
+    small = small + small_got
+    token_mean, inverse_std = norms[:, :1], norms[:, 1:]
+    by_token = lax.dynamic_index_in_dim(small, n + core, 0, keepdims=False) / model_width
+    by_token = [by_token[:tok_count], by_token[256 : 256 + tok_count]]
+    grad_gain = lax.dynamic_index_in_dim(small, row, 0, keepdims=False) / gain_local
+    scaled = norm.last(near[0], got) * gain_local
+    whitened = (tokens.astype(f32) - token_mean) * inverse_std
+    grad_x = (
+        cotangent.astype(f32)
+        + inverse_std * (scaled - by_token[0][:, None] - whitened * by_token[1][:, None])
+    ).astype(bf16)
+    return (block_out, grad_x, grad_in, grad_out, grad_bias.reshape(-1), grad_gain)
+
+
 def solution(mesh):
     return jax.shard_map(
         local,

time: 252 us -> 197 us (0.78)
  Pallas kernels: 0 us -> 110 us
  matrix products: 89.1 us -> 0 us
  waiting for transfers between devices: 72.2 us -> 36.4 us
  other arithmetic: 26.8 us -> 5.21 us
  starting transfers between devices: 51.3 us -> 36.6 us
  local copies, waits for them, and re-layouts: 10.7 us -> 6.97 us
    pallas_call x0 -> x47, Pallas kernels: none -> 110 us  [the longest x4 26.8 us: side_product(): pl.pallas_call(body, grid_spec=pltpu.PrefetchScalarGridSpec(num_scalar_pr...]
    dot_general x6 -> x0, matrix products: 89.1 us -> none  [the longest x4 61.8 us: contract(): lax.dot_general(left, right, (((left_dim,), (right_dim,)), ((), ())), pre...]
    ppermute x32 -> x28, waiting for transfers between devices: 64.2 us -> 32.5 us  [shift(): lax.ppermute(x, 'row', [(order[i], order[(i + step) % n]) for i in range(...]
    ppermute x10 -> x3, starting transfers between devices: 17.6 us -> 2.33 us  [toward(): return lax.ppermute(x, 'row', [(i, i ^ step) for i in range(n)])]
    convert_element_type x12 -> x0, other arithmetic: 12.3 us -> none  [the longest x1 4.4 us: local(): hidden_grad = joined((act_grad * gelu_slope).astype(bf16))]
    slice x17 -> x2, local copies, waits for them, and re-layouts: 5.38 us -> 0.22 us  [the longest x1 0.21 us: local(): token_mean, inverse_std = (norms[:, :1], norms[:, 1:])]
    reduce_sum x5 -> x0, other arithmetic: 5.15 us -> none  [the longest x1 2.84 us: local(): grad_bias = jnp.sum(hidden_grad.astype(f32), axis=0)]
    ppermute x15 -> x18, waiting for transfers between devices: 8.02 us -> 3.89 us  [swap(): return lax.ppermute(x, 'col', [(0, 1), (1, 0)])]
  transfers between devices with their start and end apart: 57 -> 49, of which waited for: 26 -> 22; matrix products, arithmetic and copies ran while one was open for 40% -> 3% of each run, Pallas kernels for 0% -> 48%
where the time goes in v2:
time: 197 us; the launch traced here: 196 us
  Pallas kernels  110 us (56%)
  starting transfers between devices  36.6 us (19%)
  waiting for transfers between devices  36.4 us (18%)
  local copies, waits for them, and re-layouts  6.97 us (4%)
  other arithmetic  5.21 us (3%)
    ppermute x28, waiting for transfers between devices, shift(): lax.ppermute(x, 'row', [(order[i], order[(i + step) % n]) for i in range(...  32.5 us
    ppermute x28, starting transfers between devices, shift(): lax.ppermute(x, 'row', [(order[i], order[(i + step) % n]) for i in range(...  30.9 us
    pallas_call x4, Pallas kernels, side_product(): pl.pallas_call(body, grid_spec=pltpu.PrefetchScalarGridSpec(num_scalar_pr...  26.8 us
    pallas_call x4, Pallas kernels, in_grad(): pl.pallas_call(body, grid_spec=pltpu.PrefetchScalarGridSpec(num_scalar_pr...  17.7 us
    pallas_call x4, Pallas kernels, out_grad(): pl.pallas_call(body, grid_spec=pltpu.PrefetchScalarGridSpec(num_scalar_pr...  17.4 us
    pallas_call x2, Pallas kernels, normed_pairs(): pl.pallas_call(body, grid_spec=pltpu.PrefetchScalarGridSpec(num_scalar_pr...  15.5 us
    pallas_call x2, Pallas kernels, branch_pairs(): pl.pallas_call(body, grid_spec=pltpu.PrefetchScalarGridSpec(num_scalar_pr...  14 us
    pallas_call x8, Pallas kernels, partial(): pl.pallas_call(body, grid_spec=pltpu.PrefetchScalarGridSpec(num_scalar_pr...  7.5 us
  transfers between devices with their start and end apart: 49, of which 22 were waited for; matrix products, arithmetic and copies ran while one was open for 3% of the time, Pallas kernels for 48%

profile of v2, /device:TPU:0, one launch (start us, length us, event | category | flops | bytes accessed | tf_op | source)
XLA Modules:
  0.0 196.5 jit_solution(10490401560588673931)
XLA Ops:
  0.6 3.1 %collective-permute-start.1 = (bf16[192,768]{1,0:T(8,128)(2,1)}, bf16[192,768]{1,0:T(8,128)(2,1)S(1)}, u32[]{:S(2)}, u32[]{:S(2)}) collective-permute-start(bf16[192,768]{1,0:T(8,128)(2,1)} %refs_0_.5), channel_id=1, source_target_pairs={{0,4},{4,8},{8,12},{12,14},{14,10},{10,6},{6,2},{2,0},{1,5},{5,9},... | collective-permute-start | bytes 884744 | tf_op jit(solution)/shard_map/ppermute | solution.py:38
  3.7 1.0 copy-done.20
  5.0 5.9 %collective-permute-done.1.refs_1_ = bf16[192,768]{1,0:T(8,128)(2,1)S(1)} collective-permute-done((bf16[192,768]{1,0:T(8,128)(2,1)}, bf16[192,768]{1,0:T(8,128)(2,1)S(1)}, u32[]{:S(2)}, u32[]{:S(2)}) %collective-permute-start.1) | collective-permute-done | bytes 294944 | tf_op jit(solution)/shard_map/ppermute | solution.py:38
  10.8 1.5 collective-permute-done.refs_0_
  12.7 1.7 collective-permute-start.3
  14.8 5.2 %collective-permute-done.2.refs_0_ = bf16[192,768]{1,0:T(8,128)(2,1)S(1)} collective-permute-done((bf16[192,768]{1,0:T(8,128)(2,1)S(1)}, bf16[192,768]{1,0:T(8,128)(2,1)S(1)}, u32[]{:S(2)}, u32[]{:S(2)}) %collective-permute-start.2) | collective-permute-done | bytes 294944 | tf_op jit(solution)/shard_map/ppermute | solution.py:38
  20.3 1.5 collective-permute-start.4
  23.5 3.5 %collective-permute-done.4.refs_0_ = bf16[192,768]{1,0:T(8,128)(2,1)S(1)} collective-permute-done((bf16[192,768]{1,0:T(8,128)(2,1)S(1)}, bf16[192,768]{1,0:T(8,128)(2,1)S(1)}, u32[]{:S(2)}, u32[]{:S(2)}) %collective-permute-start.4) | collective-permute-done | bytes 294944 | tf_op jit(solution)/shard_map/ppermute | solution.py:38
  27.0 1.5 collective-permute-done.5.refs_1_
  28.6 1.6 collective-permute-start.6
  30.1 0.7 broadcast_select_fusion.1
  30.9 0.7 broadcast_select_fusion.5
  32.1 3.1 %collective-permute-done.6.refs_0_.refs_4_ = bf16[192,768]{1,0:T(8,128)(2,1)S(1)} collective-permute-done((bf16[192,768]{1,0:T(8,128)(2,1)S(1)}, bf16[192,768]{1,0:T(8,128)(2,1)S(1)}, u32[]{:S(2)}, u32[]{:S(2)}) %collective-permute-start.6) | collective-permute-done | bytes 294944 | tf_op jit(solution)/shard_map/ppermute | solution.py:38
  35.3 0.8 broadcast_select_fusion.7
  36.6 1.5 collective-permute-start.12
  41.2 0.9 copy-done.34
  42.1 3.5 %shard_map.117 = (bf16[384,3072]{1,0:T(8,128)(2,1)S(1)}, f32[8,128]{1,0:T(8,128)S(1)}) custom-call(s32[4]{0:T(128)S(1)} %add_convert_fusion.near_ref, s32[10]{0:T(128)S(1)} %stack.64.slot_ref.where_ref, bf16[192,768]{1,0:T(8,128)(2,1)} %refs_0_.5, bf16[192,768]{1,0:T(8,128)(2,1)} %copy-done.24, bf16[192,768]{1,0:T(8,128)(2,1)} %copy-done.18, ...), custom_call_target="tpu_custom_call" | custom-call | flops 1024 | bytes 1024 | tf_op jit(solution)/shard_map/pallas_call | solution.py:209
  46.0 1.4 collective-permute-start.15
  48.0 6.7 %shard_map.120 = (f32[384,1536]{1,0:T(8,128)S(1)}, f32[8,128]{1,0:T(8,128)S(1)}) custom-call(s32[1]{0:T(128)} %bitcast.5.side_ref, bf16[384,3072]{1,0:T(8,128)(2,1)S(1)} %get-tuple-element.113.left_ref.normed_ref, bf16[3072,3072]{1,0:T(8,128)(2,1)} %weight_came.7, bf16[192,768]{1,0:T(8,128)(2,1)S(1)} %get-tuple-element.115.rest_0_.refs_1_), custom_call_target="tpu_custom_call" | custom-call | flops 1024 | bytes 1024 | tf_op jit(solution)/shard_map/pallas_call | solution.py:243
  55.4 1.6 collective-permute-start.18
  57.5 6.6 %shard_map.122 = (f32[384,1536]{1,0:T(8,128)S(1)}, f32[8,128]{1,0:T(8,128)S(1)}) custom-call(s32[1]{0:T(128)} %bitcast.4.side_ref.core_ref, bf16[384,3072]{1,0:T(8,128)(2,1)S(1)} %get-tuple-element.113.left_ref.normed_ref, bf16[3072,3072]{1,0:T(8,128)(2,1)} %weight_came.7, bf16[192,768]{1,0:T(8,128)(2,1)S(1)} %get-tuple-element.118.rest_0_.refs_1_.refs_2_), custom_call_target="tpu_custom_call" | custom-call | flops 1024 | bytes 1024 | tf_op jit(solution)/shard_map/pallas_call | solution.py:243
  64.8 1.3 collective-permute-done.17.refs_0_
  66.2 1.8 shard_map.125
  68.1 2.8 %collective-permute-done.19.came_ref.left_ref = bf16[384,1536]{1,0:T(8,128)(2,1)S(1)} collective-permute-done((bf16[384,1536]{1,0:T(8,128)(2,1)S(1)}, bf16[384,1536]{1,0:T(8,128)(2,1)S(1)}, u32[]{:S(2)}, u32[]{:S(2)}) %collective-permute-start.19) | collective-permute-done | bytes 1179680 | tf_op jit(solution)/shard_map/ppermute | solution.py:97
  70.9 7.0 %shard_map.126 = (bf16[2,192,768]{2,1,0:T(8,128)(2,1)S(1)}, bf16[2,192,768]{2,1,0:T(8,128)(2,1)S(1)}, f32[8,128]{1,0:T(8,128)S(1)}) custom-call(s32[10]{0:T(128)S(1)} %stack.64.slot_ref.where_ref, bf16[384,1536]{1,0:T(8,128)(2,1)S(1)} %get-tuple-element.124.own_ref.left_ref, bf16[384,1536]{1,0:T(8,128)(2,1)S(1)} %collective-permute-done.19.came_ref.left_ref, ...), custom_call_target="tpu_custom_call" | custom-call | flops 1024 | bytes 1024 | tf_op jit(solution)/shard_map/pallas_call | solution.py:324
  78.6 1.6 collective-permute-start.23
  80.9 7.0 %shard_map.128 = (bf16[2,192,768]{2,1,0:T(8,128)(2,1)S(1)}, bf16[2,192,768]{2,1,0:T(8,128)(2,1)S(1)}, f32[8,128]{1,0:T(8,128)S(1)}) custom-call(s32[10]{0:T(128)S(1)} %stack.64.slot_ref.where_ref, bf16[384,1536]{1,0:T(8,128)(2,1)S(1)} %get-tuple-element.124.own_ref.left_ref, bf16[384,1536]{1,0:T(8,128)(2,1)S(1)} %collective-permute-done.19.came_ref.left_ref, ...), custom_call_target="tpu_custom_call" | custom-call | flops 1024 | bytes 1024 | tf_op jit(solution)/shard_map/pallas_call | solution.py:324
  89.2 1.5 collective-permute-start.22
  91.6 0.7 copy-done.51
  92.3 3.2 %shard_map.130 = (bf16[384,3072]{1,0:T(8,128)(2,1)S(1)}, f32[8,128]{1,0:T(8,128)}) custom-call(s32[4]{0:T(128)S(1)} %add_convert_fusion.near_ref, s32[10]{0:T(128)S(1)} %stack.64.slot_ref.where_ref, bf16[192,768]{1,0:T(8,128)(2,1)} %refs_0_.6, bf16[192,768]{1,0:T(8,128)(2,1)} %copy-done.25, bf16[192,768]{1,0:T(8,128)(2,1)} %copy-done.7, ...), custom_call_target="tpu_custom_call" | custom-call | flops 1024 | bytes 1024 | tf_op jit(solution)/shard_map/pallas_call | solution.py:209
  95.5 6.7 %shard_map.131 = (f32[384,1536]{1,0:T(8,128)S(1)}, f32[8,128]{1,0:T(8,128)S(1)}) custom-call(s32[1]{0:T(128)} %bitcast.5.side_ref, bf16[384,3072]{1,0:T(8,128)(2,1)S(1)} %get-tuple-element.134.left_ref.right_ref, bf16[3072,3072]{1,0:T(8,128)(2,1)} %weight_ref.7, f32[8,128]{1,0:T(8,128)S(1)} %get-tuple-element.135.rest_0_), custom_call_target="tpu_custom_call" | custom-call | flops 1024 | bytes 1024 | tf_op jit(solution)/shard_map/pallas_call | solution.py:243
  102.3 0.7 shard_map.132
  103.2 1.5 collective-permute-start.28
  105.2 6.7 %shard_map.133 = (f32[384,1536]{1,0:T(8,128)S(1)}, f32[8,128]{1,0:T(8,128)S(1)}) custom-call(s32[1]{0:T(128)} %bitcast.4.side_ref.core_ref, bf16[384,3072]{1,0:T(8,128)(2,1)S(1)} %get-tuple-element.134.left_ref.right_ref, bf16[3072,3072]{1,0:T(8,128)(2,1)} %weight_ref.7, f32[8,128]{1,0:T(8,128)S(1)} %get-tuple-element.139.rest_0_.refs_1_), custom_call_target="tpu_custom_call" | custom-call | flops 1024 | bytes 1024 | tf_op jit(solution)/shard_map/pallas_call | solution.py:243
  112.5 1.2 collective-permute-done.29.refs_5_
  113.7 0.8 shard_map.134
  114.4 1.0 shard_map.136
  115.6 1.4 collective-permute-start.30
  117.6 4.3 %shard_map.137 = (bf16[3072,3072]{1,0:T(8,128)(2,1)}, f32[8,128]{1,0:T(8,128)S(1)}) custom-call(s32[1]{0:T(128)} %bitcast.4.side_ref.core_ref, bf16[384,1536]{1,0:T(8,128)(2,1)S(1)} %get-tuple-element.124.own_ref.left_ref, bf16[384,3072]{1,0:T(8,128)(2,1)S(1)} %get-tuple-element.134.left_ref.right_ref, f32[8,128]{1,0:T(8,128)S(1)} %get-tuple-element.149.rest_0_), custom_call_target="tpu_custom_call" | custom-call | flops 1024 | bytes 1024 | tf_op jit(solution)/shard_map/pallas_call | solution.py:419
  122.0 7.8 %shard_map.138 = (bf16[2,192,768]{2,1,0:T(8,128)(2,1)S(1)}, bf16[2,192,768]{2,1,0:T(8,128)(2,1)S(1)}, f32[16,768]{1,0:T(8,128)S(1)}) custom-call(s32[10]{0:T(128)S(1)} %copy-done.39, bf16[384,1536]{1,0:T(8,128)(2,1)S(1)} %get-tuple-element.147.own_ref, bf16[384,1536]{1,0:T(8,128)(2,1)S(1)} %collective-permute-done.33.came_ref, ...), custom_call_target="tpu_custom_call" | custom-call | flops 1024 | bytes 1024 | tf_op jit(solution)/shard_map/pallas_call | solution.py:381
  129.8 0.8 shard_map.139
  130.6 4.4 %shard_map.141 = (bf16[3072,3072]{1,0:T(8,128)(2,1)}, f32[8,128]{1,0:T(8,128)S(1)}) custom-call(s32[1]{0:T(128)} %bitcast.4.side_ref.core_ref, bf16[384,1536]{1,0:T(8,128)(2,1)S(1)} %get-tuple-element.124.own_ref.left_ref, bf16[384,3072]{1,0:T(8,128)(2,1)S(1)} %get-tuple-element.134.left_ref.right_ref, ...), custom_call_target="tpu_custom_call", output_to_operand_aliasing={{0}: (3, {})} | custom-call | flops 1024 | bytes 1024 | tf_op jit(solution)/shard_map/pallas_call | solution.py:419
  135.0 1.3 collective-permute-start.34
  138.3 7.7 %shard_map.143 = (bf16[2,192,768]{2,1,0:T(8,128)(2,1)S(1)}, bf16[2,192,768]{2,1,0:T(8,128)(2,1)S(1)}, f32[16,768]{1,0:T(8,128)S(1)}) custom-call(s32[10]{0:T(128)S(1)} %copy-done.39, bf16[384,1536]{1,0:T(8,128)(2,1)S(1)} %get-tuple-element.147.own_ref, bf16[384,1536]{1,0:T(8,128)(2,1)S(1)} %collective-permute-done.33.came_ref, ...), custom_call_target="tpu_custom_call" | custom-call | flops 1024 | bytes 1024 | tf_op jit(solution)/shard_map/pallas_call | solution.py:381
  146.2 5.6 %collective-permute-done.37.refs_3_.refs_4_ = bf16[192,768]{1,0:T(8,128)(2,1)S(1)} collective-permute-done((bf16[192,768]{1,0:T(8,128)(2,1)S(1)}, bf16[192,768]{1,0:T(8,128)(2,1)S(1)}, u32[]{:S(2)}, u32[]{:S(2)}) %collective-permute-start.37) | collective-permute-done | bytes 294944 | tf_op jit(solution)/shard_map/ppermute | solution.py:38
  152.3 4.3 %shard_map.146 = (bf16[3072,3072]{1,0:T(8,128)(2,1)}, f32[8,128]{1,0:T(8,128)S(1)}) custom-call(s32[1]{0:T(128)} %bitcast.5.side_ref, bf16[384,1536]{1,0:T(8,128)(2,1)S(1)} %collective-permute-done.19.came_ref.left_ref, bf16[384,3072]{1,0:T(8,128)(2,1)S(1)} %get-tuple-element.134.left_ref.right_ref, ...), custom_call_target="tpu_custom_call", output_to_operand_aliasing={{0}: (3, {})} | custom-call | flops 1024 | bytes 1024 | tf_op jit(solution)/shard_map/pallas_call | solution.py:419
  156.7 0.8 shard_map.147
  157.4 1.3 collective-permute-start.40
  158.8 0.8 collective-permute-start.41
  160.2 4.3 %shard_map.148 = (bf16[3072,3072]{1,0:T(8,128)(2,1)}, f32[8,128]{1,0:T(8,128)S(1)}) custom-call(s32[1]{0:T(128)} %bitcast.5.side_ref, bf16[384,1536]{1,0:T(8,128)(2,1)S(1)} %collective-permute-done.19.came_ref.left_ref, bf16[384,3072]{1,0:T(8,128)(2,1)S(1)} %get-tuple-element.134.left_ref.right_ref, ...), custom_call_target="tpu_custom_call", output_to_operand_aliasing={{0}: (3, {})} | custom-call | flops 1024 | bytes 1024 | tf_op jit(solution)/shard_map/pallas_call | solution.py:419
  164.6 4.8 %shard_map.149 = (bf16[3072,3072]{1,0:T(8,128)(2,1)}, f32[8,128]{1,0:T(8,128)S(1)}, f32[1,3072]{1,0:T(1,128)}) custom-call(s32[1]{0:T(128)} %bitcast.4.side_ref.core_ref, bf16[384,3072]{1,0:T(8,128)(2,1)S(1)} %get-tuple-element.113.left_ref.normed_ref, bf16[384,1536]{1,0:T(8,128)(2,1)S(1)} %get-tuple-element.147.own_ref, ...), custom_call_target="tpu_custom_call" | custom-call | flops 1024 | bytes 1024 | tf_op jit(solution)/shard_map/pallas_call | solution.py:459
  169.3 1.5 shard_map.150
  171.4 1.4 collective-permute-start.44
  173.4 1.3 copy-done.1
  174.7 4.3 %shard_map.151 = (bf16[3072,3072]{1,0:T(8,128)(2,1)}, f32[8,128]{1,0:T(8,128)S(1)}) custom-call(s32[1]{0:T(128)} %bitcast.4.side_ref.core_ref, bf16[384,3072]{1,0:T(8,128)(2,1)S(1)} %get-tuple-element.113.left_ref.normed_ref, bf16[384,1536]{1,0:T(8,128)(2,1)S(1)} %get-tuple-element.147.own_ref, ...), custom_call_target="tpu_custom_call", output_to_operand_aliasing={{0}: (4, {})} | custom-call | flops 1024 | bytes 1024 | tf_op jit(solution)/shard_map/pallas_call | solution.py:459
  179.0 4.3 %shard_map.152 = (bf16[3072,3072]{1,0:T(8,128)(2,1)}, f32[8,128]{1,0:T(8,128)S(1)}) custom-call(s32[1]{0:T(128)} %bitcast.4.side_ref.core_ref, bf16[384,3072]{1,0:T(8,128)(2,1)S(1)} %get-tuple-element.113.left_ref.normed_ref, bf16[384,1536]{1,0:T(8,128)(2,1)S(1)} %get-tuple-element.147.own_ref, ...), custom_call_target="tpu_custom_call", output_to_operand_aliasing={{0}: (4, {})} | custom-call | flops 1024 | bytes 1024 | tf_op jit(solution)/shard_map/pallas_call | solution.py:459
  183.4 1.8 shard_map.153
  185.2 1.0 collective-permute-start.48
  186.5 1.2 collective-permute-start.46
  187.7 0.9 collective-permute-start.47
  188.6 4.3 %shard_map.154 = (bf16[3072,3072]{1,0:T(8,128)(2,1)}, f32[8,128]{1,0:T(8,128)S(1)}) custom-call(s32[1]{0:T(128)} %bitcast.4.side_ref.core_ref, bf16[384,3072]{1,0:T(8,128)(2,1)S(1)} %get-tuple-element.113.left_ref.normed_ref, bf16[384,1536]{1,0:T(8,128)(2,1)S(1)} %get-tuple-element.147.own_ref, ...), custom_call_target="tpu_custom_call", output_to_operand_aliasing={{0}: (4, {})} | custom-call | flops 1024 | bytes 1024 | tf_op jit(solution)/shard_map/pallas_call | solution.py:459
  193.0 1.4 fusion.13
  194.4 0.8 collective-permute-done.47.refs_1_
  195.2 1.3 fusion.6
  (205 shorter events, 20.4 us)
Async XLA Ops:
  0.6 10.2 %collective-permute-start.1 = (bf16[192,768]{1,0:T(8,128)(2,1)}, bf16[192,768]{1,0:T(8,128)(2,1)S(1)}, u32[]{:S(2)}, u32[]{:S(2)}) collective-permute-start(bf16[192,768]{1,0:T(8,128)(2,1)} %refs_0_.5), channel_id=1, source_target_pairs={{0,4},{4,8},{8,12},{12,14},{14,10},{10,6},{6,2},{2,0},{1,5},{5,9},... | collective-permute-start | bytes 884744 | tf_op jit(solution)/shard_map/ppermute | solution.py:38
  3.7 8.7 %collective-permute-start = (bf16[192,768]{1,0:T(8,128)(2,1)}, bf16[192,768]{1,0:T(8,128)(2,1)S(1)}, u32[]{:S(2)}, u32[]{:S(2)}) collective-permute-start(bf16[192,768]{1,0:T(8,128)(2,1)} %refs_0_.5), channel_id=1, source_target_pairs={{0,2},{4,0},{8,4},{12,8},{14,12},{10,14},{6,10},{2,6},{1,3},{5,1},... | collective-permute-start | bytes 884744 | tf_op jit(solution)/shard_map/ppermute | solution.py:38
  4.7 17.6 %copy-start.41 = (bf16[192,768]{1,0:T(8,128)(2,1)S(1)}, bf16[192,768]{1,0:T(8,128)(2,1)}, u32[]{:S(2)}) copy-start(bf16[192,768]{1,0:T(8,128)(2,1)} %refs_0_.6) | copy-start | bytes 884740
  12.4 18.5 %copy-start.23 = (bf16[192,768]{1,0:T(8,128)(2,1)}, bf16[192,768]{1,0:T(8,128)(2,1)S(1)}, u32[]{:S(2)}) copy-start(bf16[192,768]{1,0:T(8,128)(2,1)S(1)} %get-tuple-element.102.refs_1_.refs_7_) | copy-start | bytes 884740
  12.4 18.5 %copy-start.24 = (bf16[192,768]{1,0:T(8,128)(2,1)}, bf16[192,768]{1,0:T(8,128)(2,1)S(1)}, u32[]{:S(2)}) copy-start(bf16[192,768]{1,0:T(8,128)(2,1)S(1)} %get-tuple-element.101.refs_0_.refs_1_) | copy-start | bytes 884740
  12.4 7.6 %collective-permute-start.2 = (bf16[192,768]{1,0:T(8,128)(2,1)S(1)}, bf16[192,768]{1,0:T(8,128)(2,1)S(1)}, u32[]{:S(2)}, u32[]{:S(2)}) collective-permute-start(bf16[192,768]{1,0:T(8,128)(2,1)S(1)} %get-tuple-element.101.refs_0_.refs_1_), channel_id=1, source_target_pairs={{0,2},{4,0},{8,4},{12,8},{14,12},{10,14},{6,10},{2,6},{1,3},{5,1},... | collective-permute-start | bytes 884744 | tf_op jit(solution)/shard_map/ppermute | solution.py:38
  12.7 7.6 %collective-permute-start.3 = (bf16[192,768]{1,0:T(8,128)(2,1)S(1)}, bf16[192,768]{1,0:T(8,128)(2,1)S(1)}, u32[]{:S(2)}, u32[]{:S(2)}) collective-permute-start(bf16[192,768]{1,0:T(8,128)(2,1)S(1)} %get-tuple-element.102.refs_1_.refs_7_), channel_id=1, source_target_pairs={{0,4},{4,8},{8,12},{12,14},{14,10},{10,6},{6,2},{2,0},{1,5},{5,9},... | collective-permute-start | bytes 884744 | tf_op jit(solution)/shard_map/ppermute | solution.py:38
  20.3 6.7 %collective-permute-start.4 = (bf16[192,768]{1,0:T(8,128)(2,1)S(1)}, bf16[192,768]{1,0:T(8,128)(2,1)S(1)}, u32[]{:S(2)}, u32[]{:S(2)}) collective-permute-start(bf16[192,768]{1,0:T(8,128)(2,1)S(1)} %get-tuple-element.105.refs_0_.refs_2_), channel_id=1, source_target_pairs={{0,2},{4,0},{8,4},{12,8},{14,12},{10,14},{6,10},{2,6},{1,3},{5,1},... | collective-permute-start | bytes 884744 | tf_op jit(solution)/shard_map/ppermute | solution.py:38
  21.8 6.7 %collective-permute-start.5 = (bf16[192,768]{1,0:T(8,128)(2,1)S(1)}, bf16[192,768]{1,0:T(8,128)(2,1)S(1)}, u32[]{:S(2)}, u32[]{:S(2)}) collective-permute-start(bf16[192,768]{1,0:T(8,128)(2,1)S(1)} %get-tuple-element.106.refs_1_.refs_6_), channel_id=1, source_target_pairs={{0,4},{4,8},{8,12},{12,14},{14,10},{10,6},{6,2},{2,0},{1,5},{5,9},... | collective-permute-start | bytes 884744 | tf_op jit(solution)/shard_map/ppermute | solution.py:38
  23.4 13.2 %collective-permute-start.9 = (bf16[192,768]{1,0:T(8,128)(2,1)S(1)}, bf16[192,768]{1,0:T(8,128)(2,1)S(1)}, u32[]{:S(2)}, u32[]{:S(2)}) collective-permute-start(bf16[192,768]{1,0:T(8,128)(2,1)S(1)} %broadcast_select_fusion.3), channel_id=1, source_target_pairs={{0,1},{1,0},{2,3},{3,2},{4,5},{5,4},{6,7},{7,6},{8,9},{9,8},{10,11... | collective-permute-start | bytes 884744 | tf_op jit(solution)/shard_map/ppermute | solution.py:97
  28.6 6.7 %collective-permute-start.6 = (bf16[192,768]{1,0:T(8,128)(2,1)S(1)}, bf16[192,768]{1,0:T(8,128)(2,1)S(1)}, u32[]{:S(2)}, u32[]{:S(2)}) collective-permute-start(bf16[192,768]{1,0:T(8,128)(2,1)S(1)} %get-tuple-element.109.refs_0_.refs_3_.refs_1_), channel_id=1, source_target_pairs={{0,2},{4,0},{8,4},{12,8},{14,12},{10,14},{6,10},{2,6},{1,3},{5,1},... | collective-permute-start | bytes 884744 | tf_op jit(solution)/shard_map/ppermute | solution.py:38
  30.9 8.0 %collective-permute-start.10 = (bf16[192,768]{1,0:T(8,128)(2,1)}, bf16[192,768]{1,0:T(8,128)(2,1)S(1)}, u32[]{:S(2)}, u32[]{:S(2)}) collective-permute-start(bf16[192,768]{1,0:T(8,128)(2,1)} %broadcast_select_fusion.1), channel_id=1, source_target_pairs={{0,1},{1,0},{2,3},{3,2},{4,5},{5,4},{6,7},{7,6},{8,9},{9,8},{10,11... | collective-permute-start | bytes 884744 | tf_op jit(solution)/shard_map/ppermute | solution.py:97
  31.6 8.1 %collective-permute-start.8 = (bf16[192,768]{1,0:T(8,128)(2,1)}, bf16[192,768]{1,0:T(8,128)(2,1)S(1)}, u32[]{:S(2)}, u32[]{:S(2)}) collective-permute-start(bf16[192,768]{1,0:T(8,128)(2,1)} %broadcast_select_fusion.5), channel_id=1, source_target_pairs={{0,1},{1,0},{2,3},{3,2},{4,5},{5,4},{6,7},{7,6},{8,9},{9,8},{10,11... | collective-permute-start | bytes 884744 | tf_op jit(solution)/shard_map/ppermute | solution.py:97
  36.1 4.2 %collective-permute-start.7 = (bf16[192,768]{1,0:T(8,128)(2,1)}, bf16[192,768]{1,0:T(8,128)(2,1)S(1)}, u32[]{:S(2)}, u32[]{:S(2)}) collective-permute-start(bf16[192,768]{1,0:T(8,128)(2,1)} %broadcast_select_fusion.7), channel_id=1, source_target_pairs={{0,1},{1,0},{2,3},{3,2},{4,5},{5,4},{6,7},{7,6},{8,9},{9,8},{10,11... | collective-permute-start | bytes 884744 | tf_op jit(solution)/shard_map/ppermute | solution.py:97
  36.1 9.6 %collective-permute-start.13 = (bf16[192,768]{1,0:T(8,128)(2,1)}, bf16[192,768]{1,0:T(8,128)(2,1)S(1)}, u32[]{:S(2)}, u32[]{:S(2)}) collective-permute-start(bf16[192,768]{1,0:T(8,128)(2,1)} %shard_map.118), channel_id=1, source_target_pairs={{0,4},{4,8},{8,12},{12,14},{14,10},{10,6},{6,2},{2,0},{1,5},{5,9},... | collective-permute-start | bytes 884744 | tf_op jit(solution)/shard_map/ppermute | solution.py:38
  36.6 9.4 %collective-permute-start.12 = (bf16[192,768]{1,0:T(8,128)(2,1)}, bf16[192,768]{1,0:T(8,128)(2,1)S(1)}, u32[]{:S(2)}, u32[]{:S(2)}) collective-permute-start(bf16[192,768]{1,0:T(8,128)(2,1)} %shard_map.118), channel_id=1, source_target_pairs={{0,2},{4,0},{8,4},{12,8},{14,12},{10,14},{6,10},{2,6},{1,3},{5,1},... | collective-permute-start | bytes 884744 | tf_op jit(solution)/shard_map/ppermute | solution.py:38
  38.9 1.4 collective-permute-start.11
  39.8 51.4 %copy-start.38 = (s32[10]{0:T(128)}, s32[10]{0:T(128)S(1)}, u32[]{:S(2)}) copy-start(s32[10]{0:T(128)S(1)} %stack.64.slot_ref.where_ref) | copy-start | bytes 124
  46.0 34.2 %copy-start.27 = (bf16[192,768]{1,0:T(8,128)(2,1)}, bf16[192,768]{1,0:T(8,128)(2,1)S(1)}, u32[]{:S(2)}) copy-start(bf16[192,768]{1,0:T(8,128)(2,1)S(1)} %get-tuple-element.116.refs_7_) | copy-start | bytes 884740
  46.0 42.0 %copy-start.25 = (bf16[192,768]{1,0:T(8,128)(2,1)}, bf16[192,768]{1,0:T(8,128)(2,1)S(1)}, u32[]{:S(2)}) copy-start(bf16[192,768]{1,0:T(8,128)(2,1)S(1)} %get-tuple-element.115.rest_0_.refs_1_) | copy-start | bytes 884740
  46.0 9.1 %collective-permute-start.15 = (bf16[192,768]{1,0:T(8,128)(2,1)S(1)}, bf16[192,768]{1,0:T(8,128)(2,1)S(1)}, u32[]{:S(2)}, u32[]{:S(2)}) collective-permute-start(bf16[192,768]{1,0:T(8,128)(2,1)S(1)} %get-tuple-element.116.refs_7_), channel_id=1, source_target_pairs={{0,4},{4,8},{8,12},{12,14},{14,10},{10,6},{6,2},{2,0},{1,5},{5,9},... | collective-permute-start | bytes 884744 | tf_op jit(solution)/shard_map/ppermute | solution.py:38
  47.4 8.0 %collective-permute-start.14 = (bf16[192,768]{1,0:T(8,128)(2,1)S(1)}, bf16[192,768]{1,0:T(8,128)(2,1)S(1)}, u32[]{:S(2)}, u32[]{:S(2)}) collective-permute-start(bf16[192,768]{1,0:T(8,128)(2,1)S(1)} %get-tuple-element.115.rest_0_.refs_1_), channel_id=1, source_target_pairs={{0,2},{4,0},{8,4},{12,8},{14,12},{10,14},{6,10},{2,6},{1,3},{5,1},... | collective-permute-start | bytes 884744 | tf_op jit(solution)/shard_map/ppermute | solution.py:38
  55.4 22.7 %copy-start.7 = (bf16[192,768]{1,0:T(8,128)(2,1)}, bf16[192,768]{1,0:T(8,128)(2,1)S(1)}, u32[]{:S(2)}) copy-start(bf16[192,768]{1,0:T(8,128)(2,1)S(1)} %get-tuple-element.118.rest_0_.refs_1_.refs_2_) | copy-start | bytes 884740
  55.4 22.7 %copy-start.29 = (bf16[192,768]{1,0:T(8,128)(2,1)}, bf16[192,768]{1,0:T(8,128)(2,1)S(1)}, u32[]{:S(2)}) copy-start(bf16[192,768]{1,0:T(8,128)(2,1)S(1)} %get-tuple-element.121.refs_6_) | copy-start | bytes 884740
  55.4 10.7 %collective-permute-start.16 = (f32[384,1536]{1,0:T(8,128)S(1)}, f32[384,1536]{1,0:T(8,128)S(1)}, u32[]{:S(2)}, u32[]{:S(2)}) collective-permute-start(f32[384,1536]{1,0:T(8,128)S(1)} %shard_map.123), channel_id=1, source_target_pairs={{0,1},{1,0},{2,3},{3,2},{4,5},{5,4},{6,7},{7,6},{8,9},{9,8},{10,11... | collective-permute-start | bytes 7077896 | tf_op jit(solution)/shard_map/ppermute | solution.py:97
  55.4 9.4 %collective-permute-start.18 = (bf16[192,768]{1,0:T(8,128)(2,1)S(1)}, bf16[192,768]{1,0:T(8,128)(2,1)S(1)}, u32[]{:S(2)}, u32[]{:S(2)}) collective-permute-start(bf16[192,768]{1,0:T(8,128)(2,1)S(1)} %get-tuple-element.121.refs_6_), channel_id=1, source_target_pairs={{0,4},{4,8},{8,12},{12,14},{14,10},{10,6},{6,2},{2,0},{1,5},{5,9},... | collective-permute-start | bytes 884744 | tf_op jit(solution)/shard_map/ppermute | solution.py:38
  57.1 9.1 %collective-permute-start.17 = (bf16[192,768]{1,0:T(8,128)(2,1)S(1)}, bf16[192,768]{1,0:T(8,128)(2,1)S(1)}, u32[]{:S(2)}, u32[]{:S(2)}) collective-permute-start(bf16[192,768]{1,0:T(8,128)(2,1)S(1)} %get-tuple-element.118.rest_0_.refs_1_.refs_2_), channel_id=1, source_target_pairs={{0,2},{4,0},{8,4},{12,8},{14,12},{10,14},{6,10},{2,6},{1,3},{5,1},... | collective-permute-start | bytes 884744 | tf_op jit(solution)/shard_map/ppermute | solution.py:38
  66.1 21.8 %copy-start.30 = (bf16[192,768]{1,0:T(8,128)(2,1)}, bf16[192,768]{1,0:T(8,128)(2,1)S(1)}, u32[]{:S(2)}) copy-start(bf16[192,768]{1,0:T(8,128)(2,1)S(1)} %get-tuple-element.133.refs_5_) | copy-start | bytes 884740
  68.0 2.9 %collective-permute-start.19 = (bf16[384,1536]{1,0:T(8,128)(2,1)S(1)}, bf16[384,1536]{1,0:T(8,128)(2,1)S(1)}, u32[]{:S(2)}, u32[]{:S(2)}) collective-permute-start(bf16[384,1536]{1,0:T(8,128)(2,1)S(1)} %get-tuple-element.125), channel_id=1, source_target_pairs={{0,1},{1,0},{2,3},{3,2},{4,5},{5,4},{6,7},{7,6},{8,9},{9,8},{10,11... | collective-permute-start | bytes 3538952 | tf_op jit(solution)/shard_map/ppermute | solution.py:97
  77.9 51.9 %copy-start.8 = (bf16[2,192,768]{2,1,0:T(8,128)(2,1)}, bf16[2,192,768]{2,1,0:T(8,128)(2,1)S(1)}, u32[]{:S(2)}) copy-start(bf16[2,192,768]{2,1,0:T(8,128)(2,1)S(1)} %get-tuple-element.126.refs_0_.refs_3_) | copy-start | bytes 1769476
  77.9 2.3 %collective-permute-start.20 = (bf16[2,192,768]{2,1,0:T(8,128)(2,1)S(1)}, bf16[2,192,768]{2,1,0:T(8,128)(2,1)S(1)}, u32[]{:S(2)}, u32[]{:S(2)}) collective-permute-start(bf16[2,192,768]{2,1,0:T(8,128)(2,1)S(1)} %get-tuple-element.127), channel_id=1, source_target_pairs={{0,1},{1,0},{2,3},{3,2},{4,5},{5,4},{6,7},{7,6},{8,9},{9,8},{10,11... | collective-permute-start | bytes 1769480 | tf_op jit(solution)/shard_map/ppermute | solution.py:97
  78.2 11.0 %collective-permute-start.26 = (bf16[192,768]{1,0:T(8,128)(2,1)S(1)}, bf16[192,768]{1,0:T(8,128)(2,1)S(1)}, u32[]{:S(2)}, u32[]{:S(2)}) collective-permute-start(bf16[192,768]{1,0:T(8,128)(2,1)S(1)} %broadcast_select_fusion.2), channel_id=1, source_target_pairs={{0,1},{1,0},{2,3},{3,2},{4,5},{5,4},{6,7},{7,6},{8,9},{9,8},{10,11... | collective-permute-start | bytes 884744 | tf_op jit(solution)/shard_map/ppermute | solution.py:97
  78.6 10.0 %collective-permute-start.23 = (bf16[192,768]{1,0:T(8,128)(2,1)S(1)}, bf16[192,768]{1,0:T(8,128)(2,1)S(1)}, u32[]{:S(2)}, u32[]{:S(2)}) collective-permute-start(bf16[192,768]{1,0:T(8,128)(2,1)S(1)} %get-tuple-element.133.refs_5_), channel_id=1, source_target_pairs={{0,4},{4,8},{8,12},{12,14},{14,10},{10,6},{6,2},{2,0},{1,5},{5,9},... | collective-permute-start | bytes 884744 | tf_op jit(solution)/shard_map/ppermute | solution.py:38
  80.2 49.6 %copy-start.10 = (bf16[2,192,768]{2,1,0:T(8,128)(2,1)}, bf16[2,192,768]{2,1,0:T(8,128)(2,1)S(1)}, u32[]{:S(2)}) copy-start(bf16[2,192,768]{2,1,0:T(8,128)(2,1)S(1)} %collective-permute-done.20.refs_1_.refs_4_) | copy-start | bytes 1769476
  87.9 14.4 %collective-permute-start.21 = (bf16[2,192,768]{2,1,0:T(8,128)(2,1)S(1)}, bf16[2,192,768]{2,1,0:T(8,128)(2,1)S(1)}, u32[]{:S(2)}, u32[]{:S(2)}) collective-permute-start(bf16[2,192,768]{2,1,0:T(8,128)(2,1)S(1)} %get-tuple-element.131), channel_id=1, source_target_pairs={{0,1},{1,0},{2,3},{3,2},{4,5},{5,4},{6,7},{7,6},{8,9},{9,8},{10,11... | collective-permute-start | bytes 1769480 | tf_op jit(solution)/shard_map/ppermute | solution.py:97
  88.0 2.7 %collective-permute-start.25 = (bf16[192,768]{1,0:T(8,128)(2,1)S(1)}, bf16[192,768]{1,0:T(8,128)(2,1)S(1)}, u32[]{:S(2)}, u32[]{:S(2)}) collective-permute-start(bf16[192,768]{1,0:T(8,128)(2,1)S(1)} %broadcast_select_fusion.4), channel_id=1, source_target_pairs={{0,1},{1,0},{2,3},{3,2},{4,5},{5,4},{6,7},{7,6},{8,9},{9,8},{10,11... | collective-permute-start | bytes 884744 | tf_op jit(solution)/shard_map/ppermute | solution.py:97
  88.6 2.2 %collective-permute-start.27 = (bf16[192,768]{1,0:T(8,128)(2,1)S(1)}, bf16[192,768]{1,0:T(8,128)(2,1)S(1)}, u32[]{:S(2)}, u32[]{:S(2)}) collective-permute-start(bf16[192,768]{1,0:T(8,128)(2,1)S(1)} %broadcast_select_fusion), channel_id=1, source_target_pairs={{0,1},{1,0},{2,3},{3,2},{4,5},{5,4},{6,7},{7,6},{8,9},{9,8},{10,11... | collective-permute-start | bytes 884744 | tf_op jit(solution)/shard_map/ppermute | solution.py:97
  88.7 2.5 %collective-permute-start.24 = (bf16[192,768]{1,0:T(8,128)(2,1)S(1)}, bf16[192,768]{1,0:T(8,128)(2,1)S(1)}, u32[]{:S(2)}, u32[]{:S(2)}) collective-permute-start(bf16[192,768]{1,0:T(8,128)(2,1)S(1)} %broadcast_select_fusion.6), channel_id=1, source_target_pairs={{0,1},{1,0},{2,3},{3,2},{4,5},{5,4},{6,7},{7,6},{8,9},{9,8},{10,11... | collective-permute-start | bytes 884744 | tf_op jit(solution)/shard_map/ppermute | solution.py:97
  89.2 13.1 %collective-permute-start.22 = (bf16[192,768]{1,0:T(8,128)(2,1)S(1)}, bf16[192,768]{1,0:T(8,128)(2,1)S(1)}, u32[]{:S(2)}, u32[]{:S(2)}) collective-permute-start(bf16[192,768]{1,0:T(8,128)(2,1)S(1)} %get-tuple-element.132), channel_id=1, source_target_pairs={{0,4},{4,8},{8,12},{12,14},{14,10},{10,6},{6,2},{2,0},{1,5},{5,9},... | collective-permute-start | bytes 884744 | tf_op jit(solution)/shard_map/ppermute | solution.py:38
  103.0 11.4 %collective-permute-start.32 = (f32[384,1536]{1,0:T(8,128)S(1)}, f32[384,1536]{1,0:T(8,128)S(1)}, u32[]{:S(2)}, u32[]{:S(2)}) collective-permute-start(f32[384,1536]{1,0:T(8,128)S(1)} %shard_map.135), channel_id=1, source_target_pairs={{0,1},{1,0},{2,3},{3,2},{4,5},{5,4},{6,7},{7,6},{8,9},{9,8},{10,11... | collective-permute-start | bytes 7077896 | tf_op jit(solution)/shard_map/ppermute | solution.py:97
  103.2 9.3 %collective-permute-start.28 = (bf16[192,768]{1,0:T(8,128)(2,1)S(1)}, bf16[192,768]{1,0:T(8,128)(2,1)S(1)}, u32[]{:S(2)}, u32[]{:S(2)}) collective-permute-start(bf16[192,768]{1,0:T(8,128)(2,1)S(1)} %get-tuple-element.137), channel_id=1, source_target_pairs={{0,4},{4,8},{8,12},{12,14},{14,10},{10,6},{6,2},{2,0},{1,5},{5,9},... | collective-permute-start | bytes 884744 | tf_op jit(solution)/shard_map/ppermute | solution.py:38
  104.7 9.0 %collective-permute-start.29 = (bf16[192,768]{1,0:T(8,128)(2,1)S(1)}, bf16[192,768]{1,0:T(8,128)(2,1)S(1)}, u32[]{:S(2)}, u32[]{:S(2)}) collective-permute-start(bf16[192,768]{1,0:T(8,128)(2,1)S(1)} %get-tuple-element.138), channel_id=1, source_target_pairs={{0,2},{4,0},{8,4},{12,8},{14,12},{10,14},{6,10},{2,6},{1,3},{5,1},... | collective-permute-start | bytes 884744 | tf_op jit(solution)/shard_map/ppermute | solution.py:38
  115.5 6.5 %collective-permute-start.33 = (bf16[384,1536]{1,0:T(8,128)(2,1)S(1)}, bf16[384,1536]{1,0:T(8,128)(2,1)S(1)}, u32[]{:S(2)}, u32[]{:S(2)}) collective-permute-start(bf16[384,1536]{1,0:T(8,128)(2,1)S(1)} %get-tuple-element.148), channel_id=1, source_target_pairs={{0,1},{1,0},{2,3},{3,2},{4,5},{5,4},{6,7},{7,6},{8,9},{9,8},{10,11... | collective-permute-start | bytes 3538952 | tf_op jit(solution)/shard_map/ppermute | solution.py:97
  115.6 14.2 %collective-permute-start.30 = (bf16[192,768]{1,0:T(8,128)(2,1)S(1)}, bf16[192,768]{1,0:T(8,128)(2,1)S(1)}, u32[]{:S(2)}, u32[]{:S(2)}) collective-permute-start(bf16[192,768]{1,0:T(8,128)(2,1)S(1)} %get-tuple-element.141), channel_id=1, source_target_pairs={{0,4},{4,8},{8,12},{12,14},{14,10},{10,6},{6,2},{2,0},{1,5},{5,9},... | collective-permute-start | bytes 884744 | tf_op jit(solution)/shard_map/ppermute | solution.py:38
  116.9 12.8 %collective-permute-start.31 = (bf16[192,768]{1,0:T(8,128)(2,1)S(1)}, bf16[192,768]{1,0:T(8,128)(2,1)S(1)}, u32[]{:S(2)}, u32[]{:S(2)}) collective-permute-start(bf16[192,768]{1,0:T(8,128)(2,1)S(1)} %get-tuple-element.142), channel_id=1, source_target_pairs={{0,2},{4,0},{8,4},{12,8},{14,12},{10,14},{6,10},{2,6},{1,3},{5,1},... | collective-permute-start | bytes 884744 | tf_op jit(solution)/shard_map/ppermute | solution.py:38
  122.0 42.6 %copy-start = (bf16[384,1536]{1,0:T(8,128)(2,1)}, bf16[384,1536]{1,0:T(8,128)(2,1)S(1)}, u32[]{:S(2)}) copy-start(bf16[384,1536]{1,0:T(8,128)(2,1)S(1)} %collective-permute-done.33.came_ref) | copy-start | bytes 3538948
  129.7 26.9 %copy-start.12 = (bf16[2,192,768]{2,1,0:T(8,128)(2,1)}, bf16[2,192,768]{2,1,0:T(8,128)(2,1)S(1)}, u32[]{:S(2)}) copy-start(bf16[2,192,768]{2,1,0:T(8,128)(2,1)S(1)} %get-tuple-element.154.refs_0_.refs_2_) | copy-start | bytes 1769476
  130.6 6.5 %collective-permute-start.36 = (bf16[2,192,768]{2,1,0:T(8,128)(2,1)S(1)}, bf16[2,192,768]{2,1,0:T(8,128)(2,1)S(1)}, u32[]{:S(2)}, u32[]{:S(2)}) collective-permute-start(bf16[2,192,768]{2,1,0:T(8,128)(2,1)S(1)} %shard_map.140), channel_id=1, source_target_pairs={{0,1},{1,0},{2,3},{3,2},{4,5},{5,4},{6,7},{7,6},{8,9},{9,8},{10,11... | collective-permute-start | bytes 1769480 | tf_op jit(solution)/shard_map/ppermute | solution.py:97
  135.0 11.0 %collective-permute-start.34 = (bf16[192,768]{1,0:T(8,128)(2,1)S(1)}, bf16[192,768]{1,0:T(8,128)(2,1)S(1)}, u32[]{:S(2)}, u32[]{:S(2)}) collective-permute-start(bf16[192,768]{1,0:T(8,128)(2,1)S(1)} %get-tuple-element.152), channel_id=1, source_target_pairs={{0,4},{4,8},{8,12},{12,14},{14,10},{10,6},{6,2},{2,0},{1,5},{5,9},... | collective-permute-start | bytes 884744 | tf_op jit(solution)/shard_map/ppermute | solution.py:38
  136.3 9.8 %collective-permute-start.35 = (bf16[192,768]{1,0:T(8,128)(2,1)S(1)}, bf16[192,768]{1,0:T(8,128)(2,1)S(1)}, u32[]{:S(2)}, u32[]{:S(2)}) collective-permute-start(bf16[192,768]{1,0:T(8,128)(2,1)S(1)} %get-tuple-element.153), channel_id=1, source_target_pairs={{0,2},{4,0},{8,4},{12,8},{14,12},{10,14},{6,10},{2,6},{1,3},{5,1},... | collective-permute-start | bytes 884744 | tf_op jit(solution)/shard_map/ppermute | solution.py:38
  137.0 19.6 %copy-start.14 = (bf16[2,192,768]{2,1,0:T(8,128)(2,1)}, bf16[2,192,768]{2,1,0:T(8,128)(2,1)S(1)}, u32[]{:S(2)}) copy-start(bf16[2,192,768]{2,1,0:T(8,128)(2,1)S(1)} %collective-permute-done.36.refs_1_.refs_3_) | copy-start | bytes 1769476
  137.7 14.1 %collective-permute-start.37 = (bf16[192,768]{1,0:T(8,128)(2,1)S(1)}, bf16[192,768]{1,0:T(8,128)(2,1)S(1)}, u32[]{:S(2)}, u32[]{:S(2)}) collective-permute-start(bf16[192,768]{1,0:T(8,128)(2,1)S(1)} %get-tuple-element.165), channel_id=1, source_target_pairs={{0,2},{4,0},{8,4},{12,8},{14,12},{10,14},{6,10},{2,6},{1,3},{5,1},... | collective-permute-start | bytes 884744 | tf_op jit(solution)/shard_map/ppermute | solution.py:38
  146.0 23.3 %copy-start.2 = (bf16[2,192,768]{2,1,0:T(8,128)(2,1)}, bf16[2,192,768]{2,1,0:T(8,128)(2,1)S(1)}, u32[]{:S(2)}) copy-start(bf16[2,192,768]{2,1,0:T(8,128)(2,1)S(1)} %get-tuple-element.163.refs_0_.refs_3_) | copy-start | bytes 1769476
  151.8 4.9 %collective-permute-start.38 = (bf16[2,192,768]{2,1,0:T(8,128)(2,1)S(1)}, bf16[2,192,768]{2,1,0:T(8,128)(2,1)S(1)}, u32[]{:S(2)}, u32[]{:S(2)}) collective-permute-start(bf16[2,192,768]{2,1,0:T(8,128)(2,1)S(1)} %get-tuple-element.166), channel_id=1, source_target_pairs={{0,1},{1,0},{2,3},{3,2},{4,5},{5,4},{6,7},{7,6},{8,9},{9,8},{10,11... | collective-permute-start | bytes 1769480 | tf_op jit(solution)/shard_map/ppermute | solution.py:97
  151.8 4.9 %collective-permute-start.39 = (f32[16,768]{1,0:T(8,128)S(1)}, f32[16,768]{1,0:T(8,128)S(1)}, u32[]{:S(2)}, u32[]{:S(2)}) collective-permute-start(f32[16,768]{1,0:T(8,128)S(1)} %get-tuple-element.167.rest_1_.refs_5_), channel_id=1, source_target_pairs={{0,1},{1,0},{2,3},{3,2},{4,5},{5,4},{6,7},{7,6},{8,9},{9,8},{10,11... | collective-permute-start | bytes 147464 | tf_op jit(solution)/shard_map/ppermute | solution.py:97
  157.4 11.9 %collective-permute-start.40 = (bf16[192,768]{1,0:T(8,128)(2,1)S(1)}, bf16[192,768]{1,0:T(8,128)(2,1)S(1)}, u32[]{:S(2)}, u32[]{:S(2)}) collective-permute-start(bf16[192,768]{1,0:T(8,128)(2,1)S(1)} %get-tuple-element.170), channel_id=1, source_target_pairs={{0,4},{4,8},{8,12},{12,14},{14,10},{10,6},{6,2},{2,0},{1,5},{5,9},... | collective-permute-start | bytes 884744 | tf_op jit(solution)/shard_map/ppermute | solution.py:38
  158.8 10.6 %collective-permute-start.41 = (bf16[192,768]{1,0:T(8,128)(2,1)S(1)}, bf16[192,768]{1,0:T(8,128)(2,1)S(1)}, u32[]{:S(2)}, u32[]{:S(2)}) collective-permute-start(bf16[192,768]{1,0:T(8,128)(2,1)S(1)} %get-tuple-element.171), channel_id=1, source_target_pairs={{0,2},{4,0},{8,4},{12,8},{14,12},{10,14},{6,10},{2,6},{1,3},{5,1},... | collective-permute-start | bytes 884744 | tf_op jit(solution)/shard_map/ppermute | solution.py:38
  159.5 9.8 %collective-permute-start.42 = (f32[16,768]{1,0:T(8,128)S(1)}, f32[16,768]{1,0:T(8,128)S(1)}, u32[]{:S(2)}, u32[]{:S(2)}) collective-permute-start(f32[16,768]{1,0:T(8,128)S(1)} %get-tuple-element.172.refs_6_), channel_id=1, source_target_pairs={{0,2},{2,0},{4,6},{6,4},{8,10},{10,8},{12,14},{14,12},{1,3},{3,1},... | collective-permute-start | bytes 147464 | tf_op jit(solution)/shard_map/ppermute | solution.py:743
  170.8 12.5 %collective-permute-start.43 = (bf16[192,768]{1,0:T(8,128)(2,1)}, bf16[192,768]{1,0:T(8,128)(2,1)}, u32[]{:S(2)}, u32[]{:S(2)}) collective-permute-start(bf16[192,768]{1,0:T(8,128)(2,1)} %get-tuple-element.177), channel_id=1, source_target_pairs={{0,4},{4,8},{8,12},{12,14},{14,10},{10,6},{6,2},{2,0},{1,5},{5,9},... | collective-permute-start | bytes 884744 | tf_op jit(solution)/shard_map/ppermute | solution.py:38
  171.4 12.0 %collective-permute-start.44 = (bf16[192,768]{1,0:T(8,128)(2,1)}, bf16[192,768]{1,0:T(8,128)(2,1)}, u32[]{:S(2)}, u32[]{:S(2)}) collective-permute-start(bf16[192,768]{1,0:T(8,128)(2,1)} %get-tuple-element.178), channel_id=1, source_target_pairs={{0,2},{4,0},{8,4},{12,8},{14,12},{10,14},{6,10},{2,6},{1,3},{5,1},... | collective-permute-start | bytes 884744 | tf_op jit(solution)/shard_map/ppermute | solution.py:38
  172.9 10.5 %collective-permute-start.45 = (f32[16,768]{1,0:T(8,128)}, f32[16,768]{1,0:T(8,128)}, u32[]{:S(2)}, u32[]{:S(2)}) collective-permute-start(f32[16,768]{1,0:T(8,128)} %get-tuple-element.179.refs_6_), channel_id=1, source_target_pairs={{0,4},{2,6},{4,0},{6,2},{8,12},{10,14},{12,8},{14,10},{1,5},{3,7},... | collective-permute-start | bytes 147464 | tf_op jit(solution)/shard_map/ppermute | solution.py:743
  185.2 7.7 %collective-permute-start.48 = (f32[16,768]{1,0:T(8,128)S(1)}, f32[16,768]{1,0:T(8,128)S(1)}, u32[]{:S(2)}, u32[]{:S(2)}) collective-permute-start(f32[16,768]{1,0:T(8,128)S(1)} %get-tuple-element.192), channel_id=1, source_target_pairs={{0,8},{2,10},{4,12},{6,14},{8,0},{10,2},{12,4},{14,6},{1,9},{3,11}... | collective-permute-start | bytes 147464 | tf_op jit(solution)/shard_map/ppermute | solution.py:743
  186.5 7.9 %collective-permute-start.46 = (bf16[192,768]{1,0:T(8,128)(2,1)S(1)}, bf16[192,768]{1,0:T(8,128)(2,1)S(1)}, u32[]{:S(2)}, u32[]{:S(2)}) collective-permute-start(bf16[192,768]{1,0:T(8,128)(2,1)S(1)} %get-tuple-element.185), channel_id=1, source_target_pairs={{0,4},{4,8},{8,12},{12,14},{14,10},{10,6},{6,2},{2,0},{1,5},{5,9},... | collective-permute-start | bytes 884744 | tf_op jit(solution)/shard_map/ppermute | solution.py:38
  187.7 7.5 %collective-permute-start.47 = (bf16[192,768]{1,0:T(8,128)(2,1)S(1)}, bf16[192,768]{1,0:T(8,128)(2,1)S(1)}, u32[]{:S(2)}, u32[]{:S(2)}) collective-permute-start(bf16[192,768]{1,0:T(8,128)(2,1)S(1)} %get-tuple-element.186), channel_id=1, source_target_pairs={{0,2},{4,0},{8,4},{12,8},{14,12},{10,14},{6,10},{2,6},{1,3},{5,1},... | collective-permute-start | bytes 884744 | tf_op jit(solution)/shard_map/ppermute | solution.py:38
  (38 other events, 217.7 us)

commit v3 on v2

--- a/solution.py
+++ b/solution.py
@@ -183,11 +183,38 @@
     )(*blocks, *known)
 
 
+def other_half(blocks, near):
+    pairs = len(blocks) // 2
+    own, width = blocks[0].shape
+    part = own // 2
+
+    def body(near_ref, *refs):
+        for j in range(pairs):
+            flag = jnp.full((part, width), near_ref[j], jnp.int32) == 1
+            chosen = jnp.where(flag, refs[j + pairs][...].astype(f32), refs[j][...].astype(f32))
+            refs[-1][j] = chosen.astype(bf16)
+
+    return pl.pallas_call(
+        body,
+        grid_spec=pltpu.PrefetchScalarGridSpec(
+            num_scalar_prefetch=1,
+            grid=(2,),
+            in_specs=[pl.BlockSpec((part, width), lambda i, s: (i, 0))] * len(blocks),
+            out_specs=pl.BlockSpec((pairs, part, width), lambda i, s: (0, i, 0)),
+        ),
+        out_shape=jax.ShapeDtypeStruct((pairs, own, width), bf16),
+        compiler_params=params(16),
+        cost_estimate=cost(),
+    )(near, *map(held, blocks))
+
+
 def assemble(blocks, came, near, slots, norm=None, after=()):
     n = len(blocks)
-    pairs = len(came)
-    own, width = came[0].shape
-    operands = [held(x) for x in [*blocks, *came]] + (list(norm) if norm else [])
+    stacked = not isinstance(came, list)
+    pairs = len(blocks) // 2
+    own, width = blocks[0].shape
+    part = own // 2
+    operands = [held(x) for x in [*blocks, *([came] if stacked else came)]] + (list(norm) if norm else [])
 
     def body(near_ref, slot_ref, *refs):
         out_ref, mark_ref = refs[-2:]
@@ -195,29 +222,38 @@
         if norm:
             here, there, gain = refs[n + pairs : n + pairs + 3]
         for j in range(pairs):
-            flag = jnp.full((own, width), near_ref[j], jnp.int32) == 1
+            flag = jnp.full((part, width), near_ref[j], jnp.int32) == 1
             kept = jnp.where(flag, refs[j][...].astype(f32), refs[j + pairs][...].astype(f32))
             at = columns(slot_ref[j], width)
-            got = refs[n + j][...].astype(f32)
+            got = (refs[n][j] if stacked else refs[n + j][...]).astype(f32)
             if norm:
                 scale = gain[:, at]
                 kept = (kept - here[:, :1]) * here[:, 1:] * scale
                 got = (got - there[:, :1]) * there[:, 1:] * scale
-            out_ref[:own, at] = kept.astype(bf16)
-            out_ref[own:, at] = got.astype(bf16)
-
-    return pl.pallas_call(
+            out_ref[0, :, at] = kept.astype(bf16)
+            out_ref[1, :, at] = got.astype(bf16)
+
+    def by_tokens(x):
+        return pl.BlockSpec((part, x.shape[1]), lambda i, *_: (i, 0))
+
+    specs = [by_tokens(x) for x in operands]
+    if norm:
+        specs[-1] = whole(operands[-1])
+    if stacked:
+        specs[n] = pl.BlockSpec((pairs, part, width), lambda i, *_: (0, i, 0))
+    out, mark = pl.pallas_call(
         body,
         grid_spec=pltpu.PrefetchScalarGridSpec(
             num_scalar_prefetch=2,
-            grid=(1,),
-            in_specs=[whole(x) for x in operands] + [FAR] * len(after),
-            out_specs=[pl.BlockSpec((2 * own, pairs * width), lambda i, *_: (0, 0)), mark_spec()],
-        ),
-        out_shape=[jax.ShapeDtypeStruct((2 * own, pairs * width), bf16), MARK],
+            grid=(2,),
+            in_specs=specs + [FAR] * len(after),
+            out_specs=[pl.BlockSpec((2, part, pairs * width), lambda i, *_: (0, i, 0)), mark_spec()],
+        ),
+        out_shape=[jax.ShapeDtypeStruct((2, own, pairs * width), bf16), MARK],
         compiler_params=params(24),
         cost_estimate=cost(),
     )(near, slots, *operands, *after)
+    return out.reshape(2 * own, pairs * width), mark
 
 
 def side_product(left, weight, side, by_rows, turn, after=()):
@@ -432,7 +468,7 @@
     )(side.reshape(1), left, right, *extra, *after)
 
 
-def in_grad(left, own, came, core, quarter, into, after=()):
+def in_grad(left, own, came, core, part, into, after=()):
     tokens, height = left.shape
     width = own.shape[1]
     block = height // 8
@@ -452,7 +488,7 @@
                 outs[2][:, at_came] = jnp.sum(came_ref[...].astype(f32), axis=0, keepdims=True)
 
     out_shape = [pltpu.HBM((height, 2 * width), bf16), MARK]
-    out_specs = [pl.BlockSpec((block, 2 * width), lambda i, s: (2 * quarter + i, 0)), mark_spec()]
+    out_specs = [pl.BlockSpec((block, 2 * width), lambda i, s: (4 * part + i, 0)), mark_spec()]
     if into is None:
         out_shape.append(jax.ShapeDtypeStruct((1, 2 * width), f32))
         out_specs.append(pl.BlockSpec((1, 2 * width), lambda i, s: (0, 0)))
@@ -460,8 +496,8 @@
         body,
         grid_spec=pltpu.PrefetchScalarGridSpec(
             num_scalar_prefetch=1,
-            grid=(2,),
-            in_specs=[pl.BlockSpec((tokens, block), lambda i, s: (0, 2 * quarter + i)), whole(own), whole(came)]
+            grid=(4,),
+            in_specs=[pl.BlockSpec((tokens, block), lambda i, s: (0, 4 * part + i)), whole(own), whole(came)]
             + [FAR] * (len(extra) + len(after)),
             out_specs=out_specs,
         ),
@@ -705,18 +741,21 @@
     act_came = swap(act_turned)
     b1, b1_give, mark = branch_pairs(act_own, act_came, down_near, where, 0, shard_width)
     c4 = tie([c4], [mark])[0]
+    b1_give = tie([b1_give], [c4])[0]
     c_blocks = [cotangent, c1[0], c2[0], c3[0], c4, c3[1], c2[1], c1[1]]
-    cot_cols, _ = assemble(c_blocks, crossed(c_blocks), near_flags, where, after=[mark])
+    c_came = swap(other_half(c_blocks, near_flags))
 
     branch = Sum(ring, near_flags, [b1, None], [swap(b1_give), None], 0)
     got, _, mark = branch.hop(1, [None, None], after=[mark])
     b2, b2_give, mark = branch_pairs(act_own, act_came, down_near, where, 2, shard_width, after=[mark])
-    branch.kept[1], branch.came[1] = b2, swap(b2_give)
+    branch.kept[1], branch.came[1] = b2, swap(tie([b2_give], [got[0]])[0])
+    cot_cols, mark = assemble(c_blocks, c_came, near_flags, where, after=[mark])
+    got, _, mark = branch.hop(2, got, after=[mark])
     grad_give, mark = side_product(cot_cols, down_near, other, True, True, after=[mark])
-    got, _, mark = branch.hop(2, got, after=[mark])
+    got, _, mark = branch.hop(3, got, after=[mark])
     grad_came = swap(tie([grad_give], [mark])[0])
     grad_keep, mark = side_product(cot_cols, down_near, core, True, False, after=[mark])
-    got, _, mark = branch.hop(3, got, after=[mark])
+    branch_got, _, mark = branch.hop(4, got, after=[mark])
     hid_own, hid_turned, mark = slope_half(grad_keep, grad_came, slope, after=[mark])
     hid_came = swap(hid_turned)
     grad_out, mark = out_grad(act_own, cot_cols, core, 0, None, after=[mark])
@@ -724,35 +763,32 @@
     n1, n1_give, small = normed_pairs(
         hid_own, hid_came, up_near, gain_half, normed_cols, where, 0, shard_width, None, after=[mark]
     )
-    branch_got, _, mark = branch.hop(4, got, after=[small])
-    n1_give = tie([n1_give], [mark])[0]
-    grad_out, mark = out_grad(act_own, cot_cols, core, 1, grad_out, after=[mark])
+    branch_got = tie(branch_got, [small])
+    block_out = (tokens.astype(f32) + branch.last(near[0], branch_got)).astype(bf16)
+    n1_give = tie([n1_give], branch_got)[0]
+    grad_out, mark = out_grad(act_own, cot_cols, core, 1, grad_out, after=[small])
     norm = Sum(ring, near_flags, [n1, None], [swap(n1_give), None], 1)
     got, _, mark = norm.hop(1, [None, None], after=[mark])
     n2, n2_give, small = normed_pairs(
         hid_own, hid_came, up_near, gain_half, normed_cols, where, 2, shard_width, small, after=[mark]
     )
-    branch_got = tie(branch_got, [small])
-    n2_give, small = tie([n2_give, small], [branch_got[0], got[1]])
+    n2_give, small = tie([n2_give, small], [got[1]])
     norm.kept[1], norm.came[1] = n2, swap(n2_give)
     small_got = swap(small)
     grad_out, mark = out_grad(act_came, cot_cols, other, 0, grad_out, after=[small])
-    block_out = (tokens.astype(f32) + branch.last(near[0], branch_got)).astype(bf16)
 
     def toward(x, step):
         return lax.ppermute(x, "row", [(i, i ^ step) for i in range(n)])
 
     got, small, mark = norm.hop(2, got, (small, small_got), after=[mark])
     small_got = toward(small, 1)
-    grad_out, mark = out_grad(act_came, cot_cols, other, 1, grad_out, after=[mark])
     grad_in, mark, grad_bias = in_grad(normed_cols, hid_own, hid_came, core, 0, None, after=[mark])
     got, small, mark = norm.hop(3, got, (small, small_got), after=[mark])
     small_got = toward(small, 2)
     grad_in, mark = in_grad(normed_cols, hid_own, hid_came, core, 1, grad_in, after=[mark])
-    grad_in, mark = in_grad(normed_cols, hid_own, hid_came, core, 2, grad_in, after=[mark])
     got, small, mark = norm.hop(4, got, (small, small_got), after=[mark])
     small_got = toward(small, 4)
-    grad_in, mark = in_grad(normed_cols, hid_own, hid_came, core, 3, grad_in, after=[mark])
+    grad_out, mark = out_grad(act_came, cot_cols, other, 1, grad_out, after=[mark])
     got = tie(got, [mark])
     small = small + small_got
     token_mean, inverse_std = norms[:, :1], norms[:, 1:]

time: 197 us -> 192 us (0.975)
  waiting for transfers between devices: 36.4 us -> 31.6 us
  local copies, waits for them, and re-layouts: 6.97 us -> 9.02 us
    pallas_call x4 -> x2, Pallas kernels: 17.7 us -> 14.9 us  [in_grad(): pl.pallas_call(body, grid_spec=pltpu.PrefetchScalarGridSpec(num_scalar_pr...]
    ppermute x28, waiting for transfers between devices: 32.5 us -> 29.9 us  [shift(): lax.ppermute(x, 'row', [(order[i], order[(i + step) % n]) for i in range(...]
    pallas_call x0 -> x1, Pallas kernels: none -> 2.45 us  [other_half(): pl.pallas_call(body, grid_spec=pltpu.PrefetchScalarGridSpec(num_scalar_pr...]
    ppermute x18 -> x15, waiting for transfers between devices: 3.89 us -> 1.75 us  [swap(): return lax.ppermute(x, 'col', [(0, 1), (1, 0)])]
    unnamed x107, local copies, waits for them, and re-layouts: 6.67 us -> 8.72 us
  transfers between devices with their start and end apart: 49 -> 46, of which waited for: 22 -> 21; matrix products, arithmetic and copies ran while one was open for 3% -> 3% of each run, Pallas kernels for 48% -> 52%
where the time goes in v3:
time: 192 us
  Pallas kernels  109 us (57%)
  starting transfers between devices  35.3 us (18%)
  waiting for transfers between devices  31.6 us (16%)
  local copies, waits for them, and re-layouts  9.02 us (5%)
  other arithmetic  5.06 us (3%)
    ppermute x28, starting transfers between devices, shift(): lax.ppermute(x, 'row', [(order[i], order[(i + step) % n]) for i in range(...  31.1 us
    ppermute x28, waiting for transfers between devices, shift(): lax.ppermute(x, 'row', [(order[i], order[(i + step) % n]) for i in range(...  29.9 us
    pallas_call x4, Pallas kernels, side_product(): pl.pallas_call(body, grid_spec=pltpu.PrefetchScalarGridSpec(num_scalar_pr...  26.8 us
    pallas_call x4, Pallas kernels, out_grad(): pl.pallas_call(body, grid_spec=pltpu.PrefetchScalarGridSpec(num_scalar_pr...  17.4 us
    pallas_call x2, Pallas kernels, normed_pairs(): pl.pallas_call(body, grid_spec=pltpu.PrefetchScalarGridSpec(num_scalar_pr...  15.5 us
    pallas_call x2, Pallas kernels, in_grad(): pl.pallas_call(body, grid_spec=pltpu.PrefetchScalarGridSpec(num_scalar_pr...  14.9 us
    pallas_call x2, Pallas kernels, branch_pairs(): pl.pallas_call(body, grid_spec=pltpu.PrefetchScalarGridSpec(num_scalar_pr...  14 us
    unnamed x107, local copies, waits for them, and re-layouts  8.72 us
  transfers between devices with their start and end apart: 46, of which 21 were waited for; matrix products, arithmetic and copies ran while one was open for 3% of the time, Pallas kernels for 52%

profile of v3, /device:TPU:0, one launch (start us, length us, event | category | flops | bytes accessed | tf_op | source)
XLA Modules:
  0.0 191.6 jit_solution(2096743060860298855)
XLA Ops:
  0.6 3.1 %collective-permute-start.1 = (bf16[192,768]{1,0:T(8,128)(2,1)}, bf16[192,768]{1,0:T(8,128)(2,1)S(1)}, u32[]{:S(2)}, u32[]{:S(2)}) collective-permute-start(bf16[192,768]{1,0:T(8,128)(2,1)} %refs_0_.6), channel_id=1, source_target_pairs={{0,4},{4,8},{8,12},{12,14},{14,10},{10,6},{6,2},{2,0},{1,5},{5,9},... | collective-permute-start | bytes 884744 | tf_op jit(solution)/shard_map/ppermute | solution.py:38
  3.7 1.0 copy-done.24
  5.0 5.9 %collective-permute-done.1.refs_1_ = bf16[192,768]{1,0:T(8,128)(2,1)S(1)} collective-permute-done((bf16[192,768]{1,0:T(8,128)(2,1)}, bf16[192,768]{1,0:T(8,128)(2,1)S(1)}, u32[]{:S(2)}, u32[]{:S(2)}) %collective-permute-start.1) | collective-permute-done | bytes 294944 | tf_op jit(solution)/shard_map/ppermute | solution.py:38
  10.8 1.5 collective-permute-done.refs_0_
  12.7 1.7 collective-permute-start.3
  14.8 5.2 %collective-permute-done.2.refs_0_ = bf16[192,768]{1,0:T(8,128)(2,1)S(1)} collective-permute-done((bf16[192,768]{1,0:T(8,128)(2,1)S(1)}, bf16[192,768]{1,0:T(8,128)(2,1)S(1)}, u32[]{:S(2)}, u32[]{:S(2)}) %collective-permute-start.2) | collective-permute-done | bytes 294944 | tf_op jit(solution)/shard_map/ppermute | solution.py:38
  20.3 1.5 collective-permute-start.4
  23.5 3.5 %collective-permute-done.4.refs_0_ = bf16[192,768]{1,0:T(8,128)(2,1)S(1)} collective-permute-done((bf16[192,768]{1,0:T(8,128)(2,1)S(1)}, bf16[192,768]{1,0:T(8,128)(2,1)S(1)}, u32[]{:S(2)}, u32[]{:S(2)}) %collective-permute-start.4) | collective-permute-done | bytes 294944 | tf_op jit(solution)/shard_map/ppermute | solution.py:38
  27.0 1.5 collective-permute-done.5.refs_1_
  28.6 1.6 collective-permute-start.6
  30.1 0.7 broadcast_select_fusion
  30.9 0.7 broadcast_select_fusion.2
  32.1 3.1 %collective-permute-done.6.refs_0_.refs_4_ = bf16[192,768]{1,0:T(8,128)(2,1)S(1)} collective-permute-done((bf16[192,768]{1,0:T(8,128)(2,1)S(1)}, bf16[192,768]{1,0:T(8,128)(2,1)S(1)}, u32[]{:S(2)}, u32[]{:S(2)}) %collective-permute-start.6) | collective-permute-done | bytes 294944 | tf_op jit(solution)/shard_map/ppermute | solution.py:38
  35.3 0.8 broadcast_select_fusion.3
  36.6 1.5 collective-permute-start.12
  41.2 0.9 copy-done.40
  42.1 3.3 %shard_map.117 = (bf16[2,192,3072]{2,1,0:T(8,128)(2,1)S(1)}, f32[8,128]{1,0:T(8,128)S(1)}) custom-call(s32[4]{0:T(128)S(1)} %add_convert_fusion.near_ref, s32[10]{0:T(128)S(1)} %stack.64.slot_ref.where_ref, bf16[192,768]{1,0:T(8,128)(2,1)} %refs_0_.6, bf16[192,768]{1,0:T(8,128)(2,1)} %copy-done.28, bf16[192,768]{1,0:T(8,128)(2,1)} %copy-done.21, ...), custom_call_target="tpu_custom_call" | custom-call | flops 1024 | bytes 1024 | tf_op jit(solution)/shard_map/pallas_call | solution.py:244
  46.0 1.4 collective-permute-start.15
  48.0 6.7 %shard_map.120 = (f32[384,1536]{1,0:T(8,128)S(1)}, f32[8,128]{1,0:T(8,128)S(1)}) custom-call(s32[1]{0:T(128)} %bitcast.5.side_ref, bf16[384,3072]{1,0:T(8,128)(2,1)S(1)} %bitcast.31, bf16[3072,3072]{1,0:T(8,128)(2,1)} %weight_came.7, bf16[192,768]{1,0:T(8,128)(2,1)S(1)} %get-tuple-element.112.rest_0_.refs_1_), custom_call_target="tpu_custom_call" | custom-call | flops 1024 | bytes 1024 | tf_op jit(solution)/shard_map/pallas_call | solution.py:279
  56.1 1.6 collective-permute-start.18
  58.2 6.6 %shard_map.122 = (f32[384,1536]{1,0:T(8,128)S(1)}, f32[8,128]{1,0:T(8,128)S(1)}) custom-call(s32[1]{0:T(128)} %bitcast.4.side_ref.core_ref, bf16[384,3072]{1,0:T(8,128)(2,1)S(1)} %bitcast.32, bf16[3072,3072]{1,0:T(8,128)(2,1)} %weight_came.7, bf16[192,768]{1,0:T(8,128)(2,1)S(1)} %get-tuple-element.115.rest_0_.refs_1_.refs_2_), custom_call_target="tpu_custom_call" | custom-call | flops 1024 | bytes 1024 | tf_op jit(solution)/shard_map/pallas_call | solution.py:279
  64.8 1.3 collective-permute-done.17.refs_0_
  66.2 1.8 shard_map.125
  68.1 1.6 collective-permute-start.20
  69.7 1.2 collective-permute-done.19.came_ref.left_ref
  70.9 7.0 %shard_map.126 = (bf16[2,192,768]{2,1,0:T(8,128)(2,1)S(1)}, bf16[2,192,768]{2,1,0:T(8,128)(2,1)S(1)}, f32[8,128]{1,0:T(8,128)S(1)}) custom-call(s32[10]{0:T(128)S(1)} %stack.64.slot_ref.where_ref, bf16[384,1536]{1,0:T(8,128)(2,1)S(1)} %get-tuple-element.121.own_ref.left_ref, bf16[384,1536]{1,0:T(8,128)(2,1)S(1)} %collective-permute-done.19.came_ref.left_ref, ...), custom_call_target="tpu_custom_call" | custom-call | flops 1024 | bytes 1024 | tf_op jit(solution)/shard_map/pallas_call | solution.py:360
  78.7 2.5 %shard_map.132 = bf16[4,192,768]{2,1,0:T(8,128)(2,1)S(1)} custom-call(s32[4]{0:T(128)S(1)} %add_convert_fusion.near_ref, bf16[192,768]{1,0:T(8,128)(2,1)} %refs_0_.8, bf16[192,768]{1,0:T(8,128)(2,1)} %copy-done.30, bf16[192,768]{1,0:T(8,128)(2,1)} %copy-done.11, bf16[192,768]{1,0:T(8,128)(2,1)} %copy-done.23, bf16[192,768]{1,0:T(8,128)(2,1)} %copy-done.29, ...), custom_call_target="tpu_custom_call" | custom-call | flops 1024 | bytes 1024 | tf_op jit(solution)/shard_map/pallas_call | solution.py:197
  82.0 1.6 collective-permute-start.22
  83.7 7.0 %shard_map.130 = (bf16[2,192,768]{2,1,0:T(8,128)(2,1)S(1)}, bf16[2,192,768]{2,1,0:T(8,128)(2,1)S(1)}, f32[8,128]{1,0:T(8,128)S(1)}) custom-call(s32[10]{0:T(128)S(1)} %stack.64.slot_ref.where_ref, bf16[384,1536]{1,0:T(8,128)(2,1)S(1)} %get-tuple-element.121.own_ref.left_ref, bf16[384,1536]{1,0:T(8,128)(2,1)S(1)} %collective-permute-done.19.came_ref.left_ref, ...), custom_call_target="tpu_custom_call" | custom-call | flops 1024 | bytes 1024 | tf_op jit(solution)/shard_map/pallas_call | solution.py:360
  91.4 1.0 copy-done.47
  92.4 2.9 %shard_map.133 = (bf16[2,192,3072]{2,1,0:T(8,128)(2,1)S(1)}, f32[8,128]{1,0:T(8,128)S(1)}) custom-call(s32[4]{0:T(128)S(1)} %add_convert_fusion.near_ref, s32[10]{0:T(128)S(1)} %stack.64.slot_ref.where_ref, bf16[192,768]{1,0:T(8,128)(2,1)} %refs_0_.8, bf16[192,768]{1,0:T(8,128)(2,1)} %copy-done.30, bf16[192,768]{1,0:T(8,128)(2,1)} %copy-done.11, ...), custom_call_target="tpu_custom_call" | custom-call | flops 1024 | bytes 1024 | tf_op jit(solution)/shard_map/pallas_call | solution.py:244
  96.0 1.6 collective-permute-start.25
  98.1 6.7 %shard_map.135 = (f32[384,1536]{1,0:T(8,128)S(1)}, f32[8,128]{1,0:T(8,128)S(1)}) custom-call(s32[1]{0:T(128)} %bitcast.5.side_ref, bf16[384,3072]{1,0:T(8,128)(2,1)S(1)} %bitcast.37, bf16[3072,3072]{1,0:T(8,128)(2,1)} %weight_ref.7, f32[8,128]{1,0:T(8,128)S(1)} %get-tuple-element.136.rest_0_), custom_call_target="tpu_custom_call" | custom-call | flops 1024 | bytes 1024 | tf_op jit(solution)/shard_map/pallas_call | solution.py:279
  105.5 1.3 collective-permute-done.26.refs_5_
  106.8 0.8 shard_map.136
  107.6 1.5 collective-permute-start.27
  109.7 6.7 %shard_map.137 = (f32[384,1536]{1,0:T(8,128)S(1)}, f32[8,128]{1,0:T(8,128)S(1)}) custom-call(s32[1]{0:T(128)} %bitcast.4.side_ref.core_ref, bf16[384,3072]{1,0:T(8,128)(2,1)S(1)} %bitcast.38, bf16[3072,3072]{1,0:T(8,128)(2,1)} %weight_ref.7, f32[8,128]{1,0:T(8,128)S(1)} %get-tuple-element.140.rest_0_.refs_1_), custom_call_target="tpu_custom_call" | custom-call | flops 1024 | bytes 1024 | tf_op jit(solution)/shard_map/pallas_call | solution.py:279
  117.0 1.2 collective-permute-done.28.refs_5_
  118.3 0.8 shard_map.138
  119.0 1.0 shard_map.140
  120.2 1.1 collective-permute-start.29
  121.3 1.0 collective-permute-start.30
  122.2 4.3 %shard_map.141 = (bf16[3072,3072]{1,0:T(8,128)(2,1)}, f32[8,128]{1,0:T(8,128)S(1)}) custom-call(s32[1]{0:T(128)} %bitcast.4.side_ref.core_ref, bf16[384,1536]{1,0:T(8,128)(2,1)S(1)} %get-tuple-element.121.own_ref.left_ref, bf16[384,3072]{1,0:T(8,128)(2,1)S(1)} %bitcast.39, f32[8,128]{1,0:T(8,128)S(1)} %get-tuple-element.150.rest_0_), custom_call_target="tpu_custom_call" | custom-call | flops 1024 | bytes 1024 | tf_op jit(solution)/shard_map/pallas_call | solution.py:455
  126.6 7.8 %shard_map.142 = (bf16[2,192,768]{2,1,0:T(8,128)(2,1)S(1)}, bf16[2,192,768]{2,1,0:T(8,128)(2,1)S(1)}, f32[16,768]{1,0:T(8,128)S(1)}) custom-call(s32[10]{0:T(128)S(1)} %copy-done.43, bf16[384,1536]{1,0:T(8,128)(2,1)S(1)} %get-tuple-element.148.own_ref, bf16[384,1536]{1,0:T(8,128)(2,1)S(1)} %collective-permute-done.32.came_ref, ...), custom_call_target="tpu_custom_call" | custom-call | flops 1024 | bytes 1024 | tf_op jit(solution)/shard_map/pallas_call | solution.py:417
  134.4 0.9 copy-done.37
  135.3 4.3 %shard_map.145 = (bf16[3072,3072]{1,0:T(8,128)(2,1)}, f32[8,128]{1,0:T(8,128)S(1)}) custom-call(s32[1]{0:T(128)} %bitcast.4.side_ref.core_ref, bf16[384,1536]{1,0:T(8,128)(2,1)S(1)} %get-tuple-element.121.own_ref.left_ref, bf16[384,3072]{1,0:T(8,128)(2,1)S(1)} %bitcast.40, ...), custom_call_target="tpu_custom_call", output_to_operand_aliasing={{0}: (3, {})} | custom-call | flops 1024 | bytes 1024 | tf_op jit(solution)/shard_map/pallas_call | solution.py:455
  140.8 7.8 %shard_map.147 = (bf16[2,192,768]{2,1,0:T(8,128)(2,1)S(1)}, bf16[2,192,768]{2,1,0:T(8,128)(2,1)S(1)}, f32[16,768]{1,0:T(8,128)S(1)}) custom-call(s32[10]{0:T(128)S(1)} %copy-done.43, bf16[384,1536]{1,0:T(8,128)(2,1)S(1)} %get-tuple-element.148.own_ref, bf16[384,1536]{1,0:T(8,128)(2,1)S(1)} %collective-permute-done.32.came_ref, ...), custom_call_target="tpu_custom_call" | custom-call | flops 1024 | bytes 1024 | tf_op jit(solution)/shard_map/pallas_call | solution.py:417
  148.6 1.1 collective-permute-done.34.refs_2_.refs_4_
  150.2 4.3 %shard_map.149 = (bf16[3072,3072]{1,0:T(8,128)(2,1)}, f32[8,128]{1,0:T(8,128)S(1)}) custom-call(s32[1]{0:T(128)} %bitcast.5.side_ref, bf16[384,1536]{1,0:T(8,128)(2,1)S(1)} %collective-permute-done.19.came_ref.left_ref, bf16[384,3072]{1,0:T(8,128)(2,1)S(1)} %bitcast.41, ...), custom_call_target="tpu_custom_call", output_to_operand_aliasing={{0}: (3, {})} | custom-call | flops 1024 | bytes 1024 | tf_op jit(solution)/shard_map/pallas_call | solution.py:455
  154.6 0.7 shard_map.150
  155.3 1.1 collective-permute-start.37
  156.5 1.0 collective-permute-start.38
  158.0 7.7 %shard_map.151 = (bf16[3072,3072]{1,0:T(8,128)(2,1)}, f32[8,128]{1,0:T(8,128)S(1)}, f32[1,3072]{1,0:T(1,128)}) custom-call(s32[1]{0:T(128)} %bitcast.4.side_ref.core_ref, bf16[384,3072]{1,0:T(8,128)(2,1)S(1)} %bitcast.35, bf16[384,1536]{1,0:T(8,128)(2,1)S(1)} %get-tuple-element.148.own_ref, bf16[384,1536]{1,0:T(8,128)(2,1)S(1)} %collective-permute-done.32.came_ref, ...), custom_call_target="tpu_custom_call" | custom-call | flops 1024 | bytes 1024 | tf_op jit(solution)/shard_map/pallas_call | solution.py:495
  165.7 1.5 shard_map.152
  167.7 1.5 collective-permute-start.41
  169.7 1.3 copy-done.3
  171.0 7.2 %shard_map.153 = (bf16[3072,3072]{1,0:T(8,128)(2,1)}, f32[8,128]{1,0:T(8,128)S(1)}) custom-call(s32[1]{0:T(128)} %bitcast.4.side_ref.core_ref, bf16[384,3072]{1,0:T(8,128)(2,1)S(1)} %bitcast.36, bf16[384,1536]{1,0:T(8,128)(2,1)S(1)} %get-tuple-element.148.own_ref, bf16[384,1536]{1,0:T(8,128)(2,1)S(1)} %copy-done.3, ...), custom_call_target="tpu_custom_call", output_to_operand_aliasing={{0}: (4, {})} | custom-call | flops 1024 | bytes 1024 | tf_op jit(solution)/shard_map/pallas_call | solution.py:495
  178.3 2.0 %shard_map.154 = (bf16[192,768]{1,0:T(8,128)(2,1)S(1)}, bf16[192,768]{1,0:T(8,128)(2,1)S(1)}, f32[16,768]{1,0:T(8,128)S(1)}, f32[8,128]{1,0:T(8,128)S(1)}) custom-call(s32[4]{0:T(128)S(1)} %add_convert_fusion.near_ref, bf16[2,192,768]{2,1,0:T(8,128)(2,1)S(1)} %copy-done.17, bf16[2,192,768]{2,1,0:T(8,128)(2,1)S(1)} %copy-done.19, ...), custom_call_target="tpu_custom_call" | custom-call | flops 1024 | bytes 1024 | tf_op jit(solution)/shard_map/pallas_call | solution.py:552
  180.3 1.4 collective-permute-start.45
  181.9 0.9 collective-permute-start.43
  182.7 1.2 collective-permute-start.44
  184.0 4.4 %shard_map.155 = (bf16[3072,3072]{1,0:T(8,128)(2,1)}, f32[8,128]{1,0:T(8,128)S(1)}) custom-call(s32[1]{0:T(128)} %bitcast.5.side_ref, bf16[384,1536]{1,0:T(8,128)(2,1)S(1)} %copy-done.5, bf16[384,3072]{1,0:T(8,128)(2,1)S(1)} %bitcast.42, bf16[3072,3072]{1,0:T(8,128)(2,1)} %get-tuple-element.181.rest_0_, ...), custom_call_target="tpu_custom_call", output_to_operand_aliasing={{0}: (3, {})} | custom-call | flops 1024 | bytes 1024 | tf_op jit(solution)/shard_map/pallas_call | solution.py:455
  188.4 1.4 fusion.13
  190.3 1.3 fusion.6
  (196 shorter events, 19.7 us)
Async XLA Ops:
  0.6 10.2 %collective-permute-start.1 = (bf16[192,768]{1,0:T(8,128)(2,1)}, bf16[192,768]{1,0:T(8,128)(2,1)S(1)}, u32[]{:S(2)}, u32[]{:S(2)}) collective-permute-start(bf16[192,768]{1,0:T(8,128)(2,1)} %refs_0_.6), channel_id=1, source_target_pairs={{0,4},{4,8},{8,12},{12,14},{14,10},{10,6},{6,2},{2,0},{1,5},{5,9},... | collective-permute-start | bytes 884744 | tf_op jit(solution)/shard_map/ppermute | solution.py:38
  3.7 8.7 %collective-permute-start = (bf16[192,768]{1,0:T(8,128)(2,1)}, bf16[192,768]{1,0:T(8,128)(2,1)S(1)}, u32[]{:S(2)}, u32[]{:S(2)}) collective-permute-start(bf16[192,768]{1,0:T(8,128)(2,1)} %refs_0_.6), channel_id=1, source_target_pairs={{0,2},{4,0},{8,4},{12,8},{14,12},{10,14},{6,10},{2,6},{1,3},{5,1},... | collective-permute-start | bytes 884744 | tf_op jit(solution)/shard_map/ppermute | solution.py:38
  4.7 17.6 %copy-start.45 = (bf16[192,768]{1,0:T(8,128)(2,1)S(1)}, bf16[192,768]{1,0:T(8,128)(2,1)}, u32[]{:S(2)}) copy-start(bf16[192,768]{1,0:T(8,128)(2,1)} %refs_0_.8) | copy-start | bytes 884740
  12.4 18.5 %copy-start.27 = (bf16[192,768]{1,0:T(8,128)(2,1)}, bf16[192,768]{1,0:T(8,128)(2,1)S(1)}, u32[]{:S(2)}) copy-start(bf16[192,768]{1,0:T(8,128)(2,1)S(1)} %get-tuple-element.99.refs_1_.refs_7_) | copy-start | bytes 884740
  12.4 18.5 %copy-start.28 = (bf16[192,768]{1,0:T(8,128)(2,1)}, bf16[192,768]{1,0:T(8,128)(2,1)S(1)}, u32[]{:S(2)}) copy-start(bf16[192,768]{1,0:T(8,128)(2,1)S(1)} %get-tuple-element.98.refs_0_.refs_1_) | copy-start | bytes 884740
  12.4 7.6 %collective-permute-start.2 = (bf16[192,768]{1,0:T(8,128)(2,1)S(1)}, bf16[192,768]{1,0:T(8,128)(2,1)S(1)}, u32[]{:S(2)}, u32[]{:S(2)}) collective-permute-start(bf16[192,768]{1,0:T(8,128)(2,1)S(1)} %get-tuple-element.98.refs_0_.refs_1_), channel_id=1, source_target_pairs={{0,2},{4,0},{8,4},{12,8},{14,12},{10,14},{6,10},{2,6},{1,3},{5,1},... | collective-permute-start | bytes 884744 | tf_op jit(solution)/shard_map/ppermute | solution.py:38
  12.7 7.6 %collective-permute-start.3 = (bf16[192,768]{1,0:T(8,128)(2,1)S(1)}, bf16[192,768]{1,0:T(8,128)(2,1)S(1)}, u32[]{:S(2)}, u32[]{:S(2)}) collective-permute-start(bf16[192,768]{1,0:T(8,128)(2,1)S(1)} %get-tuple-element.99.refs_1_.refs_7_), channel_id=1, source_target_pairs={{0,4},{4,8},{8,12},{12,14},{14,10},{10,6},{6,2},{2,0},{1,5},{5,9},... | collective-permute-start | bytes 884744 | tf_op jit(solution)/shard_map/ppermute | solution.py:38
  20.3 11.3 %copy-start.21 = (bf16[192,768]{1,0:T(8,128)(2,1)}, bf16[192,768]{1,0:T(8,128)(2,1)S(1)}, u32[]{:S(2)}) copy-start(bf16[192,768]{1,0:T(8,128)(2,1)S(1)} %get-tuple-element.102.refs_0_.refs_2_) | copy-start | bytes 884740
  20.3 11.3 %copy-start.22 = (bf16[192,768]{1,0:T(8,128)(2,1)}, bf16[192,768]{1,0:T(8,128)(2,1)S(1)}, u32[]{:S(2)}) copy-start(bf16[192,768]{1,0:T(8,128)(2,1)S(1)} %get-tuple-element.103.refs_1_.refs_6_) | copy-start | bytes 884740
  20.3 6.7 %collective-permute-start.4 = (bf16[192,768]{1,0:T(8,128)(2,1)S(1)}, bf16[192,768]{1,0:T(8,128)(2,1)S(1)}, u32[]{:S(2)}, u32[]{:S(2)}) collective-permute-start(bf16[192,768]{1,0:T(8,128)(2,1)S(1)} %get-tuple-element.102.refs_0_.refs_2_), channel_id=1, source_target_pairs={{0,2},{4,0},{8,4},{12,8},{14,12},{10,14},{6,10},{2,6},{1,3},{5,1},... | collective-permute-start | bytes 884744 | tf_op jit(solution)/shard_map/ppermute | solution.py:38
  21.8 6.7 %collective-permute-start.5 = (bf16[192,768]{1,0:T(8,128)(2,1)S(1)}, bf16[192,768]{1,0:T(8,128)(2,1)S(1)}, u32[]{:S(2)}, u32[]{:S(2)}) collective-permute-start(bf16[192,768]{1,0:T(8,128)(2,1)S(1)} %get-tuple-element.103.refs_1_.refs_6_), channel_id=1, source_target_pairs={{0,4},{4,8},{8,12},{12,14},{14,10},{10,6},{6,2},{2,0},{1,5},{5,9},... | collective-permute-start | bytes 884744 | tf_op jit(solution)/shard_map/ppermute | solution.py:38
  22.3 12.9 %copy-start.25 = (bf16[192,768]{1,0:T(8,128)(2,1)S(1)}, bf16[192,768]{1,0:T(8,128)(2,1)}, u32[]{:S(2)}) copy-start(bf16[192,768]{1,0:T(8,128)(2,1)} %refs_0_.6) | copy-start | bytes 884740
  23.4 13.2 %collective-permute-start.9 = (bf16[192,768]{1,0:T(8,128)(2,1)S(1)}, bf16[192,768]{1,0:T(8,128)(2,1)S(1)}, u32[]{:S(2)}, u32[]{:S(2)}) collective-permute-start(bf16[192,768]{1,0:T(8,128)(2,1)S(1)} %broadcast_select_fusion.1), channel_id=1, source_target_pairs={{0,1},{1,0},{2,3},{3,2},{4,5},{5,4},{6,7},{7,6},{8,9},{9,8},{10,11... | collective-permute-start | bytes 884744 | tf_op jit(solution)/shard_map/ppermute | solution.py:97
  28.5 10.4 %copy-start.20 = (bf16[192,768]{1,0:T(8,128)(2,1)}, bf16[192,768]{1,0:T(8,128)(2,1)S(1)}, u32[]{:S(2)}) copy-start(bf16[192,768]{1,0:T(8,128)(2,1)S(1)} %get-tuple-element.107.refs_1_.refs_5_) | copy-start | bytes 884740
  28.6 6.7 %collective-permute-start.6 = (bf16[192,768]{1,0:T(8,128)(2,1)S(1)}, bf16[192,768]{1,0:T(8,128)(2,1)S(1)}, u32[]{:S(2)}, u32[]{:S(2)}) collective-permute-start(bf16[192,768]{1,0:T(8,128)(2,1)S(1)} %get-tuple-element.106.refs_0_.refs_3_.refs_1_), channel_id=1, source_target_pairs={{0,2},{4,0},{8,4},{12,8},{14,12},{10,14},{6,10},{2,6},{1,3},{5,1},... | collective-permute-start | bytes 884744 | tf_op jit(solution)/shard_map/ppermute | solution.py:38
  30.9 8.0 %collective-permute-start.10 = (bf16[192,768]{1,0:T(8,128)(2,1)}, bf16[192,768]{1,0:T(8,128)(2,1)S(1)}, u32[]{:S(2)}, u32[]{:S(2)}) collective-permute-start(bf16[192,768]{1,0:T(8,128)(2,1)} %broadcast_select_fusion), channel_id=1, source_target_pairs={{0,1},{1,0},{2,3},{3,2},{4,5},{5,4},{6,7},{7,6},{8,9},{9,8},{10,11... | collective-permute-start | bytes 884744 | tf_op jit(solution)/shard_map/ppermute | solution.py:97
  31.6 8.1 %collective-permute-start.8 = (bf16[192,768]{1,0:T(8,128)(2,1)}, bf16[192,768]{1,0:T(8,128)(2,1)S(1)}, u32[]{:S(2)}, u32[]{:S(2)}) collective-permute-start(bf16[192,768]{1,0:T(8,128)(2,1)} %broadcast_select_fusion.2), channel_id=1, source_target_pairs={{0,1},{1,0},{2,3},{3,2},{4,5},{5,4},{6,7},{7,6},{8,9},{9,8},{10,11... | collective-permute-start | bytes 884744 | tf_op jit(solution)/shard_map/ppermute | solution.py:97
  36.1 4.2 %collective-permute-start.7 = (bf16[192,768]{1,0:T(8,128)(2,1)}, bf16[192,768]{1,0:T(8,128)(2,1)S(1)}, u32[]{:S(2)}, u32[]{:S(2)}) collective-permute-start(bf16[192,768]{1,0:T(8,128)(2,1)} %broadcast_select_fusion.3), channel_id=1, source_target_pairs={{0,1},{1,0},{2,3},{3,2},{4,5},{5,4},{6,7},{7,6},{8,9},{9,8},{10,11... | collective-permute-start | bytes 884744 | tf_op jit(solution)/shard_map/ppermute | solution.py:97
  36.1 9.6 %collective-permute-start.13 = (bf16[192,768]{1,0:T(8,128)(2,1)}, bf16[192,768]{1,0:T(8,128)(2,1)S(1)}, u32[]{:S(2)}, u32[]{:S(2)}) collective-permute-start(bf16[192,768]{1,0:T(8,128)(2,1)} %shard_map.118), channel_id=1, source_target_pairs={{0,4},{4,8},{8,12},{12,14},{14,10},{10,6},{6,2},{2,0},{1,5},{5,9},... | collective-permute-start | bytes 884744 | tf_op jit(solution)/shard_map/ppermute | solution.py:38
  36.6 9.4 %collective-permute-start.12 = (bf16[192,768]{1,0:T(8,128)(2,1)}, bf16[192,768]{1,0:T(8,128)(2,1)S(1)}, u32[]{:S(2)}, u32[]{:S(2)}) collective-permute-start(bf16[192,768]{1,0:T(8,128)(2,1)} %shard_map.118), channel_id=1, source_target_pairs={{0,2},{4,0},{8,4},{12,8},{14,12},{10,14},{6,10},{2,6},{1,3},{5,1},... | collective-permute-start | bytes 884744 | tf_op jit(solution)/shard_map/ppermute | solution.py:38
  38.9 1.4 collective-permute-start.11
  39.8 51.6 %copy-start.42 = (s32[10]{0:T(128)}, s32[10]{0:T(128)S(1)}, u32[]{:S(2)}) copy-start(s32[10]{0:T(128)S(1)} %stack.64.slot_ref.where_ref) | copy-start | bytes 124
  46.0 8.9 %collective-permute-start.15 = (bf16[192,768]{1,0:T(8,128)(2,1)S(1)}, bf16[192,768]{1,0:T(8,128)(2,1)S(1)}, u32[]{:S(2)}, u32[]{:S(2)}) collective-permute-start(bf16[192,768]{1,0:T(8,128)(2,1)S(1)} %get-tuple-element.113.refs_7_), channel_id=1, source_target_pairs={{0,4},{4,8},{8,12},{12,14},{14,10},{10,6},{6,2},{2,0},{1,5},{5,9},... | collective-permute-start | bytes 884744 | tf_op jit(solution)/shard_map/ppermute | solution.py:38
  47.4 8.0 %collective-permute-start.14 = (bf16[192,768]{1,0:T(8,128)(2,1)S(1)}, bf16[192,768]{1,0:T(8,128)(2,1)S(1)}, u32[]{:S(2)}, u32[]{:S(2)}) collective-permute-start(bf16[192,768]{1,0:T(8,128)(2,1)S(1)} %get-tuple-element.112.rest_0_.refs_1_), channel_id=1, source_target_pairs={{0,2},{4,0},{8,4},{12,8},{14,12},{10,14},{6,10},{2,6},{1,3},{5,1},... | collective-permute-start | bytes 884744 | tf_op jit(solution)/shard_map/ppermute | solution.py:38
  55.4 10.7 %collective-permute-start.16 = (f32[384,1536]{1,0:T(8,128)S(1)}, f32[384,1536]{1,0:T(8,128)S(1)}, u32[]{:S(2)}, u32[]{:S(2)}) collective-permute-start(f32[384,1536]{1,0:T(8,128)S(1)} %shard_map.123), channel_id=1, source_target_pairs={{0,1},{1,0},{2,3},{3,2},{4,5},{5,4},{6,7},{7,6},{8,9},{9,8},{10,11... | collective-permute-start | bytes 7077896 | tf_op jit(solution)/shard_map/ppermute | solution.py:97
  56.1 8.7 %collective-permute-start.18 = (bf16[192,768]{1,0:T(8,128)(2,1)S(1)}, bf16[192,768]{1,0:T(8,128)(2,1)S(1)}, u32[]{:S(2)}, u32[]{:S(2)}) collective-permute-start(bf16[192,768]{1,0:T(8,128)(2,1)S(1)} %get-tuple-element.118.refs_6_), channel_id=1, source_target_pairs={{0,4},{4,8},{8,12},{12,14},{14,10},{10,6},{6,2},{2,0},{1,5},{5,9},... | collective-permute-start | bytes 884744 | tf_op jit(solution)/shard_map/ppermute | solution.py:38
  57.7 8.4 %collective-permute-start.17 = (bf16[192,768]{1,0:T(8,128)(2,1)S(1)}, bf16[192,768]{1,0:T(8,128)(2,1)S(1)}, u32[]{:S(2)}, u32[]{:S(2)}) collective-permute-start(bf16[192,768]{1,0:T(8,128)(2,1)S(1)} %get-tuple-element.115.rest_0_.refs_1_.refs_2_), channel_id=1, source_target_pairs={{0,2},{4,0},{8,4},{12,8},{14,12},{10,14},{6,10},{2,6},{1,3},{5,1},... | collective-permute-start | bytes 884744 | tf_op jit(solution)/shard_map/ppermute | solution.py:38
  68.0 2.9 %collective-permute-start.19 = (bf16[384,1536]{1,0:T(8,128)(2,1)S(1)}, bf16[384,1536]{1,0:T(8,128)(2,1)S(1)}, u32[]{:S(2)}, u32[]{:S(2)}) collective-permute-start(bf16[384,1536]{1,0:T(8,128)(2,1)S(1)} %get-tuple-element.122), channel_id=1, source_target_pairs={{0,1},{1,0},{2,3},{3,2},{4,5},{5,4},{6,7},{7,6},{8,9},{9,8},{10,11... | collective-permute-start | bytes 3538952 | tf_op jit(solution)/shard_map/ppermute | solution.py:97
  68.1 9.8 %collective-permute-start.20 = (bf16[192,768]{1,0:T(8,128)(2,1)S(1)}, bf16[192,768]{1,0:T(8,128)(2,1)S(1)}, u32[]{:S(2)}, u32[]{:S(2)}) collective-permute-start(bf16[192,768]{1,0:T(8,128)(2,1)S(1)} %get-tuple-element.125.refs_5_), channel_id=1, source_target_pairs={{0,4},{4,8},{8,12},{12,14},{14,10},{10,6},{6,2},{2,0},{1,5},{5,9},... | collective-permute-start | bytes 884744 | tf_op jit(solution)/shard_map/ppermute | solution.py:38
  70.9 79.3 %copy-start.4 = (bf16[384,1536]{1,0:T(8,128)(2,1)}, bf16[384,1536]{1,0:T(8,128)(2,1)S(1)}, u32[]{:S(2)}) copy-start(bf16[384,1536]{1,0:T(8,128)(2,1)S(1)} %collective-permute-done.19.came_ref.left_ref) | copy-start | bytes 3538948
  77.9 40.3 %copy-start.12 = (bf16[2,192,768]{2,1,0:T(8,128)(2,1)}, bf16[2,192,768]{2,1,0:T(8,128)(2,1)S(1)}, u32[]{:S(2)}) copy-start(bf16[2,192,768]{2,1,0:T(8,128)(2,1)S(1)} %get-tuple-element.123.refs_0_.refs_3_) | copy-start | bytes 1769476
  78.0 3.4 %collective-permute-start.21 = (bf16[2,192,768]{2,1,0:T(8,128)(2,1)S(1)}, bf16[2,192,768]{2,1,0:T(8,128)(2,1)S(1)}, u32[]{:S(2)}, u32[]{:S(2)}) collective-permute-start(bf16[2,192,768]{2,1,0:T(8,128)(2,1)S(1)} %shard_map.128), channel_id=1, source_target_pairs={{0,1},{1,0},{2,3},{3,2},{4,5},{5,4},{6,7},{7,6},{8,9},{9,8},{10,11... | collective-permute-start | bytes 1769480 | tf_op jit(solution)/shard_map/ppermute | solution.py:97
  81.2 10.2 %collective-permute-start.24 = (bf16[4,192,768]{2,1,0:T(8,128)(2,1)S(1)}, bf16[4,192,768]{2,1,0:T(8,128)(2,1)S(1)}, u32[]{:S(2)}, u32[]{:S(2)}) collective-permute-start(bf16[4,192,768]{2,1,0:T(8,128)(2,1)S(1)} %shard_map.132), channel_id=1, source_target_pairs={{0,1},{1,0},{2,3},{3,2},{4,5},{5,4},{6,7},{7,6},{8,9},{9,8},{10,11... | collective-permute-start | bytes 3538952 | tf_op jit(solution)/shard_map/ppermute | solution.py:97
  81.4 36.9 %copy-start.14 = (bf16[2,192,768]{2,1,0:T(8,128)(2,1)}, bf16[2,192,768]{2,1,0:T(8,128)(2,1)S(1)}, u32[]{:S(2)}) copy-start(bf16[2,192,768]{2,1,0:T(8,128)(2,1)S(1)} %collective-permute-done.21.refs_1_.refs_4_) | copy-start | bytes 1769476
  82.0 9.3 %collective-permute-start.22 = (bf16[192,768]{1,0:T(8,128)(2,1)S(1)}, bf16[192,768]{1,0:T(8,128)(2,1)S(1)}, u32[]{:S(2)}, u32[]{:S(2)}) collective-permute-start(bf16[192,768]{1,0:T(8,128)(2,1)S(1)} %get-tuple-element.130), channel_id=1, source_target_pairs={{0,4},{4,8},{8,12},{12,14},{14,10},{10,6},{6,2},{2,0},{1,5},{5,9},... | collective-permute-start | bytes 884744 | tf_op jit(solution)/shard_map/ppermute | solution.py:38
  91.4 3.9 %collective-permute-start.23 = (bf16[2,192,768]{2,1,0:T(8,128)(2,1)S(1)}, bf16[2,192,768]{2,1,0:T(8,128)(2,1)S(1)}, u32[]{:S(2)}, u32[]{:S(2)}) collective-permute-start(bf16[2,192,768]{2,1,0:T(8,128)(2,1)S(1)} %shard_map.131), channel_id=1, source_target_pairs={{0,1},{1,0},{2,3},{3,2},{4,5},{5,4},{6,7},{7,6},{8,9},{9,8},{10,11... | collective-permute-start | bytes 1769480 | tf_op jit(solution)/shard_map/ppermute | solution.py:97
  95.3 55.0 %copy-start = (bf16[2,192,3072]{2,1,0:T(8,128)(2,1)}, bf16[2,192,3072]{2,1,0:T(8,128)(2,1)S(1)}, u32[]{:S(2)}) copy-start(bf16[2,192,3072]{2,1,0:T(8,128)(2,1)S(1)} %get-tuple-element.135) | copy-start | bytes 7077892
  96.0 9.5 %collective-permute-start.25 = (bf16[192,768]{1,0:T(8,128)(2,1)S(1)}, bf16[192,768]{1,0:T(8,128)(2,1)S(1)}, u32[]{:S(2)}, u32[]{:S(2)}) collective-permute-start(bf16[192,768]{1,0:T(8,128)(2,1)S(1)} %get-tuple-element.133), channel_id=1, source_target_pairs={{0,4},{4,8},{8,12},{12,14},{14,10},{10,6},{6,2},{2,0},{1,5},{5,9},... | collective-permute-start | bytes 884744 | tf_op jit(solution)/shard_map/ppermute | solution.py:38
  97.6 9.1 %collective-permute-start.26 = (bf16[192,768]{1,0:T(8,128)(2,1)S(1)}, bf16[192,768]{1,0:T(8,128)(2,1)S(1)}, u32[]{:S(2)}, u32[]{:S(2)}) collective-permute-start(bf16[192,768]{1,0:T(8,128)(2,1)S(1)} %get-tuple-element.134), channel_id=1, source_target_pairs={{0,2},{4,0},{8,4},{12,8},{14,12},{10,14},{6,10},{2,6},{1,3},{5,1},... | collective-permute-start | bytes 884744 | tf_op jit(solution)/shard_map/ppermute | solution.py:38
  107.5 11.5 %collective-permute-start.31 = (f32[384,1536]{1,0:T(8,128)S(1)}, f32[384,1536]{1,0:T(8,128)S(1)}, u32[]{:S(2)}, u32[]{:S(2)}) collective-permute-start(f32[384,1536]{1,0:T(8,128)S(1)} %shard_map.139), channel_id=1, source_target_pairs={{0,1},{1,0},{2,3},{3,2},{4,5},{5,4},{6,7},{7,6},{8,9},{9,8},{10,11... | collective-permute-start | bytes 7077896 | tf_op jit(solution)/shard_map/ppermute | solution.py:97
  107.6 9.4 %collective-permute-start.27 = (bf16[192,768]{1,0:T(8,128)(2,1)S(1)}, bf16[192,768]{1,0:T(8,128)(2,1)S(1)}, u32[]{:S(2)}, u32[]{:S(2)}) collective-permute-start(bf16[192,768]{1,0:T(8,128)(2,1)S(1)} %get-tuple-element.138), channel_id=1, source_target_pairs={{0,4},{4,8},{8,12},{12,14},{14,10},{10,6},{6,2},{2,0},{1,5},{5,9},... | collective-permute-start | bytes 884744 | tf_op jit(solution)/shard_map/ppermute | solution.py:38
  109.2 9.1 %collective-permute-start.28 = (bf16[192,768]{1,0:T(8,128)(2,1)S(1)}, bf16[192,768]{1,0:T(8,128)(2,1)S(1)}, u32[]{:S(2)}, u32[]{:S(2)}) collective-permute-start(bf16[192,768]{1,0:T(8,128)(2,1)S(1)} %get-tuple-element.139), channel_id=1, source_target_pairs={{0,2},{4,0},{8,4},{12,8},{14,12},{10,14},{6,10},{2,6},{1,3},{5,1},... | collective-permute-start | bytes 884744 | tf_op jit(solution)/shard_map/ppermute | solution.py:38
  120.1 6.5 %collective-permute-start.32 = (bf16[384,1536]{1,0:T(8,128)(2,1)S(1)}, bf16[384,1536]{1,0:T(8,128)(2,1)S(1)}, u32[]{:S(2)}, u32[]{:S(2)}) collective-permute-start(bf16[384,1536]{1,0:T(8,128)(2,1)S(1)} %get-tuple-element.149), channel_id=1, source_target_pairs={{0,1},{1,0},{2,3},{3,2},{4,5},{5,4},{6,7},{7,6},{8,9},{9,8},{10,11... | collective-permute-start | bytes 3538952 | tf_op jit(solution)/shard_map/ppermute | solution.py:97
  120.2 14.2 %collective-permute-start.29 = (bf16[192,768]{1,0:T(8,128)(2,1)S(1)}, bf16[192,768]{1,0:T(8,128)(2,1)S(1)}, u32[]{:S(2)}, u32[]{:S(2)}) collective-permute-start(bf16[192,768]{1,0:T(8,128)(2,1)S(1)} %get-tuple-element.142), channel_id=1, source_target_pairs={{0,4},{4,8},{8,12},{12,14},{14,10},{10,6},{6,2},{2,0},{1,5},{5,9},... | collective-permute-start | bytes 884744 | tf_op jit(solution)/shard_map/ppermute | solution.py:38
  121.3 13.1 %collective-permute-start.30 = (bf16[192,768]{1,0:T(8,128)(2,1)S(1)}, bf16[192,768]{1,0:T(8,128)(2,1)S(1)}, u32[]{:S(2)}, u32[]{:S(2)}) collective-permute-start(bf16[192,768]{1,0:T(8,128)(2,1)S(1)} %get-tuple-element.143), channel_id=1, source_target_pairs={{0,2},{4,0},{8,4},{12,8},{14,12},{10,14},{6,10},{2,6},{1,3},{5,1},... | collective-permute-start | bytes 884744 | tf_op jit(solution)/shard_map/ppermute | solution.py:38
  126.6 31.4 %copy-start.2 = (bf16[384,1536]{1,0:T(8,128)(2,1)}, bf16[384,1536]{1,0:T(8,128)(2,1)S(1)}, u32[]{:S(2)}) copy-start(bf16[384,1536]{1,0:T(8,128)(2,1)S(1)} %collective-permute-done.32.came_ref) | copy-start | bytes 3538948
  134.3 20.2 %copy-start.16 = (bf16[2,192,768]{2,1,0:T(8,128)(2,1)}, bf16[2,192,768]{2,1,0:T(8,128)(2,1)S(1)}, u32[]{:S(2)}) copy-start(bf16[2,192,768]{2,1,0:T(8,128)(2,1)S(1)} %get-tuple-element.155.refs_0_.refs_2_) | copy-start | bytes 1769476
  135.3 4.4 %collective-permute-start.33 = (bf16[2,192,768]{2,1,0:T(8,128)(2,1)S(1)}, bf16[2,192,768]{2,1,0:T(8,128)(2,1)S(1)}, u32[]{:S(2)}, u32[]{:S(2)}) collective-permute-start(bf16[2,192,768]{2,1,0:T(8,128)(2,1)S(1)} %shard_map.144), channel_id=1, source_target_pairs={{0,1},{1,0},{2,3},{3,2},{4,5},{5,4},{6,7},{7,6},{8,9},{9,8},{10,11... | collective-permute-start | bytes 1769480 | tf_op jit(solution)/shard_map/ppermute | solution.py:97
  139.6 15.0 %copy-start.18 = (bf16[2,192,768]{2,1,0:T(8,128)(2,1)}, bf16[2,192,768]{2,1,0:T(8,128)(2,1)S(1)}, u32[]{:S(2)}) copy-start(bf16[2,192,768]{2,1,0:T(8,128)(2,1)S(1)} %collective-permute-done.33.refs_1_.refs_3_) | copy-start | bytes 1769476
  140.2 9.5 %collective-permute-start.34 = (bf16[192,768]{1,0:T(8,128)(2,1)S(1)}, bf16[192,768]{1,0:T(8,128)(2,1)S(1)}, u32[]{:S(2)}, u32[]{:S(2)}) collective-permute-start(bf16[192,768]{1,0:T(8,128)(2,1)S(1)} %get-tuple-element.163), channel_id=1, source_target_pairs={{0,2},{4,0},{8,4},{12,8},{14,12},{10,14},{6,10},{2,6},{1,3},{5,1},... | collective-permute-start | bytes 884744 | tf_op jit(solution)/shard_map/ppermute | solution.py:38
  148.6 17.1 %copy-start.6 = (bf16[2,192,768]{2,1,0:T(8,128)(2,1)}, bf16[2,192,768]{2,1,0:T(8,128)(2,1)S(1)}, u32[]{:S(2)}) copy-start(bf16[2,192,768]{2,1,0:T(8,128)(2,1)S(1)} %get-tuple-element.160.refs_0_.refs_3_) | copy-start | bytes 1769476
  149.7 4.9 %collective-permute-start.35 = (bf16[2,192,768]{2,1,0:T(8,128)(2,1)S(1)}, bf16[2,192,768]{2,1,0:T(8,128)(2,1)S(1)}, u32[]{:S(2)}, u32[]{:S(2)}) collective-permute-start(bf16[2,192,768]{2,1,0:T(8,128)(2,1)S(1)} %get-tuple-element.164), channel_id=1, source_target_pairs={{0,1},{1,0},{2,3},{3,2},{4,5},{5,4},{6,7},{7,6},{8,9},{9,8},{10,11... | collective-permute-start | bytes 1769480 | tf_op jit(solution)/shard_map/ppermute | solution.py:97
  149.7 4.9 %collective-permute-start.36 = (f32[16,768]{1,0:T(8,128)S(1)}, f32[16,768]{1,0:T(8,128)S(1)}, u32[]{:S(2)}, u32[]{:S(2)}) collective-permute-start(f32[16,768]{1,0:T(8,128)S(1)} %get-tuple-element.165.rest_1_.refs_5_), channel_id=1, source_target_pairs={{0,1},{1,0},{2,3},{3,2},{4,5},{5,4},{6,7},{7,6},{8,9},{9,8},{10,11... | collective-permute-start | bytes 147464 | tf_op jit(solution)/shard_map/ppermute | solution.py:97
  154.6 11.1 %copy-start.8 = (bf16[2,192,768]{2,1,0:T(8,128)(2,1)}, bf16[2,192,768]{2,1,0:T(8,128)(2,1)S(1)}, u32[]{:S(2)}) copy-start(bf16[2,192,768]{2,1,0:T(8,128)(2,1)S(1)} %collective-permute-done.35.refs_1_.refs_4_) | copy-start | bytes 1769476
  155.3 10.3 %collective-permute-start.37 = (bf16[192,768]{1,0:T(8,128)(2,1)S(1)}, bf16[192,768]{1,0:T(8,128)(2,1)S(1)}, u32[]{:S(2)}, u32[]{:S(2)}) collective-permute-start(bf16[192,768]{1,0:T(8,128)(2,1)S(1)} %get-tuple-element.168), channel_id=1, source_target_pairs={{0,4},{4,8},{8,12},{12,14},{14,10},{10,6},{6,2},{2,0},{1,5},{5,9},... | collective-permute-start | bytes 884744 | tf_op jit(solution)/shard_map/ppermute | solution.py:38
  156.5 9.2 %collective-permute-start.38 = (bf16[192,768]{1,0:T(8,128)(2,1)S(1)}, bf16[192,768]{1,0:T(8,128)(2,1)S(1)}, u32[]{:S(2)}, u32[]{:S(2)}) collective-permute-start(bf16[192,768]{1,0:T(8,128)(2,1)S(1)} %get-tuple-element.169), channel_id=1, source_target_pairs={{0,2},{4,0},{8,4},{12,8},{14,12},{10,14},{6,10},{2,6},{1,3},{5,1},... | collective-permute-start | bytes 884744 | tf_op jit(solution)/shard_map/ppermute | solution.py:38
  157.4 8.2 %collective-permute-start.39 = (f32[16,768]{1,0:T(8,128)S(1)}, f32[16,768]{1,0:T(8,128)S(1)}, u32[]{:S(2)}, u32[]{:S(2)}) collective-permute-start(f32[16,768]{1,0:T(8,128)S(1)} %get-tuple-element.170.refs_6_), channel_id=1, source_target_pairs={{0,2},{2,0},{4,6},{6,4},{8,10},{10,8},{12,14},{14,12},{1,3},{3,1},... | collective-permute-start | bytes 147464 | tf_op jit(solution)/shard_map/ppermute | solution.py:781
  167.2 11.1 %collective-permute-start.40 = (bf16[192,768]{1,0:T(8,128)(2,1)}, bf16[192,768]{1,0:T(8,128)(2,1)}, u32[]{:S(2)}, u32[]{:S(2)}) collective-permute-start(bf16[192,768]{1,0:T(8,128)(2,1)} %get-tuple-element.173), channel_id=1, source_target_pairs={{0,4},{4,8},{8,12},{12,14},{14,10},{10,6},{6,2},{2,0},{1,5},{5,9},... | collective-permute-start | bytes 884744 | tf_op jit(solution)/shard_map/ppermute | solution.py:38
  167.7 10.6 %collective-permute-start.41 = (bf16[192,768]{1,0:T(8,128)(2,1)}, bf16[192,768]{1,0:T(8,128)(2,1)}, u32[]{:S(2)}, u32[]{:S(2)}) collective-permute-start(bf16[192,768]{1,0:T(8,128)(2,1)} %get-tuple-element.174), channel_id=1, source_target_pairs={{0,2},{4,0},{8,4},{12,8},{14,12},{10,14},{6,10},{2,6},{1,3},{5,1},... | collective-permute-start | bytes 884744 | tf_op jit(solution)/shard_map/ppermute | solution.py:38
  169.2 9.1 %collective-permute-start.42 = (f32[16,768]{1,0:T(8,128)}, f32[16,768]{1,0:T(8,128)}, u32[]{:S(2)}, u32[]{:S(2)}) collective-permute-start(f32[16,768]{1,0:T(8,128)} %get-tuple-element.175.refs_6_), channel_id=1, source_target_pairs={{0,4},{2,6},{4,0},{6,2},{8,12},{10,14},{12,8},{14,10},{1,5},{3,7},... | collective-permute-start | bytes 147464 | tf_op jit(solution)/shard_map/ppermute | solution.py:781
  171.0 12.9 %copy-start.5 = (bf16[384,1536]{1,0:T(8,128)(2,1)S(1)}, bf16[384,1536]{1,0:T(8,128)(2,1)}, u32[]{:S(2)}) copy-start(bf16[384,1536]{1,0:T(8,128)(2,1)} %copy-done.4) | copy-start | bytes 3538948
  180.3 8.1 %collective-permute-start.45 = (f32[16,768]{1,0:T(8,128)S(1)}, f32[16,768]{1,0:T(8,128)S(1)}, u32[]{:S(2)}, u32[]{:S(2)}) collective-permute-start(f32[16,768]{1,0:T(8,128)S(1)} %get-tuple-element.186), channel_id=1, source_target_pairs={{0,8},{2,10},{4,12},{6,14},{8,0},{10,2},{12,4},{14,6},{1,9},{3,11}... | collective-permute-start | bytes 147464 | tf_op jit(solution)/shard_map/ppermute | solution.py:781
  181.9 8.0 %collective-permute-start.43 = (bf16[192,768]{1,0:T(8,128)(2,1)S(1)}, bf16[192,768]{1,0:T(8,128)(2,1)S(1)}, u32[]{:S(2)}, u32[]{:S(2)}) collective-permute-start(bf16[192,768]{1,0:T(8,128)(2,1)S(1)} %get-tuple-element.179), channel_id=1, source_target_pairs={{0,4},{4,8},{8,12},{12,14},{14,10},{10,6},{6,2},{2,0},{1,5},{5,9},... | collective-permute-start | bytes 884744 | tf_op jit(solution)/shard_map/ppermute | solution.py:38
  182.7 7.5 %collective-permute-start.44 = (bf16[192,768]{1,0:T(8,128)(2,1)S(1)}, bf16[192,768]{1,0:T(8,128)(2,1)S(1)}, u32[]{:S(2)}, u32[]{:S(2)}) collective-permute-start(bf16[192,768]{1,0:T(8,128)(2,1)S(1)} %get-tuple-element.180), channel_id=1, source_target_pairs={{0,2},{4,0},{8,4},{12,8},{14,12},{10,14},{6,10},{2,6},{1,3},{5,1},... | collective-permute-start | bytes 884744 | tf_op jit(solution)/shard_map/ppermute | solution.py:38
  (35 other events, 157.6 us)

commit v4 on v3

--- a/solution.py
+++ b/solution.py
@@ -728,7 +728,7 @@
     t_blocks = [tokens, t1[0], t2[0], t3[0], t4, t3[1], t2[1], t1[1]]
     normed_cols, mark = assemble(t_blocks, crossed(t_blocks), near_flags, where, (norms, swap(norms), gain_half))
 
-    c1 = tie(c1, [mark])
+    c1 = tie(c1, [norms])
     c2 = hop(*c1)
     hidden_give, mark = side_product(normed_cols, up_near, other, False, True, after=[c1[0]])
     c2 = tie(c2, [mark])

time: 192 us -> 194 us (1.010)
  waiting for transfers between devices: 31.6 us -> 34.9 us
  local copies, waits for them, and re-layouts: 9.02 us -> 6.47 us
    ppermute x28, waiting for transfers between devices: 29.9 us -> 32.6 us  [shift(): lax.ppermute(x, 'row', [(order[i], order[(i + step) % n]) for i in range(...]
    unnamed x107 -> x101, local copies, waits for them, and re-layouts: 8.72 us -> 6.15 us
  transfers between devices with their start and end apart: 46 -> 46, of which waited for: 21 -> 19; matrix products, arithmetic and copies ran while one was open for 3% -> 2% of each run, Pallas kernels for 52% -> 52%
where the time goes in v4:
time: 194 us; the launch traced here: 193 us
  Pallas kernels  110 us (57%)
  starting transfers between devices  36.2 us (19%)
  waiting for transfers between devices  34.9 us (18%)
  local copies, waits for them, and re-layouts  6.47 us (3%)
  other arithmetic  4.31 us (2%)
    ppermute x28, waiting for transfers between devices, shift(): lax.ppermute(x, 'row', [(order[i], order[(i + step) % n]) for i in range(...  32.6 us
    ppermute x28, starting transfers between devices, shift(): lax.ppermute(x, 'row', [(order[i], order[(i + step) % n]) for i in range(...  31.1 us
    pallas_call x4, Pallas kernels, side_product(): pl.pallas_call(body, grid_spec=pltpu.PrefetchScalarGridSpec(num_scalar_pr...  26.8 us
    pallas_call x4, Pallas kernels, out_grad(): pl.pallas_call(body, grid_spec=pltpu.PrefetchScalarGridSpec(num_scalar_pr...  17.4 us
    pallas_call x2, Pallas kernels, normed_pairs(): pl.pallas_call(body, grid_spec=pltpu.PrefetchScalarGridSpec(num_scalar_pr...  15.5 us
    pallas_call x2, Pallas kernels, in_grad(): pl.pallas_call(body, grid_spec=pltpu.PrefetchScalarGridSpec(num_scalar_pr...  14.9 us
    pallas_call x2, Pallas kernels, branch_pairs(): pl.pallas_call(body, grid_spec=pltpu.PrefetchScalarGridSpec(num_scalar_pr...  14 us
    pallas_call x8, Pallas kernels, partial(): pl.pallas_call(body, grid_spec=pltpu.PrefetchScalarGridSpec(num_scalar_pr...  7.64 us
  transfers between devices with their start and end apart: 46, of which 19 were waited for; matrix products, arithmetic and copies ran while one was open for 2% of the time, Pallas kernels for 52%

profile of v4, /device:TPU:0, one launch (start us, length us, event | category | flops | bytes accessed | tf_op | source)
XLA Modules:
  0.0 193.2 jit_solution(13530373780353962880)
XLA Ops:
  0.6 3.1 %collective-permute-start.1 = (bf16[192,768]{1,0:T(8,128)(2,1)}, bf16[192,768]{1,0:T(8,128)(2,1)S(1)}, u32[]{:S(2)}, u32[]{:S(2)}) collective-permute-start(bf16[192,768]{1,0:T(8,128)(2,1)} %refs_0_.6), channel_id=1, source_target_pairs={{0,4},{4,8},{8,12},{12,14},{14,10},{10,6},{6,2},{2,0},{1,5},{5,9},... | collective-permute-start | bytes 884744 | tf_op jit(solution)/shard_map/ppermute | solution.py:38
  3.7 1.0 copy-done.24
  5.0 5.9 %collective-permute-done.1.refs_1_ = bf16[192,768]{1,0:T(8,128)(2,1)S(1)} collective-permute-done((bf16[192,768]{1,0:T(8,128)(2,1)}, bf16[192,768]{1,0:T(8,128)(2,1)S(1)}, u32[]{:S(2)}, u32[]{:S(2)}) %collective-permute-start.1) | collective-permute-done | bytes 294944 | tf_op jit(solution)/shard_map/ppermute | solution.py:38
  10.8 1.5 collective-permute-done.refs_0_
  12.7 1.7 collective-permute-start.3
  14.8 5.2 %collective-permute-done.2.refs_0_ = bf16[192,768]{1,0:T(8,128)(2,1)S(1)} collective-permute-done((bf16[192,768]{1,0:T(8,128)(2,1)S(1)}, bf16[192,768]{1,0:T(8,128)(2,1)S(1)}, u32[]{:S(2)}, u32[]{:S(2)}) %collective-permute-start.2) | collective-permute-done | bytes 294944 | tf_op jit(solution)/shard_map/ppermute | solution.py:38
  20.3 1.5 collective-permute-start.4
  22.8 4.2 %collective-permute-done.4.refs_0_ = bf16[192,768]{1,0:T(8,128)(2,1)S(1)} collective-permute-done((bf16[192,768]{1,0:T(8,128)(2,1)S(1)}, bf16[192,768]{1,0:T(8,128)(2,1)S(1)}, u32[]{:S(2)}, u32[]{:S(2)}) %collective-permute-start.4) | collective-permute-done | bytes 294944 | tf_op jit(solution)/shard_map/ppermute | solution.py:38
  27.0 2.3 %collective-permute-done.5.refs_1_ = bf16[192,768]{1,0:T(8,128)(2,1)S(1)} collective-permute-done((bf16[192,768]{1,0:T(8,128)(2,1)S(1)}, bf16[192,768]{1,0:T(8,128)(2,1)S(1)}, u32[]{:S(2)}, u32[]{:S(2)}) %collective-permute-start.5) | collective-permute-done | bytes 294944 | tf_op jit(solution)/shard_map/ppermute | solution.py:38
  29.8 1.6 collective-permute-start.12
  31.4 1.6 collective-permute-start.6
  33.0 0.7 broadcast_select_fusion
  33.7 0.8 broadcast_select_fusion.2
  34.9 5.8 %collective-permute-done.6.refs_0_.refs_4_ = bf16[192,768]{1,0:T(8,128)(2,1)S(1)} collective-permute-done((bf16[192,768]{1,0:T(8,128)(2,1)S(1)}, bf16[192,768]{1,0:T(8,128)(2,1)S(1)}, u32[]{:S(2)}, u32[]{:S(2)}) %collective-permute-start.6) | collective-permute-done | bytes 294944 | tf_op jit(solution)/shard_map/ppermute | solution.py:38
  41.7 1.0 collective-permute-start.15
  42.7 1.1 collective-permute-start.14
  44.1 1.1 collective-permute-done.11.refs_13_
  45.9 3.8 %shard_map.117 = (bf16[2,192,3072]{2,1,0:T(8,128)(2,1)S(1)}, f32[8,128]{1,0:T(8,128)}) custom-call(s32[4]{0:T(128)S(1)} %add_convert_fusion.near_ref, s32[10]{0:T(128)S(1)} %stack.64.slot_ref.where_ref, bf16[192,768]{1,0:T(8,128)(2,1)} %refs_0_.6, bf16[192,768]{1,0:T(8,128)(2,1)} %copy-done.28, bf16[192,768]{1,0:T(8,128)(2,1)} %copy-done.21, ...), custom_call_target="tpu_custom_call" | custom-call | flops 1024 | bytes 1024 | tf_op jit(solution)/shard_map/pallas_call | solution.py:244
  49.8 6.7 %shard_map.120 = (f32[384,1536]{1,0:T(8,128)S(1)}, f32[8,128]{1,0:T(8,128)S(1)}) custom-call(s32[1]{0:T(128)} %bitcast.5.side_ref, bf16[384,3072]{1,0:T(8,128)(2,1)S(1)} %bitcast.31, bf16[3072,3072]{1,0:T(8,128)(2,1)} %weight_came.7, bf16[192,768]{1,0:T(8,128)(2,1)} %get-tuple-element.110.rest_0_.refs_1_), custom_call_target="tpu_custom_call" | custom-call | flops 1024 | bytes 1024 | tf_op jit(solution)/shard_map/pallas_call | solution.py:279
  57.2 0.9 collective-permute-start.18
  58.2 1.1 collective-permute-start.17
  59.2 6.6 %shard_map.122 = (f32[384,1536]{1,0:T(8,128)S(1)}, f32[8,128]{1,0:T(8,128)S(1)}) custom-call(s32[1]{0:T(128)} %bitcast.4.side_ref.core_ref, bf16[384,3072]{1,0:T(8,128)(2,1)S(1)} %bitcast.32, bf16[3072,3072]{1,0:T(8,128)(2,1)} %weight_came.7, bf16[192,768]{1,0:T(8,128)(2,1)S(1)} %get-tuple-element.113.rest_0_.refs_1_.refs_2_), custom_call_target="tpu_custom_call" | custom-call | flops 1024 | bytes 1024 | tf_op jit(solution)/shard_map/pallas_call | solution.py:279
  67.0 1.8 shard_map.125
  68.9 1.6 collective-permute-start.20
  70.5 1.2 collective-permute-done.19.came_ref.left_ref
  71.7 7.0 %shard_map.126 = (bf16[2,192,768]{2,1,0:T(8,128)(2,1)S(1)}, bf16[2,192,768]{2,1,0:T(8,128)(2,1)S(1)}, f32[8,128]{1,0:T(8,128)S(1)}) custom-call(s32[10]{0:T(128)S(1)} %stack.64.slot_ref.where_ref, bf16[384,1536]{1,0:T(8,128)(2,1)S(1)} %get-tuple-element.119.own_ref.left_ref, bf16[384,1536]{1,0:T(8,128)(2,1)S(1)} %collective-permute-done.19.came_ref.left_ref, ...), custom_call_target="tpu_custom_call" | custom-call | flops 1024 | bytes 1024 | tf_op jit(solution)/shard_map/pallas_call | solution.py:360
  79.6 2.5 %shard_map.132 = bf16[4,192,768]{2,1,0:T(8,128)(2,1)S(1)} custom-call(s32[4]{0:T(128)S(1)} %add_convert_fusion.near_ref, bf16[192,768]{1,0:T(8,128)(2,1)} %refs_0_.8, bf16[192,768]{1,0:T(8,128)(2,1)} %get-tuple-element.110.rest_0_.refs_1_, bf16[192,768]{1,0:T(8,128)(2,1)} %copy-done.11, bf16[192,768]{1,0:T(8,128)(2,1)} %copy-done.23, ...), custom_call_target="tpu_custom_call" | custom-call | flops 1024 | bytes 1024 | tf_op jit(solution)/shard_map/pallas_call | solution.py:197
  82.8 1.6 collective-permute-start.22
  84.5 7.0 %shard_map.130 = (bf16[2,192,768]{2,1,0:T(8,128)(2,1)S(1)}, bf16[2,192,768]{2,1,0:T(8,128)(2,1)S(1)}, f32[8,128]{1,0:T(8,128)S(1)}) custom-call(s32[10]{0:T(128)S(1)} %stack.64.slot_ref.where_ref, bf16[384,1536]{1,0:T(8,128)(2,1)S(1)} %get-tuple-element.119.own_ref.left_ref, bf16[384,1536]{1,0:T(8,128)(2,1)S(1)} %collective-permute-done.19.came_ref.left_ref, ...), custom_call_target="tpu_custom_call" | custom-call | flops 1024 | bytes 1024 | tf_op jit(solution)/shard_map/pallas_call | solution.py:360
  92.2 1.0 copy-done.44
  93.2 2.9 %shard_map.133 = (bf16[2,192,3072]{2,1,0:T(8,128)(2,1)S(1)}, f32[8,128]{1,0:T(8,128)S(1)}) custom-call(s32[4]{0:T(128)S(1)} %add_convert_fusion.near_ref, s32[10]{0:T(128)S(1)} %stack.64.slot_ref.where_ref, bf16[192,768]{1,0:T(8,128)(2,1)} %refs_0_.8, bf16[192,768]{1,0:T(8,128)(2,1)} %get-tuple-element.110.rest_0_.refs_1_, bf16[192,768]{1,0:T(8,128)(2,1)} %copy-done.11, ...), custom_call_target="tpu_custom_call" | custom-call | flops 1024 | bytes 1024 | tf_op jit(solution)/shard_map/pallas_call | solution.py:244
  96.8 1.6 collective-permute-start.25
  98.9 6.7 %shard_map.135 = (f32[384,1536]{1,0:T(8,128)S(1)}, f32[8,128]{1,0:T(8,128)S(1)}) custom-call(s32[1]{0:T(128)} %bitcast.5.side_ref, bf16[384,3072]{1,0:T(8,128)(2,1)S(1)} %bitcast.37, bf16[3072,3072]{1,0:T(8,128)(2,1)} %weight_ref.7, f32[8,128]{1,0:T(8,128)S(1)} %get-tuple-element.134.rest_0_), custom_call_target="tpu_custom_call" | custom-call | flops 1024 | bytes 1024 | tf_op jit(solution)/shard_map/pallas_call | solution.py:279
  106.3 1.3 collective-permute-done.26.refs_5_
  107.6 0.8 shard_map.136
  108.5 1.6 collective-permute-start.27
  110.5 6.7 %shard_map.137 = (f32[384,1536]{1,0:T(8,128)S(1)}, f32[8,128]{1,0:T(8,128)S(1)}) custom-call(s32[1]{0:T(128)} %bitcast.4.side_ref.core_ref, bf16[384,3072]{1,0:T(8,128)(2,1)S(1)} %bitcast.38, bf16[3072,3072]{1,0:T(8,128)(2,1)} %weight_ref.7, f32[8,128]{1,0:T(8,128)S(1)} %get-tuple-element.138.rest_0_.refs_1_), custom_call_target="tpu_custom_call" | custom-call | flops 1024 | bytes 1024 | tf_op jit(solution)/shard_map/pallas_call | solution.py:279
  117.9 1.3 collective-permute-done.28.refs_5_
  119.2 0.8 shard_map.138
  119.9 1.0 shard_map.140
  121.0 1.7 collective-permute-start.29
  123.1 4.3 %shard_map.141 = (bf16[3072,3072]{1,0:T(8,128)(2,1)}, f32[8,128]{1,0:T(8,128)S(1)}) custom-call(s32[1]{0:T(128)} %bitcast.4.side_ref.core_ref, bf16[384,1536]{1,0:T(8,128)(2,1)S(1)} %get-tuple-element.119.own_ref.left_ref, bf16[384,3072]{1,0:T(8,128)(2,1)S(1)} %bitcast.39, f32[8,128]{1,0:T(8,128)S(1)} %get-tuple-element.148.rest_0_), custom_call_target="tpu_custom_call" | custom-call | flops 1024 | bytes 1024 | tf_op jit(solution)/shard_map/pallas_call | solution.py:455
  127.5 7.8 %shard_map.142 = (bf16[2,192,768]{2,1,0:T(8,128)(2,1)S(1)}, bf16[2,192,768]{2,1,0:T(8,128)(2,1)S(1)}, f32[16,768]{1,0:T(8,128)S(1)}) custom-call(s32[10]{0:T(128)S(1)} %copy-done.40, bf16[384,1536]{1,0:T(8,128)(2,1)S(1)} %get-tuple-element.146.own_ref, bf16[384,1536]{1,0:T(8,128)(2,1)S(1)} %collective-permute-done.32.came_ref, ...), custom_call_target="tpu_custom_call" | custom-call | flops 1024 | bytes 1024 | tf_op jit(solution)/shard_map/pallas_call | solution.py:417
  135.3 0.9 copy-done.35
  136.2 4.3 %shard_map.145 = (bf16[3072,3072]{1,0:T(8,128)(2,1)}, f32[8,128]{1,0:T(8,128)S(1)}) custom-call(s32[1]{0:T(128)} %bitcast.4.side_ref.core_ref, bf16[384,1536]{1,0:T(8,128)(2,1)S(1)} %get-tuple-element.119.own_ref.left_ref, bf16[384,3072]{1,0:T(8,128)(2,1)S(1)} %bitcast.40, ...), custom_call_target="tpu_custom_call", output_to_operand_aliasing={{0}: (3, {})} | custom-call | flops 1024 | bytes 1024 | tf_op jit(solution)/shard_map/pallas_call | solution.py:455
  141.7 7.7 %shard_map.147 = (bf16[2,192,768]{2,1,0:T(8,128)(2,1)S(1)}, bf16[2,192,768]{2,1,0:T(8,128)(2,1)S(1)}, f32[16,768]{1,0:T(8,128)S(1)}) custom-call(s32[10]{0:T(128)S(1)} %copy-done.40, bf16[384,1536]{1,0:T(8,128)(2,1)S(1)} %get-tuple-element.146.own_ref, bf16[384,1536]{1,0:T(8,128)(2,1)S(1)} %collective-permute-done.32.came_ref, ...), custom_call_target="tpu_custom_call" | custom-call | flops 1024 | bytes 1024 | tf_op jit(solution)/shard_map/pallas_call | solution.py:417
  149.4 1.2 collective-permute-done.34.refs_2_.refs_4_
  151.1 4.3 %shard_map.149 = (bf16[3072,3072]{1,0:T(8,128)(2,1)}, f32[8,128]{1,0:T(8,128)S(1)}) custom-call(s32[1]{0:T(128)} %bitcast.5.side_ref, bf16[384,1536]{1,0:T(8,128)(2,1)S(1)} %collective-permute-done.19.came_ref.left_ref, bf16[384,3072]{1,0:T(8,128)(2,1)S(1)} %bitcast.41, ...), custom_call_target="tpu_custom_call", output_to_operand_aliasing={{0}: (3, {})} | custom-call | flops 1024 | bytes 1024 | tf_op jit(solution)/shard_map/pallas_call | solution.py:455
  155.5 0.7 shard_map.150
  156.3 1.7 collective-permute-start.37
  158.8 7.7 %shard_map.151 = (bf16[3072,3072]{1,0:T(8,128)(2,1)}, f32[8,128]{1,0:T(8,128)S(1)}, f32[1,3072]{1,0:T(1,128)}) custom-call(s32[1]{0:T(128)} %bitcast.4.side_ref.core_ref, bf16[384,3072]{1,0:T(8,128)(2,1)S(1)} %bitcast.35, bf16[384,1536]{1,0:T(8,128)(2,1)S(1)} %get-tuple-element.146.own_ref, bf16[384,1536]{1,0:T(8,128)(2,1)S(1)} %collective-permute-done.32.came_ref, ...), custom_call_target="tpu_custom_call" | custom-call | flops 1024 | bytes 1024 | tf_op jit(solution)/shard_map/pallas_call | solution.py:495
  166.6 1.5 shard_map.152
  168.1 1.1 collective-permute-start.40
  169.2 0.9 collective-permute-start.41
  170.1 1.1 collective-permute-start.42
  171.2 1.3 copy-done.3
  172.5 7.2 %shard_map.153 = (bf16[3072,3072]{1,0:T(8,128)(2,1)}, f32[8,128]{1,0:T(8,128)S(1)}) custom-call(s32[1]{0:T(128)} %bitcast.4.side_ref.core_ref, bf16[384,3072]{1,0:T(8,128)(2,1)S(1)} %bitcast.36, bf16[384,1536]{1,0:T(8,128)(2,1)S(1)} %get-tuple-element.146.own_ref, bf16[384,1536]{1,0:T(8,128)(2,1)S(1)} %copy-done.3, ...), custom_call_target="tpu_custom_call", output_to_operand_aliasing={{0}: (4, {})} | custom-call | flops 1024 | bytes 1024 | tf_op jit(solution)/shard_map/pallas_call | solution.py:495
  179.8 2.0 %shard_map.154 = (bf16[192,768]{1,0:T(8,128)(2,1)S(1)}, bf16[192,768]{1,0:T(8,128)(2,1)S(1)}, f32[16,768]{1,0:T(8,128)S(1)}, f32[8,128]{1,0:T(8,128)S(1)}) custom-call(s32[4]{0:T(128)S(1)} %add_convert_fusion.near_ref, bf16[2,192,768]{2,1,0:T(8,128)(2,1)S(1)} %copy-done.17, bf16[2,192,768]{2,1,0:T(8,128)(2,1)S(1)} %copy-done.19, ...), custom_call_target="tpu_custom_call" | custom-call | flops 1024 | bytes 1024 | tf_op jit(solution)/shard_map/pallas_call | solution.py:552
  181.8 1.5 collective-permute-start.45
  183.5 0.9 collective-permute-start.43
  184.4 1.2 collective-permute-start.44
  185.7 4.4 %shard_map.155 = (bf16[3072,3072]{1,0:T(8,128)(2,1)}, f32[8,128]{1,0:T(8,128)S(1)}) custom-call(s32[1]{0:T(128)} %bitcast.5.side_ref, bf16[384,1536]{1,0:T(8,128)(2,1)S(1)} %copy-done.5, bf16[384,3072]{1,0:T(8,128)(2,1)S(1)} %bitcast.42, bf16[3072,3072]{1,0:T(8,128)(2,1)} %get-tuple-element.179.rest_0_, ...), custom_call_target="tpu_custom_call", output_to_operand_aliasing={{0}: (3, {})} | custom-call | flops 1024 | bytes 1024 | tf_op jit(solution)/shard_map/pallas_call | solution.py:455
  190.1 1.4 fusion.13
  192.0 1.3 fusion.6
  (190 shorter events, 16.0 us)
Async XLA Ops:
  0.6 10.2 %collective-permute-start.1 = (bf16[192,768]{1,0:T(8,128)(2,1)}, bf16[192,768]{1,0:T(8,128)(2,1)S(1)}, u32[]{:S(2)}, u32[]{:S(2)}) collective-permute-start(bf16[192,768]{1,0:T(8,128)(2,1)} %refs_0_.6), channel_id=1, source_target_pairs={{0,4},{4,8},{8,12},{12,14},{14,10},{10,6},{6,2},{2,0},{1,5},{5,9},... | collective-permute-start | bytes 884744 | tf_op jit(solution)/shard_map/ppermute | solution.py:38
  3.7 8.7 %collective-permute-start = (bf16[192,768]{1,0:T(8,128)(2,1)}, bf16[192,768]{1,0:T(8,128)(2,1)S(1)}, u32[]{:S(2)}, u32[]{:S(2)}) collective-permute-start(bf16[192,768]{1,0:T(8,128)(2,1)} %refs_0_.6), channel_id=1, source_target_pairs={{0,2},{4,0},{8,4},{12,8},{14,12},{10,14},{6,10},{2,6},{1,3},{5,1},... | collective-permute-start | bytes 884744 | tf_op jit(solution)/shard_map/ppermute | solution.py:38
  4.7 17.6 %copy-start.42 = (bf16[192,768]{1,0:T(8,128)(2,1)S(1)}, bf16[192,768]{1,0:T(8,128)(2,1)}, u32[]{:S(2)}) copy-start(bf16[192,768]{1,0:T(8,128)(2,1)} %refs_0_.8) | copy-start | bytes 884740
  12.4 20.6 %copy-start.27 = (bf16[192,768]{1,0:T(8,128)(2,1)}, bf16[192,768]{1,0:T(8,128)(2,1)S(1)}, u32[]{:S(2)}) copy-start(bf16[192,768]{1,0:T(8,128)(2,1)S(1)} %get-tuple-element.98.refs_1_.refs_7_) | copy-start | bytes 884740
  12.4 21.3 %copy-start.28 = (bf16[192,768]{1,0:T(8,128)(2,1)}, bf16[192,768]{1,0:T(8,128)(2,1)S(1)}, u32[]{:S(2)}) copy-start(bf16[192,768]{1,0:T(8,128)(2,1)S(1)} %get-tuple-element.97.refs_0_.refs_1_) | copy-start | bytes 884740
  12.4 7.6 %collective-permute-start.2 = (bf16[192,768]{1,0:T(8,128)(2,1)S(1)}, bf16[192,768]{1,0:T(8,128)(2,1)S(1)}, u32[]{:S(2)}, u32[]{:S(2)}) collective-permute-start(bf16[192,768]{1,0:T(8,128)(2,1)S(1)} %get-tuple-element.97.refs_0_.refs_1_), channel_id=1, source_target_pairs={{0,2},{4,0},{8,4},{12,8},{14,12},{10,14},{6,10},{2,6},{1,3},{5,1},... | collective-permute-start | bytes 884744 | tf_op jit(solution)/shard_map/ppermute | solution.py:38
  12.7 7.6 %collective-permute-start.3 = (bf16[192,768]{1,0:T(8,128)(2,1)S(1)}, bf16[192,768]{1,0:T(8,128)(2,1)S(1)}, u32[]{:S(2)}, u32[]{:S(2)}) collective-permute-start(bf16[192,768]{1,0:T(8,128)(2,1)S(1)} %get-tuple-element.98.refs_1_.refs_7_), channel_id=1, source_target_pairs={{0,4},{4,8},{8,12},{12,14},{14,10},{10,6},{6,2},{2,0},{1,5},{5,9},... | collective-permute-start | bytes 884744 | tf_op jit(solution)/shard_map/ppermute | solution.py:38
  20.3 13.4 %copy-start.21 = (bf16[192,768]{1,0:T(8,128)(2,1)}, bf16[192,768]{1,0:T(8,128)(2,1)S(1)}, u32[]{:S(2)}) copy-start(bf16[192,768]{1,0:T(8,128)(2,1)S(1)} %get-tuple-element.101.refs_0_.refs_2_) | copy-start | bytes 884740
  20.3 13.4 %copy-start.22 = (bf16[192,768]{1,0:T(8,128)(2,1)}, bf16[192,768]{1,0:T(8,128)(2,1)S(1)}, u32[]{:S(2)}) copy-start(bf16[192,768]{1,0:T(8,128)(2,1)S(1)} %get-tuple-element.102.refs_1_.refs_6_) | copy-start | bytes 884740
  20.3 6.7 %collective-permute-start.4 = (bf16[192,768]{1,0:T(8,128)(2,1)S(1)}, bf16[192,768]{1,0:T(8,128)(2,1)S(1)}, u32[]{:S(2)}, u32[]{:S(2)}) collective-permute-start(bf16[192,768]{1,0:T(8,128)(2,1)S(1)} %get-tuple-element.101.refs_0_.refs_2_), channel_id=1, source_target_pairs={{0,2},{4,0},{8,4},{12,8},{14,12},{10,14},{6,10},{2,6},{1,3},{5,1},... | collective-permute-start | bytes 884744 | tf_op jit(solution)/shard_map/ppermute | solution.py:38
  21.8 7.5 %collective-permute-start.5 = (bf16[192,768]{1,0:T(8,128)(2,1)S(1)}, bf16[192,768]{1,0:T(8,128)(2,1)S(1)}, u32[]{:S(2)}, u32[]{:S(2)}) collective-permute-start(bf16[192,768]{1,0:T(8,128)(2,1)S(1)} %get-tuple-element.102.refs_1_.refs_6_), channel_id=1, source_target_pairs={{0,4},{4,8},{8,12},{12,14},{14,10},{10,6},{6,2},{2,0},{1,5},{5,9},... | collective-permute-start | bytes 884744 | tf_op jit(solution)/shard_map/ppermute | solution.py:38
  22.7 18.0 %copy-start.25 = (bf16[192,768]{1,0:T(8,128)(2,1)S(1)}, bf16[192,768]{1,0:T(8,128)(2,1)}, u32[]{:S(2)}) copy-start(bf16[192,768]{1,0:T(8,128)(2,1)} %refs_0_.6) | copy-start | bytes 884740
  22.7 20.0 %collective-permute-start.9 = (bf16[192,768]{1,0:T(8,128)(2,1)S(1)}, bf16[192,768]{1,0:T(8,128)(2,1)S(1)}, u32[]{:S(2)}, u32[]{:S(2)}) collective-permute-start(bf16[192,768]{1,0:T(8,128)(2,1)S(1)} %broadcast_select_fusion.1), channel_id=1, source_target_pairs={{0,1},{1,0},{2,3},{3,2},{4,5},{5,4},{6,7},{7,6},{8,9},{9,8},{10,11... | collective-permute-start | bytes 884744 | tf_op jit(solution)/shard_map/ppermute | solution.py:97
  29.4 12.3 %copy-start.20 = (bf16[192,768]{1,0:T(8,128)(2,1)}, bf16[192,768]{1,0:T(8,128)(2,1)S(1)}, u32[]{:S(2)}) copy-start(bf16[192,768]{1,0:T(8,128)(2,1)S(1)} %get-tuple-element.106.refs_1_.refs_5_) | copy-start | bytes 884740
  29.4 11.3 %collective-permute-start.13 = (bf16[192,768]{1,0:T(8,128)(2,1)S(1)}, bf16[192,768]{1,0:T(8,128)(2,1)}, u32[]{:S(2)}, u32[]{:S(2)}) collective-permute-start(bf16[192,768]{1,0:T(8,128)(2,1)S(1)} %shard_map.118), channel_id=1, source_target_pairs={{0,4},{4,8},{8,12},{12,14},{14,10},{10,6},{6,2},{2,0},{1,5},{5,9},... | collective-permute-start | bytes 884744 | tf_op jit(solution)/shard_map/ppermute | solution.py:38
  29.8 11.9 %collective-permute-start.12 = (bf16[192,768]{1,0:T(8,128)(2,1)S(1)}, bf16[192,768]{1,0:T(8,128)(2,1)}, u32[]{:S(2)}, u32[]{:S(2)}) collective-permute-start(bf16[192,768]{1,0:T(8,128)(2,1)S(1)} %shard_map.118), channel_id=1, source_target_pairs={{0,2},{4,0},{8,4},{12,8},{14,12},{10,14},{6,10},{2,6},{1,3},{5,1},... | collective-permute-start | bytes 884744 | tf_op jit(solution)/shard_map/ppermute | solution.py:38
  31.4 9.2 %collective-permute-start.6 = (bf16[192,768]{1,0:T(8,128)(2,1)S(1)}, bf16[192,768]{1,0:T(8,128)(2,1)S(1)}, u32[]{:S(2)}, u32[]{:S(2)}) collective-permute-start(bf16[192,768]{1,0:T(8,128)(2,1)S(1)} %get-tuple-element.105.refs_0_.refs_3_.refs_1_), channel_id=1, source_target_pairs={{0,2},{4,0},{8,4},{12,8},{14,12},{10,14},{6,10},{2,6},{1,3},{5,1},... | collective-permute-start | bytes 884744 | tf_op jit(solution)/shard_map/ppermute | solution.py:38
  34.8 9.0 %collective-permute-start.10 = (bf16[192,768]{1,0:T(8,128)(2,1)}, bf16[192,768]{1,0:T(8,128)(2,1)S(1)}, u32[]{:S(2)}, u32[]{:S(2)}) collective-permute-start(bf16[192,768]{1,0:T(8,128)(2,1)} %broadcast_select_fusion), channel_id=1, source_target_pairs={{0,1},{1,0},{2,3},{3,2},{4,5},{5,4},{6,7},{7,6},{8,9},{9,8},{10,11... | collective-permute-start | bytes 884744 | tf_op jit(solution)/shard_map/ppermute | solution.py:97
  40.6 3.4 %collective-permute-start.8 = (bf16[192,768]{1,0:T(8,128)(2,1)}, bf16[192,768]{1,0:T(8,128)(2,1)S(1)}, u32[]{:S(2)}, u32[]{:S(2)}) collective-permute-start(bf16[192,768]{1,0:T(8,128)(2,1)} %broadcast_select_fusion.2), channel_id=1, source_target_pairs={{0,1},{1,0},{2,3},{3,2},{4,5},{5,4},{6,7},{7,6},{8,9},{9,8},{10,11... | collective-permute-start | bytes 884744 | tf_op jit(solution)/shard_map/ppermute | solution.py:97
  40.7 4.5 %collective-permute-start.7 = (bf16[192,768]{1,0:T(8,128)(2,1)S(1)}, bf16[192,768]{1,0:T(8,128)(2,1)S(1)}, u32[]{:S(2)}, u32[]{:S(2)}) collective-permute-start(bf16[192,768]{1,0:T(8,128)(2,1)S(1)} %broadcast_select_fusion.3), channel_id=1, source_target_pairs={{0,1},{1,0},{2,3},{3,2},{4,5},{5,4},{6,7},{7,6},{8,9},{9,8},{10,11... | collective-permute-start | bytes 884744 | tf_op jit(solution)/shard_map/ppermute | solution.py:97
  41.7 14.8 %copy-start.37 = (f32[192,2]{1,0:T(8,128)}, f32[192,2]{1,0:T(8,128)S(1)}, u32[]{:S(2)}) copy-start(f32[192,2]{1,0:T(8,128)S(1)} %shard_map.116.refs_12_.refs_2_) | copy-start | bytes 4612
  41.7 14.8 %collective-permute-start.15 = (bf16[192,768]{1,0:T(8,128)(2,1)}, bf16[192,768]{1,0:T(8,128)(2,1)S(1)}, u32[]{:S(2)}, u32[]{:S(2)}) collective-permute-start(bf16[192,768]{1,0:T(8,128)(2,1)} %get-tuple-element.111.refs_7_), channel_id=1, source_target_pairs={{0,4},{4,8},{8,12},{12,14},{14,10},{10,6},{6,2},{2,0},{1,5},{5,9},... | collective-permute-start | bytes 884744 | tf_op jit(solution)/shard_map/ppermute | solution.py:38
  42.7 13.8 %collective-permute-start.14 = (bf16[192,768]{1,0:T(8,128)(2,1)}, bf16[192,768]{1,0:T(8,128)(2,1)S(1)}, u32[]{:S(2)}, u32[]{:S(2)}) collective-permute-start(bf16[192,768]{1,0:T(8,128)(2,1)} %get-tuple-element.110.rest_0_.refs_1_), channel_id=1, source_target_pairs={{0,2},{4,0},{8,4},{12,8},{14,12},{10,14},{6,10},{2,6},{1,3},{5,1},... | collective-permute-start | bytes 884744 | tf_op jit(solution)/shard_map/ppermute | solution.py:38
  43.9 1.3 collective-permute-start.11
  44.1 48.1 %copy-start.39 = (s32[10]{0:T(128)}, s32[10]{0:T(128)S(1)}, u32[]{:S(2)}) copy-start(s32[10]{0:T(128)S(1)} %stack.64.slot_ref.where_ref) | copy-start | bytes 124
  56.5 10.4 %collective-permute-start.16 = (f32[384,1536]{1,0:T(8,128)S(1)}, f32[384,1536]{1,0:T(8,128)S(1)}, u32[]{:S(2)}, u32[]{:S(2)}) collective-permute-start(f32[384,1536]{1,0:T(8,128)S(1)} %shard_map.123), channel_id=1, source_target_pairs={{0,1},{1,0},{2,3},{3,2},{4,5},{5,4},{6,7},{7,6},{8,9},{9,8},{10,11... | collective-permute-start | bytes 7077896 | tf_op jit(solution)/shard_map/ppermute | solution.py:97
  57.2 9.1 %collective-permute-start.18 = (bf16[192,768]{1,0:T(8,128)(2,1)S(1)}, bf16[192,768]{1,0:T(8,128)(2,1)S(1)}, u32[]{:S(2)}, u32[]{:S(2)}) collective-permute-start(bf16[192,768]{1,0:T(8,128)(2,1)S(1)} %get-tuple-element.116.refs_6_), channel_id=1, source_target_pairs={{0,4},{4,8},{8,12},{12,14},{14,10},{10,6},{6,2},{2,0},{1,5},{5,9},... | collective-permute-start | bytes 884744 | tf_op jit(solution)/shard_map/ppermute | solution.py:38
  58.2 8.8 %collective-permute-start.17 = (bf16[192,768]{1,0:T(8,128)(2,1)S(1)}, bf16[192,768]{1,0:T(8,128)(2,1)S(1)}, u32[]{:S(2)}, u32[]{:S(2)}) collective-permute-start(bf16[192,768]{1,0:T(8,128)(2,1)S(1)} %get-tuple-element.113.rest_0_.refs_1_.refs_2_), channel_id=1, source_target_pairs={{0,2},{4,0},{8,4},{12,8},{14,12},{10,14},{6,10},{2,6},{1,3},{5,1},... | collective-permute-start | bytes 884744 | tf_op jit(solution)/shard_map/ppermute | solution.py:38
  68.8 2.9 %collective-permute-start.19 = (bf16[384,1536]{1,0:T(8,128)(2,1)S(1)}, bf16[384,1536]{1,0:T(8,128)(2,1)S(1)}, u32[]{:S(2)}, u32[]{:S(2)}) collective-permute-start(bf16[384,1536]{1,0:T(8,128)(2,1)S(1)} %get-tuple-element.120), channel_id=1, source_target_pairs={{0,1},{1,0},{2,3},{3,2},{4,5},{5,4},{6,7},{7,6},{8,9},{9,8},{10,11... | collective-permute-start | bytes 3538952 | tf_op jit(solution)/shard_map/ppermute | solution.py:97
  68.9 9.8 %collective-permute-start.20 = (bf16[192,768]{1,0:T(8,128)(2,1)S(1)}, bf16[192,768]{1,0:T(8,128)(2,1)S(1)}, u32[]{:S(2)}, u32[]{:S(2)}) collective-permute-start(bf16[192,768]{1,0:T(8,128)(2,1)S(1)} %get-tuple-element.123.refs_5_), channel_id=1, source_target_pairs={{0,4},{4,8},{8,12},{12,14},{14,10},{10,6},{6,2},{2,0},{1,5},{5,9},... | collective-permute-start | bytes 884744 | tf_op jit(solution)/shard_map/ppermute | solution.py:38
  71.7 79.4 %copy-start.4 = (bf16[384,1536]{1,0:T(8,128)(2,1)}, bf16[384,1536]{1,0:T(8,128)(2,1)S(1)}, u32[]{:S(2)}) copy-start(bf16[384,1536]{1,0:T(8,128)(2,1)S(1)} %collective-permute-done.19.came_ref.left_ref) | copy-start | bytes 3538948
  78.7 40.4 %copy-start.12 = (bf16[2,192,768]{2,1,0:T(8,128)(2,1)}, bf16[2,192,768]{2,1,0:T(8,128)(2,1)S(1)}, u32[]{:S(2)}) copy-start(bf16[2,192,768]{2,1,0:T(8,128)(2,1)S(1)} %get-tuple-element.121.refs_0_.refs_3_) | copy-start | bytes 1769476
  78.8 3.5 %collective-permute-start.21 = (bf16[2,192,768]{2,1,0:T(8,128)(2,1)S(1)}, bf16[2,192,768]{2,1,0:T(8,128)(2,1)S(1)}, u32[]{:S(2)}, u32[]{:S(2)}) collective-permute-start(bf16[2,192,768]{2,1,0:T(8,128)(2,1)S(1)} %shard_map.128), channel_id=1, source_target_pairs={{0,1},{1,0},{2,3},{3,2},{4,5},{5,4},{6,7},{7,6},{8,9},{9,8},{10,11... | collective-permute-start | bytes 1769480 | tf_op jit(solution)/shard_map/ppermute | solution.py:97
  82.0 10.2 %collective-permute-start.24 = (bf16[4,192,768]{2,1,0:T(8,128)(2,1)S(1)}, bf16[4,192,768]{2,1,0:T(8,128)(2,1)S(1)}, u32[]{:S(2)}, u32[]{:S(2)}) collective-permute-start(bf16[4,192,768]{2,1,0:T(8,128)(2,1)S(1)} %shard_map.132), channel_id=1, source_target_pairs={{0,1},{1,0},{2,3},{3,2},{4,5},{5,4},{6,7},{7,6},{8,9},{9,8},{10,11... | collective-permute-start | bytes 3538952 | tf_op jit(solution)/shard_map/ppermute | solution.py:97
  82.2 36.9 %copy-start.14 = (bf16[2,192,768]{2,1,0:T(8,128)(2,1)}, bf16[2,192,768]{2,1,0:T(8,128)(2,1)S(1)}, u32[]{:S(2)}) copy-start(bf16[2,192,768]{2,1,0:T(8,128)(2,1)S(1)} %collective-permute-done.21.refs_1_.refs_4_) | copy-start | bytes 1769476
  82.8 9.3 %collective-permute-start.22 = (bf16[192,768]{1,0:T(8,128)(2,1)S(1)}, bf16[192,768]{1,0:T(8,128)(2,1)S(1)}, u32[]{:S(2)}, u32[]{:S(2)}) collective-permute-start(bf16[192,768]{1,0:T(8,128)(2,1)S(1)} %get-tuple-element.128), channel_id=1, source_target_pairs={{0,4},{4,8},{8,12},{12,14},{14,10},{10,6},{6,2},{2,0},{1,5},{5,9},... | collective-permute-start | bytes 884744 | tf_op jit(solution)/shard_map/ppermute | solution.py:38
  92.2 3.9 %collective-permute-start.23 = (bf16[2,192,768]{2,1,0:T(8,128)(2,1)S(1)}, bf16[2,192,768]{2,1,0:T(8,128)(2,1)S(1)}, u32[]{:S(2)}, u32[]{:S(2)}) collective-permute-start(bf16[2,192,768]{2,1,0:T(8,128)(2,1)S(1)} %shard_map.131), channel_id=1, source_target_pairs={{0,1},{1,0},{2,3},{3,2},{4,5},{5,4},{6,7},{7,6},{8,9},{9,8},{10,11... | collective-permute-start | bytes 1769480 | tf_op jit(solution)/shard_map/ppermute | solution.py:97
  96.1 55.1 %copy-start = (bf16[2,192,3072]{2,1,0:T(8,128)(2,1)}, bf16[2,192,3072]{2,1,0:T(8,128)(2,1)S(1)}, u32[]{:S(2)}) copy-start(bf16[2,192,3072]{2,1,0:T(8,128)(2,1)S(1)} %get-tuple-element.133) | copy-start | bytes 7077892
  96.8 9.5 %collective-permute-start.25 = (bf16[192,768]{1,0:T(8,128)(2,1)S(1)}, bf16[192,768]{1,0:T(8,128)(2,1)S(1)}, u32[]{:S(2)}, u32[]{:S(2)}) collective-permute-start(bf16[192,768]{1,0:T(8,128)(2,1)S(1)} %get-tuple-element.131), channel_id=1, source_target_pairs={{0,4},{4,8},{8,12},{12,14},{14,10},{10,6},{6,2},{2,0},{1,5},{5,9},... | collective-permute-start | bytes 884744 | tf_op jit(solution)/shard_map/ppermute | solution.py:38
  98.5 9.1 %collective-permute-start.26 = (bf16[192,768]{1,0:T(8,128)(2,1)S(1)}, bf16[192,768]{1,0:T(8,128)(2,1)S(1)}, u32[]{:S(2)}, u32[]{:S(2)}) collective-permute-start(bf16[192,768]{1,0:T(8,128)(2,1)S(1)} %get-tuple-element.132), channel_id=1, source_target_pairs={{0,2},{4,0},{8,4},{12,8},{14,12},{10,14},{6,10},{2,6},{1,3},{5,1},... | collective-permute-start | bytes 884744 | tf_op jit(solution)/shard_map/ppermute | solution.py:38
  108.4 11.5 %collective-permute-start.31 = (f32[384,1536]{1,0:T(8,128)S(1)}, f32[384,1536]{1,0:T(8,128)S(1)}, u32[]{:S(2)}, u32[]{:S(2)}) collective-permute-start(f32[384,1536]{1,0:T(8,128)S(1)} %shard_map.139), channel_id=1, source_target_pairs={{0,1},{1,0},{2,3},{3,2},{4,5},{5,4},{6,7},{7,6},{8,9},{9,8},{10,11... | collective-permute-start | bytes 7077896 | tf_op jit(solution)/shard_map/ppermute | solution.py:97
  108.5 9.4 %collective-permute-start.27 = (bf16[192,768]{1,0:T(8,128)(2,1)S(1)}, bf16[192,768]{1,0:T(8,128)(2,1)S(1)}, u32[]{:S(2)}, u32[]{:S(2)}) collective-permute-start(bf16[192,768]{1,0:T(8,128)(2,1)S(1)} %get-tuple-element.136), channel_id=1, source_target_pairs={{0,4},{4,8},{8,12},{12,14},{14,10},{10,6},{6,2},{2,0},{1,5},{5,9},... | collective-permute-start | bytes 884744 | tf_op jit(solution)/shard_map/ppermute | solution.py:38
  110.1 9.1 %collective-permute-start.28 = (bf16[192,768]{1,0:T(8,128)(2,1)S(1)}, bf16[192,768]{1,0:T(8,128)(2,1)S(1)}, u32[]{:S(2)}, u32[]{:S(2)}) collective-permute-start(bf16[192,768]{1,0:T(8,128)(2,1)S(1)} %get-tuple-element.137), channel_id=1, source_target_pairs={{0,2},{4,0},{8,4},{12,8},{14,12},{10,14},{6,10},{2,6},{1,3},{5,1},... | collective-permute-start | bytes 884744 | tf_op jit(solution)/shard_map/ppermute | solution.py:38
  121.0 6.5 %collective-permute-start.32 = (bf16[384,1536]{1,0:T(8,128)(2,1)S(1)}, bf16[384,1536]{1,0:T(8,128)(2,1)S(1)}, u32[]{:S(2)}, u32[]{:S(2)}) collective-permute-start(bf16[384,1536]{1,0:T(8,128)(2,1)S(1)} %get-tuple-element.147), channel_id=1, source_target_pairs={{0,1},{1,0},{2,3},{3,2},{4,5},{5,4},{6,7},{7,6},{8,9},{9,8},{10,11... | collective-permute-start | bytes 3538952 | tf_op jit(solution)/shard_map/ppermute | solution.py:97
  121.0 14.2 %collective-permute-start.29 = (bf16[192,768]{1,0:T(8,128)(2,1)S(1)}, bf16[192,768]{1,0:T(8,128)(2,1)S(1)}, u32[]{:S(2)}, u32[]{:S(2)}) collective-permute-start(bf16[192,768]{1,0:T(8,128)(2,1)S(1)} %get-tuple-element.140), channel_id=1, source_target_pairs={{0,4},{4,8},{8,12},{12,14},{14,10},{10,6},{6,2},{2,0},{1,5},{5,9},... | collective-permute-start | bytes 884744 | tf_op jit(solution)/shard_map/ppermute | solution.py:38
  122.7 12.5 %collective-permute-start.30 = (bf16[192,768]{1,0:T(8,128)(2,1)S(1)}, bf16[192,768]{1,0:T(8,128)(2,1)S(1)}, u32[]{:S(2)}, u32[]{:S(2)}) collective-permute-start(bf16[192,768]{1,0:T(8,128)(2,1)S(1)} %get-tuple-element.141), channel_id=1, source_target_pairs={{0,2},{4,0},{8,4},{12,8},{14,12},{10,14},{6,10},{2,6},{1,3},{5,1},... | collective-permute-start | bytes 884744 | tf_op jit(solution)/shard_map/ppermute | solution.py:38
  127.5 31.3 %copy-start.2 = (bf16[384,1536]{1,0:T(8,128)(2,1)}, bf16[384,1536]{1,0:T(8,128)(2,1)S(1)}, u32[]{:S(2)}) copy-start(bf16[384,1536]{1,0:T(8,128)(2,1)S(1)} %collective-permute-done.32.came_ref) | copy-start | bytes 3538948
  135.2 20.3 %copy-start.16 = (bf16[2,192,768]{2,1,0:T(8,128)(2,1)}, bf16[2,192,768]{2,1,0:T(8,128)(2,1)S(1)}, u32[]{:S(2)}) copy-start(bf16[2,192,768]{2,1,0:T(8,128)(2,1)S(1)} %get-tuple-element.153.refs_0_.refs_2_) | copy-start | bytes 1769476
  136.2 4.4 %collective-permute-start.33 = (bf16[2,192,768]{2,1,0:T(8,128)(2,1)S(1)}, bf16[2,192,768]{2,1,0:T(8,128)(2,1)S(1)}, u32[]{:S(2)}, u32[]{:S(2)}) collective-permute-start(bf16[2,192,768]{2,1,0:T(8,128)(2,1)S(1)} %shard_map.144), channel_id=1, source_target_pairs={{0,1},{1,0},{2,3},{3,2},{4,5},{5,4},{6,7},{7,6},{8,9},{9,8},{10,11... | collective-permute-start | bytes 1769480 | tf_op jit(solution)/shard_map/ppermute | solution.py:97
  140.5 15.0 %copy-start.18 = (bf16[2,192,768]{2,1,0:T(8,128)(2,1)}, bf16[2,192,768]{2,1,0:T(8,128)(2,1)S(1)}, u32[]{:S(2)}) copy-start(bf16[2,192,768]{2,1,0:T(8,128)(2,1)S(1)} %collective-permute-done.33.refs_1_.refs_3_) | copy-start | bytes 1769476
  141.2 9.5 %collective-permute-start.34 = (bf16[192,768]{1,0:T(8,128)(2,1)S(1)}, bf16[192,768]{1,0:T(8,128)(2,1)S(1)}, u32[]{:S(2)}, u32[]{:S(2)}) collective-permute-start(bf16[192,768]{1,0:T(8,128)(2,1)S(1)} %get-tuple-element.161), channel_id=1, source_target_pairs={{0,2},{4,0},{8,4},{12,8},{14,12},{10,14},{6,10},{2,6},{1,3},{5,1},... | collective-permute-start | bytes 884744 | tf_op jit(solution)/shard_map/ppermute | solution.py:38
  149.4 17.2 %copy-start.6 = (bf16[2,192,768]{2,1,0:T(8,128)(2,1)}, bf16[2,192,768]{2,1,0:T(8,128)(2,1)S(1)}, u32[]{:S(2)}) copy-start(bf16[2,192,768]{2,1,0:T(8,128)(2,1)S(1)} %get-tuple-element.158.refs_0_.refs_3_) | copy-start | bytes 1769476
  150.6 4.9 %collective-permute-start.35 = (bf16[2,192,768]{2,1,0:T(8,128)(2,1)S(1)}, bf16[2,192,768]{2,1,0:T(8,128)(2,1)S(1)}, u32[]{:S(2)}, u32[]{:S(2)}) collective-permute-start(bf16[2,192,768]{2,1,0:T(8,128)(2,1)S(1)} %get-tuple-element.162), channel_id=1, source_target_pairs={{0,1},{1,0},{2,3},{3,2},{4,5},{5,4},{6,7},{7,6},{8,9},{9,8},{10,11... | collective-permute-start | bytes 1769480 | tf_op jit(solution)/shard_map/ppermute | solution.py:97
  150.6 4.9 %collective-permute-start.36 = (f32[16,768]{1,0:T(8,128)S(1)}, f32[16,768]{1,0:T(8,128)S(1)}, u32[]{:S(2)}, u32[]{:S(2)}) collective-permute-start(f32[16,768]{1,0:T(8,128)S(1)} %get-tuple-element.163.rest_1_.refs_5_), channel_id=1, source_target_pairs={{0,1},{1,0},{2,3},{3,2},{4,5},{5,4},{6,7},{7,6},{8,9},{9,8},{10,11... | collective-permute-start | bytes 147464 | tf_op jit(solution)/shard_map/ppermute | solution.py:97
  156.3 10.2 %collective-permute-start.37 = (bf16[192,768]{1,0:T(8,128)(2,1)S(1)}, bf16[192,768]{1,0:T(8,128)(2,1)S(1)}, u32[]{:S(2)}, u32[]{:S(2)}) collective-permute-start(bf16[192,768]{1,0:T(8,128)(2,1)S(1)} %get-tuple-element.166), channel_id=1, source_target_pairs={{0,4},{4,8},{8,12},{12,14},{14,10},{10,6},{6,2},{2,0},{1,5},{5,9},... | collective-permute-start | bytes 884744 | tf_op jit(solution)/shard_map/ppermute | solution.py:38
  157.9 8.7 %collective-permute-start.38 = (bf16[192,768]{1,0:T(8,128)(2,1)S(1)}, bf16[192,768]{1,0:T(8,128)(2,1)S(1)}, u32[]{:S(2)}, u32[]{:S(2)}) collective-permute-start(bf16[192,768]{1,0:T(8,128)(2,1)S(1)} %get-tuple-element.167), channel_id=1, source_target_pairs={{0,2},{4,0},{8,4},{12,8},{14,12},{10,14},{6,10},{2,6},{1,3},{5,1},... | collective-permute-start | bytes 884744 | tf_op jit(solution)/shard_map/ppermute | solution.py:38
  158.3 8.2 %collective-permute-start.39 = (f32[16,768]{1,0:T(8,128)S(1)}, f32[16,768]{1,0:T(8,128)S(1)}, u32[]{:S(2)}, u32[]{:S(2)}) collective-permute-start(f32[16,768]{1,0:T(8,128)S(1)} %get-tuple-element.168.refs_6_), channel_id=1, source_target_pairs={{0,2},{2,0},{4,6},{6,4},{8,10},{10,8},{12,14},{14,12},{1,3},{3,1},... | collective-permute-start | bytes 147464 | tf_op jit(solution)/shard_map/ppermute | solution.py:781
  168.1 11.7 %collective-permute-start.40 = (bf16[192,768]{1,0:T(8,128)(2,1)}, bf16[192,768]{1,0:T(8,128)(2,1)}, u32[]{:S(2)}, u32[]{:S(2)}) collective-permute-start(bf16[192,768]{1,0:T(8,128)(2,1)} %get-tuple-element.171), channel_id=1, source_target_pairs={{0,4},{4,8},{8,12},{12,14},{14,10},{10,6},{6,2},{2,0},{1,5},{5,9},... | collective-permute-start | bytes 884744 | tf_op jit(solution)/shard_map/ppermute | solution.py:38
  169.2 10.6 %collective-permute-start.41 = (bf16[192,768]{1,0:T(8,128)(2,1)}, bf16[192,768]{1,0:T(8,128)(2,1)}, u32[]{:S(2)}, u32[]{:S(2)}) collective-permute-start(bf16[192,768]{1,0:T(8,128)(2,1)} %get-tuple-element.172), channel_id=1, source_target_pairs={{0,2},{4,0},{8,4},{12,8},{14,12},{10,14},{6,10},{2,6},{1,3},{5,1},... | collective-permute-start | bytes 884744 | tf_op jit(solution)/shard_map/ppermute | solution.py:38
  170.1 9.6 %collective-permute-start.42 = (f32[16,768]{1,0:T(8,128)}, f32[16,768]{1,0:T(8,128)}, u32[]{:S(2)}, u32[]{:S(2)}) collective-permute-start(f32[16,768]{1,0:T(8,128)} %get-tuple-element.173.refs_6_), channel_id=1, source_target_pairs={{0,4},{2,6},{4,0},{6,2},{8,12},{10,14},{12,8},{14,10},{1,5},{3,7},... | collective-permute-start | bytes 147464 | tf_op jit(solution)/shard_map/ppermute | solution.py:781
  172.5 13.1 %copy-start.5 = (bf16[384,1536]{1,0:T(8,128)(2,1)S(1)}, bf16[384,1536]{1,0:T(8,128)(2,1)}, u32[]{:S(2)}) copy-start(bf16[384,1536]{1,0:T(8,128)(2,1)} %copy-done.4) | copy-start | bytes 3538948
  181.8 8.3 %collective-permute-start.45 = (f32[16,768]{1,0:T(8,128)S(1)}, f32[16,768]{1,0:T(8,128)S(1)}, u32[]{:S(2)}, u32[]{:S(2)}) collective-permute-start(f32[16,768]{1,0:T(8,128)S(1)} %get-tuple-element.184), channel_id=1, source_target_pairs={{0,8},{2,10},{4,12},{6,14},{8,0},{10,2},{12,4},{14,6},{1,9},{3,11}... | collective-permute-start | bytes 147464 | tf_op jit(solution)/shard_map/ppermute | solution.py:781
  183.5 8.0 %collective-permute-start.43 = (bf16[192,768]{1,0:T(8,128)(2,1)S(1)}, bf16[192,768]{1,0:T(8,128)(2,1)S(1)}, u32[]{:S(2)}, u32[]{:S(2)}) collective-permute-start(bf16[192,768]{1,0:T(8,128)(2,1)S(1)} %get-tuple-element.177), channel_id=1, source_target_pairs={{0,4},{4,8},{8,12},{12,14},{14,10},{10,6},{6,2},{2,0},{1,5},{5,9},... | collective-permute-start | bytes 884744 | tf_op jit(solution)/shard_map/ppermute | solution.py:38
  184.4 7.5 %collective-permute-start.44 = (bf16[192,768]{1,0:T(8,128)(2,1)S(1)}, bf16[192,768]{1,0:T(8,128)(2,1)S(1)}, u32[]{:S(2)}, u32[]{:S(2)}) collective-permute-start(bf16[192,768]{1,0:T(8,128)(2,1)S(1)} %get-tuple-element.178), channel_id=1, source_target_pairs={{0,2},{4,0},{8,4},{12,8},{14,12},{10,14},{6,10},{2,6},{1,3},{5,1},... | collective-permute-start | bytes 884744 | tf_op jit(solution)/shard_map/ppermute | solution.py:38
  (32 other events, 155.0 us)
